TPU v7x, 128 devices: a whole 4x4x4 slice. The times are simulated.
128 devices in a mesh: row: 8 (over z, core), col: 16 (over y, x).
Axes of the slice: x: 4, y: 4, z: 4, core: 2. Of those that a mesh axis runs over, the one named last changes fastest.
Arguments:
- atom_single: bfloat16 [16384, 128], P(('row', 'col')), may hold values from -6 to 6
- atom_token: int32 [16384], P(('row', 'col')), may hold values from 0 to 2047, as said below
- atom_cot: bfloat16 [16384, 128], P(('row', 'col')), may hold values from -6 to 6
- token_cond: bfloat16 [2048, 768], P('row'), may hold values from -6 to 6
- pair: bfloat16 [2048, 2048, 128], P('row', 'col'), may hold values from -12 to 12
- w_pool: bfloat16 [128, 768], replicated, may hold values from -0.5 to 0.5
- w_qkv: bfloat16 [3, 768, 768], P(None, None, 'col'), may hold values from -0.21875 to 0.21875
- w_bias: bfloat16 [128, 16], replicated, may hold values from -0.8 to 0.8
- w_out: bfloat16 [768, 768], P('col'), may hold values from -0.21875 to 0.21875
- w_dec: bfloat16 [768, 128], replicated, may hold values from -0.21875 to 0.21875
Outputs:
- atom_out: bfloat16 [16384, 128], P(('row', 'col'))
- grad_atom: float32 [16384, 128], P(('row', 'col'))
- grad_bias: float32 [128, 16], replicated
Inputs may be any that keep to these rules, and one draw needn't show every extreme that they name: `atom_token`: every token has 1 to 24 atoms and some token exactly 24; the atoms stand in no particular order.
All inputs are finite; a program needn't handle non-finite values.
Results may differ from a plain program's by a relative error of at most 0.014.
The roundings to bfloat16 on the way count: a program that leaves them out, or rounds other values in their place, can miss the bound.
Values may be sent and summed in bfloat16 or wider, within the bound.
No kernel may reach another device: no remote copies, remote signals or barrier semaphores. Data moves between devices by JAX's collectives and lax.ppermute only.
A program may use at most 64 MiB of HBM per device.

v0:
```python
import math

import jax
import jax.numpy as jnp
from jax import lax
from jax.sharding import PartitionSpec as P

HD = 48


EPSILON = 1e-05


def layer_norm(single):
    center = single - jnp.mean(single, axis=-1, keepdims=True)
    inverse = lax.rsqrt(jnp.mean(center * center, axis=-1, keepdims=True) + EPSILON)
    return (center * inverse, inverse)


def norm_grad(upstream, normal, inverse):
    return inverse * (
        upstream
        - jnp.mean(upstream, axis=-1, keepdims=True)
        - normal * jnp.mean(upstream * normal, axis=-1, keepdims=True)
    )


def transposed_dot(left, right):
    return lax.dot_general(
        left, right, (((1,), (1,)), ((), ())), preferred_element_type=jnp.float32
    )


def on_device(
    atom_single, atom_token, atom_cot, token_cond, pair, w_pool, w_qkv, w_bias, w_out, w_dec
):
    tok_rows = token_cond.shape[0]
    total_tokens = tok_rows * lax.axis_size("row")
    width = w_out.shape[0]
    local_heads = width // HD
    atom_width = atom_single.shape[1]
    scale = 1.0 / math.sqrt(HD)
    onehot = (atom_token[:, None] == jnp.arange(total_tokens, dtype=jnp.int32)[None, :]).astype(
        jnp.bfloat16
    )
    stacked = jnp.concatenate([atom_single, atom_cot], axis=1)
    partial_sums = lax.dot_general(
        onehot, stacked, (((0,), (0,)), ((), ())), preferred_element_type=jnp.float32
    )
    partial_counts = jnp.sum(onehot.astype(jnp.float32), axis=0)
    share_sums, share_counts = (
        lax.psum_scatter(partial_sums, ("row", "col"), scatter_dimension=0, tiled=True),
        lax.psum_scatter(partial_counts, ("row", "col"), scatter_dimension=0, tiled=True),
    )
    share_rows = jnp.concatenate(
        [share_sums[:, :atom_width] / share_counts[:, None], share_sums[:, atom_width:]], axis=1
    ).astype(jnp.bfloat16)
    row_pooled, row_counts = (
        lax.all_gather(share_rows, "col", axis=0, tiled=True),
        lax.all_gather(share_counts.astype(jnp.bfloat16), "col", axis=0, tiled=True),
    )
    pooled = row_pooled[:, :atom_width]
    cot_pooled = row_pooled[:, atom_width:]
    counts = row_counts.astype(jnp.float32)
    single = token_cond.astype(jnp.float32) + jnp.dot(
        pooled, w_pool, preferred_element_type=jnp.float32
    )
    normal, inverse = layer_norm(single)
    normed = normal.astype(jnp.bfloat16)
    projected = jnp.einsum("td,kdf->ktf", normed, w_qkv, preferred_element_type=jnp.float32).astype(
        jnp.bfloat16
    )
    gathered = lax.all_gather(projected[1:], "row", axis=1, tiled=True)
    queries = projected[0].reshape(tok_rows, local_heads, HD)
    keys_all = gathered[0].reshape(total_tokens, local_heads, HD)
    values_all = gathered[1].reshape(total_tokens, local_heads, HD)
    bias_local = jnp.einsum("ijc,ch->hij", pair, w_bias, preferred_element_type=jnp.float32).astype(
        jnp.bfloat16
    )
    bias_rows = lax.all_to_all(bias_local, "col", split_axis=0, concat_axis=2, tiled=True)
    logits = jnp.einsum(
        "ihd,jhd->hij", queries, keys_all, preferred_element_type=jnp.float32
    ) * scale + bias_rows.astype(jnp.float32)
    shifted = jnp.exp(logits - jnp.max(logits, axis=-1, keepdims=True))
    probs = shifted / jnp.sum(shifted, axis=-1, keepdims=True)
    probs_low = probs.astype(jnp.bfloat16)
    attended = (
        jnp.einsum("hij,jhd->ihd", probs_low, values_all, preferred_element_type=jnp.float32)
        .astype(jnp.bfloat16)
        .reshape(tok_rows, width)
    )
    partial_update = jnp.dot(attended, w_out, preferred_element_type=jnp.float32)
    update = lax.psum(partial_update.astype(jnp.bfloat16), "col").astype(jnp.float32)
    token_out = (single + update).astype(jnp.bfloat16)
    token_back = jnp.dot(token_out, w_dec, preferred_element_type=jnp.float32).astype(jnp.bfloat16)
    all_back = lax.all_gather(token_back, "row", axis=0, tiled=True)
    atom_out = (
        atom_single.astype(jnp.float32)
        + jnp.dot(onehot, all_back, preferred_element_type=jnp.float32)
    ).astype(jnp.bfloat16)
    grad_out = transposed_dot(cot_pooled, w_dec)
    grad_update = grad_out.astype(jnp.bfloat16)
    grad_attended = (
        transposed_dot(grad_update, w_out).astype(jnp.bfloat16).reshape(tok_rows, local_heads, HD)
    )
    grad_probs = jnp.einsum(
        "ihd,jhd->hij", grad_attended, values_all, preferred_element_type=jnp.float32
    )
    delta = jnp.sum(probs * grad_probs, axis=-1, keepdims=True)
    grad_logits = (probs * (grad_probs - delta)).astype(jnp.bfloat16)
    grad_queries = (
        (
            jnp.einsum("hij,jhd->ihd", grad_logits, keys_all, preferred_element_type=jnp.float32)
            * scale
        )
        .astype(jnp.bfloat16)
        .reshape(tok_rows, width)
    )
    key_terms = jnp.stack(
        [
            jnp.einsum("hij,ihd->jhd", grad_logits, queries, preferred_element_type=jnp.float32),
            jnp.einsum(
                "hij,ihd->jhd", probs_low, grad_attended, preferred_element_type=jnp.float32
            ),
        ]
    ).reshape(2, total_tokens, width)
    key_sums = lax.psum_scatter(
        key_terms.astype(jnp.bfloat16), "row", scatter_dimension=1, tiled=True
    ).astype(jnp.float32)
    grad_keys = (key_sums[0] * scale).astype(jnp.bfloat16)
    grad_values = key_sums[1].astype(jnp.bfloat16)
    grad_proj = jnp.stack([grad_queries, grad_keys, grad_values])
    normed_part = jnp.einsum("ktf,kdf->td", grad_proj, w_qkv, preferred_element_type=jnp.float32)
    grad_normed = lax.psum(normed_part.astype(jnp.bfloat16), "col").astype(jnp.float32)
    grad_single = (grad_out + norm_grad(grad_normed, normal, inverse)).astype(jnp.bfloat16)
    token_grad = (transposed_dot(grad_single, w_pool) / counts[:, None]).astype(jnp.bfloat16)
    all_grad = lax.all_gather(token_grad, "row", axis=0, tiled=True)
    grad_atom = atom_cot.astype(jnp.float32) + jnp.dot(
        onehot, all_grad, preferred_element_type=jnp.float32
    )
    bias_back = lax.all_to_all(grad_logits, "col", split_axis=2, concat_axis=0, tiled=True)
    weight_part = jnp.einsum("ijc,hij->ch", pair, bias_back, preferred_element_type=jnp.float32)
    grad_bias = lax.psum(weight_part, ("row", "col"))
    return (atom_out, grad_atom, grad_bias)


def solution(mesh):
    return jax.shard_map(
        on_device,
        mesh=mesh,
        in_specs=(
            P(("row", "col"), None),
            P(("row", "col")),
            P(("row", "col"), None),
            P("row", None),
            P("row", "col", None),
            P(),
            P(None, None, "col"),
            P(),
            P("col", None),
            P(),
        ),
        out_specs=(P(("row", "col"), None), P(("row", "col"), None), P()),
        check_vma=False,
    )
```

profile of v0, /device:TPU:1, one launch (start us, length us, event | category | flops | bytes accessed | tf_op | source)
XLA Modules:
  0.0 887.3 jit_solution(13562085472055508647)
XLA Ops:
  7.2 2.7 fusion.13
  10.0 5.7 convolution_convert_fusion.2
  15.6 1.3 copy.17
  16.9 7.6 all-to-all-start
  24.8 72.7 %all-reduce.1 = f32[2048]{0:T(1024)S(1)} all-reduce(f32[2048]{0:T(1024)S(1)} %convert_reduce_fusion.1), channel_id=3, replica_groups=mesh['row'=8,'col'=16] {'row','col'}, use_global_device_ids=true, to_apply=%region_2.0.clone | all-reduce | flops 2048 | bytes 16384
  98.9 524.3 %reduce-scatter.3.cloned.1.call-done = f32[16,256]{1,0:T(8,128)} async-done(((f32[2048,256]{1,0:T(8,128)}), f32[16,256]{1,0:T(8,128)}) %reduce-scatter.3.cloned.1.call-update) | async-done | bytes 16400 | tf_op jit(solution)/shard_map/reduce_scatter | solution.py:52
  624.7 17.2 %all_gather.15 = bf16[256,256]{1,0:T(8,128)(2,1)S(1)} all-gather(bf16[16,256]{1,0:T(8,128)(2,1)S(1)} %pad_maximum_fusion), channel_id=1, replica_groups=mesh['row'=8,'col'=16] {'col'}, dimensions={0}, use_global_device_ids=true | all-gather | bytes 139264 | tf_op jit(solution)/shard_map/all_gather | solution.py:59
  641.9 1.3 fusion.54
  643.9 48.4 %all_gather.16 = bf16[2,2048,48]{1,2,0:T(8,128)(2,1)S(1)} all-gather(bf16[2,256,48]{1,2,0:T(8,128)(2,1)S(1)} %slice.49), channel_id=1, replica_groups=mesh['row'=8,'col'=16] {'row'}, dimensions={1}, use_global_device_ids=true | all-gather | bytes 442368 | tf_op jit(solution)/shard_map/all_gather | solution.py:73
  698.2 5.9 copy.19
  704.6 12.6 %reduce.6 = bf16[2048,256]{1,0:T(8,128)(2,1)} reduce(bf16[2048,1,256]{2,1,0:T(2,128)(2,1)} %bitcast.103, bf16[]{:T(256)} %broadcast.56), dimensions={1}, to_apply=%bitcast.75.reduce_sub_computation | reduce | bytes 2097154
  717.3 2.2 reshape.125
  719.4 5.3 all-to-all-start.1
  724.8 1.7 fusion.10
  726.4 2.5 convolution_convert_fusion.3
  733.1 33.2 %all-reduce = bf16[256]{0:T(256)(128)(2,1)S(1)} all-reduce(bf16[256]{0:T(256)(128)(2,1)S(1)} %dynamic-update-slice), channel_id=1, replica_groups=mesh['row'=8,'col'=16] {'col'}, use_global_device_ids=true, to_apply=%add | all-reduce | flops 256 | bytes 1024
  766.3 4.3 reshape.126
  771.8 1.9 copy.21
  773.7 4.7 convolution_bitcast_fusion.1
  778.4 70.0 %psum.23 = f32[128,16]{0,1:T(8,128)} all-reduce(f32[128,16]{0,1:T(8,128)S(1)} %convolution_bitcast_fusion.1), channel_id=1, replica_groups=mesh['row'=8,'col'=16] {'row','col'}, use_global_device_ids=true, to_apply=%region_13.0 | all-reduce | flops 2048 | bytes 16384 | tf_op jit(solution)/shard_map/psum | solution.py:143
  848.5 1.3 convert_reduce_fusion
  849.8 1.5 fusion.6
  851.3 14.0 %all_gather.19 = bf16[2048,128]{1,0:T(8,128)(2,1)S(1)} all-gather(bf16[256,128]{1,0:T(8,128)(2,1)S(1)} %fusion.6), channel_id=1, replica_groups=mesh['row'=8,'col'=16] {'row'}, dimensions={0}, use_global_device_ids=true | all-gather | bytes 589824 | tf_op jit(solution)/shard_map/all_gather | solution.py:137
  866.6 13.1 %all_gather.17 = bf16[2048,128]{1,0:T(8,128)(2,1)S(1)} all-gather(bf16[256,128]{1,0:T(8,128)(2,1)S(1)} %convolution_convert_fusion.4), channel_id=1, replica_groups=mesh['row'=8,'col'=16] {'row'}, dimensions={0}, use_global_device_ids=true | all-gather | bytes 589824 | tf_op jit(solution)/shard_map/all_gather | solution.py:96
  (75 shorter events, 17.1 us)
Async XLA Ops:
  7.2 636.3 %copy-start = (bf16[3,768,48]{1,2,0:T(8,128)(2,1)S(1)}, bf16[3,768,48]{1,2,0:T(8,128)(2,1)}, u32[]{:S(2)}) copy-start(bf16[3,768,48]{1,2,0:T(8,128)(2,1)} %param.16) | copy-start | bytes 663556
  7.2 2.8 copy-start.12
  7.2 616.1 %reduce-scatter.3.cloned.1.call-start = ((), (), s32[]{:S(2)}) async-start(), calls=%async_computation.4 | async-start | bytes 2113536 | tf_op jit(solution)/shard_map/reduce_scatter | solution.py:52
  15.6 8.9 %copy-start.13 = (s32[128]{0:T(128)S(1)}, s32[128]{0:T(128)}, u32[]{:S(2)}) copy-start(s32[128]{0:T(128)} %param.11) | copy-start | bytes 1540
  16.9 80.6 %all-to-all-start = ((bf16[16,256,128]{2,1,0:T(8,128)(2,1)}), bf16[16,256,128]{2,1,0:T(8,128)(2,1)S(1)}, u32[]{:S(2)}, u32[]{:S(2)}) async-start(bf16[16,256,128]{2,1,0:T(8,128)(2,1)} %copy.17), calls=%async_computation.1 | async-start | bytes 2097152 | tf_op jit(solution)/shard_map/all_to_all | solution.py:80
  24.5 704.5 %reduce-scatter.5.cloned.1.call-start = ((), (), s32[]{:S(2)}) async-start(), calls=%async_computation.5 | async-start | bytes 442368 | tf_op jit(solution)/shard_map/reduce_scatter | solution.py:127
  97.7 544.2 %copy-start.6 = (bf16[256,768]{1,0:T(8,128)(2,1)S(1)}, bf16[256,768]{1,0:T(8,128)(2,1)}, u32[]{:S(2)}) copy-start(bf16[256,768]{1,0:T(8,128)(2,1)} %param.13) | copy-start | bytes 1179652
  641.9 50.4 %copy-start.4 = (bf16[768,128]{1,0:T(8,128)(2,1)S(1)}, bf16[768,128]{1,0:T(8,128)(2,1)}, u32[]{:S(2)}) copy-start(bf16[768,128]{1,0:T(8,128)(2,1)} %param.19) | copy-start | bytes 589828
  692.6 1.5 copy-start.2
  693.7 0.9 copy-start.8
  696.1 1.0 copy-start.1
  719.4 46.8 %all-to-all-start.1 = ((bf16[16,2,16384]{2,1,0:T(2,128)(2,1)}), bf16[16,2,16384]{2,1,0:T(2,128)(2,1)}, u32[]{:S(2)}, u32[]{:S(2)}) async-start(bf16[16,2,16384]{2,1,0:T(2,128)(2,1)} %reshape.125), calls=%async_computation.3 | async-start | bytes 2097152 | tf_op jit(solution)/shard_map/all_to_all | solution.py:141
  724.7 123.8 %all-reduce.5.cloned.1.call-start = ((), (), s32[]{:S(2)}) async-start(), calls=%async_computation.6 | async-start | bytes 1572864 | tf_op jit(solution)/shard_map/psum | solution.py:93
  726.4 5.1 copy-start.14
  773.7 76.1 %copy-start.3 = (f32[256,768]{1,0:T(8,128)S(1)}, f32[256,768]{1,0:T(8,128)}, u32[]{:S(2)}) copy-start(f32[256,768]{1,0:T(8,128)} %copy-done.2) | copy-start | bytes 2359300
  773.7 76.1 %copy-start.9 = (bf16[128,768]{1,0:T(8,128)(2,1)S(1)}, bf16[128,768]{1,0:T(8,128)(2,1)}, u32[]{:S(2)}) copy-start(bf16[128,768]{1,0:T(8,128)(2,1)} %param.15) | copy-start | bytes 589828
  778.4 86.9 %copy-start.10 = (bf16[128,128]{1,0:T(8,128)(2,1)S(1)}, bf16[128,128]{1,0:T(8,128)(2,1)}, u32[]{:S(2)}) copy-start(bf16[128,128]{1,0:T(8,128)(2,1)} %param.12) | copy-start | bytes 98308
  849.8 16.6 %copy-start.5 = (bf16[768,128]{1,0:T(8,128)(2,1)S(1)}, bf16[768,128]{1,0:T(8,128)(2,1)}, u32[]{:S(2)}) copy-start(bf16[768,128]{1,0:T(8,128)(2,1)} %param.19) | copy-start | bytes 589828
  849.8 16.6 %copy-start.7 = (bf16[256,768]{1,0:T(8,128)(2,1)S(1)}, bf16[256,768]{1,0:T(8,128)(2,1)}, u32[]{:S(2)}) copy-start(bf16[256,768]{1,0:T(8,128)(2,1)} %get-tuple-element.5) | copy-start | bytes 1179652
  851.3 28.4 %copy-start.11 = (bf16[128,128]{1,0:T(8,128)(2,1)S(1)}, bf16[128,128]{1,0:T(8,128)(2,1)}, u32[]{:S(2)}) copy-start(bf16[128,128]{1,0:T(8,128)(2,1)} %param.10) | copy-start | bytes 98308
Sparse Core Ops, SparseCore 0:
  10.4 612.8 reduce-scatter.2
  698.3 25.8 reduce-scatter.4
  731.7 84.3 all-reduce.4
where the time goes:
time: 889 us; the launch traced here: 887 us
  waiting for transfers between devices  524 us (59%)
  blocking collectives  269 us (30%)
  matrix products  26.6 us (3%)
  local copies, waits for them, and re-layouts  22.3 us (3%)
  other arithmetic  17.6 us (2%)
  between operations  14.7 us (2%)
  starting transfers between devices  13 us (1%)
    reduce_scatter x1, waiting for transfers between devices, on_device(): lax.psum_scatter(partial_sums, ('row', 'col'), scatter_dimension=0, tiled...  524 us
    unnamed x2, blocking collectives  106 us
    psum x1, blocking collectives, on_device(): grad_bias = lax.psum(weight_part, ('row', 'col'))  70 us
    all_gather x1, blocking collectives, on_device(): gathered = lax.all_gather(projected[1:], 'row', axis=1, tiled=True)  48.4 us
  transfers between devices with their start and end apart: 5, of which 1 were waited for; matrix products, arithmetic and copies ran while one was open for 6% of the time, Pallas kernels for 0%

commit v1 on v0

v1 whole, which is shorter than its diff:
```python
import math

import jax
import jax.numpy as jnp
from jax import lax
from jax.sharding import PartitionSpec as P

HD = 48


EPSILON = 1e-05
BF = jnp.bfloat16
F32 = jnp.float32


def norm_grad(upstream, normal, inverse):
    return inverse * (
        upstream
        - jnp.mean(upstream, axis=-1, keepdims=True)
        - normal * jnp.mean(upstream * normal, axis=-1, keepdims=True)
    )


def nt(left, right):
    return lax.dot_general(left, right, (((1,), (1,)), ((), ())), preferred_element_type=F32)


def tn(left, right):
    return lax.dot_general(left, right, (((0,), (0,)), ((), ())), preferred_element_type=F32)


def nn(left, right):
    return jnp.dot(left, right, preferred_element_type=F32)


def exchange(blocks, axis):
    return lax.all_to_all(blocks, axis, split_axis=0, concat_axis=0, tiled=True)


def spread(block, axis):
    return exchange(jnp.broadcast_to(block[None], (lax.axis_size(axis),) + block.shape), axis)


def split_ids(ids):
    return jnp.concatenate([ids // 64, ids % 64]).astype(BF)[None]


def join_ids(rows):
    half = rows.shape[-1] // 2
    rows = rows.astype(F32)
    return (rows[:, :half] * 64.0 + rows[:, half:]).astype(jnp.int32)


def on_device(
    atom_single, atom_token, atom_cot, token_cond, pair, w_pool, w_qkv, w_bias, w_out, w_dec
):
    rows, cols = lax.axis_size("row"), lax.axis_size("col")
    row, col = lax.axis_index("row"), lax.axis_index("col")
    tok_rows = token_cond.shape[0]
    total_tokens = tok_rows * rows
    n_atoms, width = atom_single.shape
    scale = 1.0 / math.sqrt(HD)
    tile = tok_rows // cols

    own_ids = split_ids(atom_token)
    stacked = jnp.concatenate([atom_single, atom_cot], axis=1)
    payload = jnp.concatenate([stacked, jnp.pad(own_ids, ((0, 15), (0, 0)))], axis=0)
    by_col = spread(payload, "col")

    bias_local = jnp.einsum("ijc,ch->hij", pair, w_bias, preferred_element_type=F32).astype(BF)

    atoms = by_col[:, :n_atoms].reshape(cols * n_atoms, 2 * width)
    ids = join_ids(by_col[:, n_atoms]).reshape(-1)
    onehot = (jnp.arange(total_tokens, dtype=jnp.int32)[:, None] == ids[None, :]).astype(BF)
    partial_sums = nn(onehot, atoms).astype(BF).reshape(rows, tok_rows, 2 * width)
    partial_counts = jnp.sum(onehot.astype(F32), axis=1).astype(BF).reshape(rows, 1, tok_rows)
    extra = jnp.concatenate(
        [
            partial_counts,
            jnp.broadcast_to(own_ids[None], (rows, 1, 2 * width)),
            jnp.zeros((rows, 14, 2 * width), BF),
        ],
        axis=1,
    )
    by_row = exchange(jnp.concatenate([partial_sums, extra], axis=1), "row")
    bias = exchange(bias_local, "col")

    sums = jnp.sum(by_row[:, :tok_rows].astype(F32), axis=0)
    counts = jnp.sum(by_row[:, tok_rows].astype(F32), axis=0)[:, None]
    column_ids = join_ids(by_row[:, tok_rows + 1]).reshape(-1)
    pooled = (sums[:, :width] / counts).astype(BF)
    cot_pooled = sums[:, width:].astype(BF)
    single = token_cond.astype(F32) + nn(pooled, w_pool)
    center = single - jnp.mean(single, axis=-1, keepdims=True)
    inverse = lax.rsqrt(jnp.mean(center * center, axis=-1, keepdims=True) + EPSILON)
    normal = center * inverse
    normed = normal.astype(BF)
    w_t = jnp.transpose(w_qkv, (0, 2, 1))
    queries = nt(normed, w_t[0]).astype(BF)
    kv_t = nt(w_t[1:].reshape(2 * HD, -1), normed).astype(BF)
    kv_all = spread(kv_t, "row")
    keys_t = jnp.transpose(kv_all[:, :HD], (1, 0, 2)).reshape(HD, total_tokens)
    values_t = jnp.transpose(kv_all[:, HD:], (1, 0, 2)).reshape(HD, total_tokens)
    grad_out = nt(cot_pooled, w_dec)
    grad_attended = nt(grad_out.astype(BF), w_out).astype(BF)

    bias_rows = jnp.transpose(bias, (1, 0, 2)).reshape(tok_rows, total_tokens)
    logits = nn(queries, keys_t) * scale + bias_rows.astype(F32)
    shifted = jnp.exp(logits - jnp.max(logits, axis=-1, keepdims=True))
    probs = shifted / jnp.sum(shifted, axis=-1, keepdims=True)
    probs_low = probs.astype(BF)
    attended = nt(probs_low, values_t).astype(BF)
    grad_probs = nn(grad_attended, values_t)
    delta = jnp.sum(probs * grad_probs, axis=-1, keepdims=True)
    grad_logits = (probs * (grad_probs - delta)).astype(BF)
    grad_queries = (nt(grad_logits, keys_t) * scale).astype(BF)
    gk_t = tn(queries, grad_logits)
    gv_t = tn(grad_attended, probs_low)
    gkv_t = jnp.transpose(
        jnp.concatenate([gk_t, gv_t], axis=0).astype(BF).reshape(2 * HD, rows, tok_rows), (1, 0, 2)
    )
    gkv_parts = exchange(gkv_t, "row")
    logits_back = jnp.transpose(
        grad_logits.reshape(tok_rows, cols, total_tokens // cols), (1, 0, 2)
    )
    bias_back = exchange(logits_back, "col")

    update = nn(attended, w_out).astype(BF)
    back_parts = exchange(nn(update, w_dec).astype(BF).reshape(cols, tile, width), "col")
    single_tile = lax.dynamic_slice_in_dim(single, col * tile, tile, 0)
    back_tile = (
        nn(single_tile.astype(BF), w_dec) + jnp.sum(back_parts.astype(F32), axis=0)
    ).astype(BF)

    gkv = jnp.sum(gkv_parts.astype(F32), axis=0)
    grad_keys = (gkv[:HD] * scale).astype(BF)
    grad_values = gkv[HD:].astype(BF)
    normed_part = nn(grad_queries, w_t[0]) + tn(grad_keys, w_t[1]) + tn(grad_values, w_t[2])
    base = jnp.where(col == 0, grad_out, 0.0)
    single_part = (base + norm_grad(normed_part, normal, inverse)).astype(BF)
    grad_part = (nt(single_part, w_pool) / counts).astype(BF)

    weight_part = jnp.einsum("ijc,hij->hc", pair, bias_back, preferred_element_type=F32)
    high = weight_part.astype(BF)
    low = (weight_part - high.astype(F32)).astype(BF)
    parts = spread(jnp.concatenate([grad_part, back_tile, high, low], axis=0), "col")
    token_grad = jnp.sum(parts[:, :tok_rows].astype(F32), axis=0).astype(BF)
    token_back = parts[:, tok_rows : tok_rows + tile].reshape(tok_rows, width)
    weight_row = jnp.sum(parts[:, tok_rows + tile :].astype(F32), axis=0)
    weight_row = weight_row[:16] + weight_row[16:]

    local_ids = column_ids - row * tok_rows
    pick = (local_ids[:, None] == jnp.arange(tok_rows, dtype=jnp.int32)[None, :]).astype(BF)
    picked = nn(pick, jnp.concatenate([token_back, token_grad], axis=1)).astype(BF)
    high = weight_row.astype(BF)
    low = (weight_row - high.astype(F32)).astype(BF)
    tail = jnp.broadcast_to(jnp.concatenate([high, low], axis=1)[None], (rows, 16, 2 * width))
    final = exchange(
        jnp.concatenate([picked.reshape(rows, n_atoms, 2 * width), tail], axis=1), "row"
    )
    final = jnp.sum(final.astype(F32), axis=0)
    atom_out = (atom_single.astype(F32) + final[:n_atoms, :width]).astype(BF)
    grad_atom = atom_cot.astype(F32) + final[:n_atoms, width:]
    grad_bias = jnp.transpose(final[n_atoms:, :width] + final[n_atoms:, width:])
    return (atom_out, grad_atom, grad_bias)


def solution(mesh):
    return jax.shard_map(
        on_device,
        mesh=mesh,
        in_specs=(
            P(("row", "col"), None),
            P(("row", "col")),
            P(("row", "col"), None),
            P("row", None),
            P("row", "col", None),
            P(),
            P(None, None, "col"),
            P(),
            P("col", None),
            P(),
        ),
        out_specs=(P(("row", "col"), None), P(("row", "col"), None), P()),
        check_vma=False,
    )
```

time: 889 us -> 194 us (0.22)
  waiting for transfers between devices: 524 us -> 92.1 us
  blocking collectives: 269 us -> 16.1 us
  starting transfers between devices: 13 us -> 42.7 us
  local copies, waits for them, and re-layouts: 22.3 us -> 7.09 us
  between operations: 14.7 us -> 1.06 us
    reduce_scatter x2 -> x0, waiting for transfers between devices: 524 us -> none  [the longest x1 524 us: on_device(): lax.psum_scatter(partial_sums, ('row', 'col'), scatter_dimension=0, tiled...]
    unnamed x2 -> x0, blocking collectives: 106 us -> none
    all_gather x4 -> x0, blocking collectives: 92.8 us -> none  [the longest x1 48.4 us: on_device(): gathered = lax.all_gather(projected[1:], 'row', axis=1, tiled=True)]
    all_to_all x2 -> x8, waiting for transfers between devices: 0.01 us -> 92.1 us  [exchange(): return lax.all_to_all(blocks, axis, split_axis=0, concat_axis=0, tiled=True)]
    psum x1 -> x0, blocking collectives: 70 us -> none  [on_device(): grad_bias = lax.psum(weight_part, ('row', 'col'))]
    all_to_all x2 -> x8, starting transfers between devices: 12.9 us -> 42.7 us  [exchange(): return lax.all_to_all(blocks, axis, split_axis=0, concat_axis=0, tiled=True)]
    all_to_all x0 -> x1, blocking collectives: none -> 16.1 us  [exchange(): return lax.all_to_all(blocks, axis, split_axis=0, concat_axis=0, tiled=True)]
    unnamed x1 -> x0, other arithmetic: 12.6 us -> none
  transfers between devices with their start and end apart: 5 -> 8, of which waited for: 1 -> 8; matrix products, arithmetic and copies ran while one was open for 6% -> 7% of each run, Pallas kernels for 0% -> 0%
where the time goes in v1:
time: 194 us; the launch traced here: 193 us
  waiting for transfers between devices  92.1 us (47%)
  starting transfers between devices  42.7 us (22%)
  matrix products  24.8 us (13%)
  blocking collectives  16.1 us (8%)
  other arithmetic  8.97 us (5%)
  local copies, waits for them, and re-layouts  7.09 us (4%)
    all_to_all x8, waiting for transfers between devices, exchange(): return lax.all_to_all(blocks, axis, split_axis=0, concat_axis=0, tiled=True)  92.1 us
    all_to_all x8, starting transfers between devices, exchange(): return lax.all_to_all(blocks, axis, split_axis=0, concat_axis=0, tiled=True)  42.7 us
    all_to_all x1, blocking collectives, exchange(): return lax.all_to_all(blocks, axis, split_axis=0, concat_axis=0, tiled=True)  16.1 us
    dot_general x8, matrix products, nn(): return jnp.dot(left, right, preferred_element_type=F32)  8.2 us
    dot_general x1, matrix products, on_device(): jnp.einsum('ijc,ch->hij', pair, w_bias, preferred_element_type=F32)  5.66 us
    dot_general x1, matrix products, on_device(): jnp.einsum('ijc,hij->hc', pair, bias_back, preferred_element_type=F32)  5.02 us
  transfers between devices with their start and end apart: 8, of which 8 were waited for; matrix products, arithmetic and copies ran while one was open for 7% of the time, Pallas kernels for 0%

profile of v1, /device:TPU:1, one launch (start us, length us, event | category | flops | bytes accessed | tf_op | source)
XLA Modules:
  0.0 192.9 jit_solution(5112689455593933459)
XLA Ops:
  3.2 7.6 %all-to-all-start = ((bf16[16,144,256]{2,1,0:T(8,128)(2,1)}), bf16[16,144,256]{2,1,0:T(8,128)(2,1)S(1)}, u32[]{:S(2)}, u32[]{:S(2)}) async-start(bf16[16,144,256]{2,1,0:T(8,128)(2,1)} %broadcast_in_dim.15), calls=%async_computation | async-start | bytes 2359296 | tf_op jit(solution)/shard_map/all_to_all | solution.py:37
  10.9 17.3 %all-to-all-done = bf16[16,144,256]{2,1,0:T(8,128)(2,1)S(1)} async-done(((bf16[16,144,256]{2,1,0:T(8,128)(2,1)}), bf16[16,144,256]{2,1,0:T(8,128)(2,1)S(1)}, u32[]{:S(2)}, u32[]{:S(2)}) %all-to-all-start) | async-done | bytes 1179680 | tf_op jit(solution)/shard_map/all_to_all | solution.py:37
  28.3 1.7 fusion.2
  30.1 3.2 %fusion.5 = bf16[2048,256]{1,0:T(8,128)(2,1)S(1)} fusion(bf16[2048,256]{1,0:T(8,128)(2,1)S(1)} %bitcast.95, s32[2048]{0:T(1024)S(1)} %fusion.39), kind=kOutput, calls=%fused_computation.7 | convolution fusion | flops 2152202240 | bytes 2105344 | tf_op jit(solution)/shard_map/dot_general | solution.py:33
  34.6 8.2 %all-to-all-start.1 = ((bf16[8,272,256]{2,1,0:T(8,128)(2,1)}), bf16[8,272,256]{2,1,0:T(8,128)(2,1)S(1)}, u32[]{:S(2)}, u32[]{:S(2)}) async-start(bf16[8,272,256]{2,1,0:T(8,128)(2,1)} %maximum_maximum_fusion), calls=%async_computation.1 | async-start | bytes 2228224 | tf_op jit(solution)/shard_map/all_to_all | solution.py:37
  42.9 15.8 %all-to-all-done.1 = bf16[8,272,256]{2,1,0:T(8,128)(2,1)S(1)} async-done(((bf16[8,272,256]{2,1,0:T(8,128)(2,1)}), bf16[8,272,256]{2,1,0:T(8,128)(2,1)S(1)}, u32[]{:S(2)}, u32[]{:S(2)}) %all-to-all-start.1) | async-done | bytes 1114144 | tf_op jit(solution)/shard_map/all_to_all | solution.py:37
  61.7 4.2 %all-to-all-start.2 = ((bf16[8,96,256]{2,1,0:T(8,128)(2,1)}), bf16[8,96,256]{2,1,0:T(8,128)(2,1)S(1)}, u32[]{:S(2)}, u32[]{:S(2)}) async-start(bf16[8,96,256]{2,1,0:T(8,128)(2,1)} %broadcast_in_dim.19), calls=%async_computation.2 | async-start | bytes 786432 | tf_op jit(solution)/shard_map/all_to_all | solution.py:37
  65.9 5.7 %convolution_convert_fusion.2 = bf16[16,256,128]{2,0,1:T(8,128)(2,1)S(1)} fusion(bf16[256,128,128]{2,1,0:T(8,128)(2,1)} %param.14, bf16[128,16]{0,1:T(8,128)(2,1)S(1)} %copy-done.11), kind=kOutput, calls=%fused_computation.17 | convolution fusion | flops 134742016 | bytes 9441280 | tf_op jit(solution)/shard_map/ijc,ch->hij/dot_general | solution.py:70
  71.5 1.3 copy.25
  74.0 3.8 %all-to-all-start.3 = ((bf16[16,256,128]{2,1,0:T(8,128)(2,1)}), bf16[16,256,128]{2,1,0:T(8,128)(2,1)S(1)}, u32[]{:S(2)}, u32[]{:S(2)}) async-start(bf16[16,256,128]{2,1,0:T(8,128)(2,1)} %copy.25), calls=%async_computation.3 | async-start | bytes 2097152 | tf_op jit(solution)/shard_map/all_to_all | solution.py:37
  79.6 14.1 %all-to-all-done.3 = bf16[16,256,128]{2,1,0:T(8,128)(2,1)S(1)} async-done(((bf16[16,256,128]{2,1,0:T(8,128)(2,1)}), bf16[16,256,128]{2,1,0:T(8,128)(2,1)S(1)}, u32[]{:S(2)}, u32[]{:S(2)}) %all-to-all-start.3) | async-done | bytes 1048608 | tf_op jit(solution)/shard_map/all_to_all | solution.py:37
  97.4 1.8 fusion.13
  99.2 1.3 bitcast_bitcast_fusion
  101.5 4.6 %all-to-all-start.5 = ((bf16[16,16,128]{2,1,0:T(8,128)(2,1)}), bf16[16,16,128]{2,1,0:T(8,128)(2,1)S(1)}, u32[]{:S(2)}, u32[]{:S(2)}) async-start(bf16[16,16,128]{2,1,0:T(8,128)(2,1)} %bitcast.17), calls=%async_computation.5 | async-start | bytes 131072 | tf_op jit(solution)/shard_map/all_to_all | solution.py:37
  107.0 5.7 %all-to-all-done.5 = bf16[16,16,128]{2,1,0:T(8,128)(2,1)S(1)} async-done(((bf16[16,16,128]{2,1,0:T(8,128)(2,1)}), bf16[16,16,128]{2,1,0:T(8,128)(2,1)S(1)}, u32[]{:S(2)}, u32[]{:S(2)}) %all-to-all-start.5) | async-done | bytes 65568 | tf_op jit(solution)/shard_map/all_to_all | solution.py:37
  112.6 6.1 %all-to-all-start.4 = ((bf16[8,96,256]{2,1,0:T(8,128)(2,1)}), bf16[8,96,256]{2,1,0:T(8,128)(2,1)S(1)}, u32[]{:S(2)}, u32[]{:S(2)}) async-start(bf16[8,96,256]{2,1,0:T(8,128)(2,1)} %maximum_bitcast_fusion), calls=%async_computation.4 | async-start | bytes 786432 | tf_op jit(solution)/shard_map/all_to_all | solution.py:37
  118.9 7.9 %all-to-all-done.4 = bf16[8,96,256]{2,1,0:T(8,128)(2,1)S(1)} async-done(((bf16[8,96,256]{2,1,0:T(8,128)(2,1)}), bf16[8,96,256]{2,1,0:T(8,128)(2,1)S(1)}, u32[]{:S(2)}, u32[]{:S(2)}) %all-to-all-start.4) | async-done | bytes 393248 | tf_op jit(solution)/shard_map/all_to_all | solution.py:37
  126.8 3.7 %all-to-all-start.6 = ((bf16[16,256,128]{2,1,0:T(8,128)(2,1)}), bf16[16,256,128]{2,1,0:T(8,128)(2,1)S(1)}, u32[]{:S(2)}, u32[]{:S(2)}) async-start(bf16[16,256,128]{2,1,0:T(8,128)(2,1)} %bitcast_bitcast_fusion), calls=%async_computation.6 | async-start | bytes 2097152 | tf_op jit(solution)/shard_map/all_to_all | solution.py:37
  130.5 1.5 convolution_add_fusion.1
  132.9 13.6 %all-to-all-done.6 = bf16[16,256,128]{2,1,0:T(8,128)(2,1)S(1)} async-done(((bf16[16,256,128]{2,1,0:T(8,128)(2,1)}), bf16[16,256,128]{2,1,0:T(8,128)(2,1)S(1)}, u32[]{:S(2)}, u32[]{:S(2)}) %all-to-all-start.6) | async-done | bytes 1048608 | tf_op jit(solution)/shard_map/all_to_all | solution.py:37
  146.5 5.0 %subtract_convert_fusion.1 = (bf16[16,128]{1,0:T(8,128)(2,1)S(1)}, bf16[16,128]{1,0:T(8,128)(2,1)S(1)}) fusion(bf16[256,128,128]{2,1,0:T(8,128)(2,1)} %param.14, bf16[16,256,128]{2,1,0:T(8,128)(2,1)S(1)} %all-to-all-done.6), kind=kOutput, calls=%fused_computation.103 | convolution fusion | flops 134225920 | bytes 9445376 | tf_op jit(solution)/shard_map/ijc,hij->hc/dot_general | solution.py:143
  152.8 4.6 %all-to-all-start.7 = ((bf16[16,304,128]{2,1,0:T(8,128)(2,1)}), bf16[16,304,128]{2,1,0:T(8,128)(2,1)S(1)}, u32[]{:S(2)}, u32[]{:S(2)}) async-start(bf16[16,304,128]{2,1,0:T(8,128)(2,1)} %broadcast_in_dim.20), calls=%async_computation.7 | async-start | bytes 2490368 | tf_op jit(solution)/shard_map/all_to_all | solution.py:37
  158.2 16.6 %all-to-all-done.7 = bf16[16,304,128]{2,1,0:T(8,128)(2,1)S(1)} async-done(((bf16[16,304,128]{2,1,0:T(8,128)(2,1)}), bf16[16,304,128]{2,1,0:T(8,128)(2,1)S(1)}, u32[]{:S(2)}, u32[]{:S(2)}) %all-to-all-start.7) | async-done | bytes 1245216 | tf_op jit(solution)/shard_map/all_to_all | solution.py:37
  175.4 16.1 %all_to_all.45 = bf16[8,144,256]{2,1,0:T(8,128)(2,1)S(1)} all-to-all(bf16[8,144,256]{2,1,0:T(8,128)(2,1)S(1)} %pad_maximum_fusion), channel_id=1, replica_groups=mesh['row'=8,'col'=16] {'row'}, dimensions={0} | all-to-all | bytes 1179648 | tf_op jit(solution)/shard_map/all_to_all | solution.py:37
  (88 shorter events, 20.6 us)
Async XLA Ops:
  0.6 77.5 %copy-start = (bf16[768,128]{1,0:T(8,128)(2,1)S(1)}, bf16[768,128]{1,0:T(8,128)(2,1)}, u32[]{:S(2)}) copy-start(bf16[768,128]{1,0:T(8,128)(2,1)} %param.19) | copy-start | bytes 589828
  3.2 25.0 %all-to-all-start = ((bf16[16,144,256]{2,1,0:T(8,128)(2,1)}), bf16[16,144,256]{2,1,0:T(8,128)(2,1)S(1)}, u32[]{:S(2)}, u32[]{:S(2)}) async-start(bf16[16,144,256]{2,1,0:T(8,128)(2,1)} %broadcast_in_dim.15), calls=%async_computation | async-start | bytes 2359296 | tf_op jit(solution)/shard_map/all_to_all | solution.py:37
  33.3 9.5 %copy-start.2 = (bf16[3,768,48]{1,2,0:T(8,128)(2,1)S(1)}, bf16[3,768,48]{1,2,0:T(8,128)(2,1)}, u32[]{:S(2)}) copy-start(bf16[3,768,48]{1,2,0:T(8,128)(2,1)} %param.16) | copy-start | bytes 663556
  34.6 25.2 %copy-start.5 = (bf16[128,768]{1,0:T(8,128)(2,1)S(1)}, bf16[128,768]{1,0:T(8,128)(2,1)}, u32[]{:S(2)}) copy-start(bf16[128,768]{1,0:T(8,128)(2,1)} %param.15) | copy-start | bytes 589828
  34.6 25.2 %copy-start.7 = (bf16[256,768]{1,0:T(8,128)(2,1)S(1)}, bf16[256,768]{1,0:T(8,128)(2,1)}, u32[]{:S(2)}) copy-start(bf16[256,768]{1,0:T(8,128)(2,1)} %param.13) | copy-start | bytes 1179652
  34.6 24.0 %all-to-all-start.1 = ((bf16[8,272,256]{2,1,0:T(8,128)(2,1)}), bf16[8,272,256]{2,1,0:T(8,128)(2,1)S(1)}, u32[]{:S(2)}, u32[]{:S(2)}) async-start(bf16[8,272,256]{2,1,0:T(8,128)(2,1)} %maximum_maximum_fusion), calls=%async_computation.1 | async-start | bytes 2228224 | tf_op jit(solution)/shard_map/all_to_all | solution.py:37
  58.6 1.0 copy-start.1
  60.2 5.7 %copy-start.11 = (bf16[128,16]{0,1:T(8,128)(2,1)S(1)}, bf16[128,16]{0,1:T(8,128)(2,1)}, u32[]{:S(2)}) copy-start(bf16[128,16]{0,1:T(8,128)(2,1)} %param.17) | copy-start | bytes 12292
  61.7 12.3 %all-to-all-start.2 = ((bf16[8,96,256]{2,1,0:T(8,128)(2,1)}), bf16[8,96,256]{2,1,0:T(8,128)(2,1)S(1)}, u32[]{:S(2)}, u32[]{:S(2)}) async-start(bf16[8,96,256]{2,1,0:T(8,128)(2,1)} %broadcast_in_dim.19), calls=%async_computation.2 | async-start | bytes 786432 | tf_op jit(solution)/shard_map/all_to_all | solution.py:37
  74.0 19.7 %all-to-all-start.3 = ((bf16[16,256,128]{2,1,0:T(8,128)(2,1)}), bf16[16,256,128]{2,1,0:T(8,128)(2,1)S(1)}, u32[]{:S(2)}, u32[]{:S(2)}) async-start(bf16[16,256,128]{2,1,0:T(8,128)(2,1)} %copy.25), calls=%async_computation.3 | async-start | bytes 2097152 | tf_op jit(solution)/shard_map/all_to_all | solution.py:37
  96.1 1.3 copy-start.3
  97.4 3.1 %copy-start.10 = (bf16[48,768]{1,0:T(8,128)(2,1)S(1)}, bf16[48,768]{1,0:T(8,128)(2,1)}, u32[]{:S(2)}) copy-start(bf16[48,768]{1,0:T(8,128)(2,1)} %param.18) | copy-start | bytes 221188
  99.2 6.9 %copy-start.4 = (bf16[48,2048]{1,0:T(8,128)(2,1)S(1)}, bf16[48,2048]{1,0:T(8,128)(2,1)}, u32[]{:S(2)}) copy-start(bf16[48,2048]{1,0:T(8,128)(2,1)} %convolution_convert_fusion.1) | copy-start | bytes 589828
  101.5 11.1 %all-to-all-start.5 = ((bf16[16,16,128]{2,1,0:T(8,128)(2,1)}), bf16[16,16,128]{2,1,0:T(8,128)(2,1)S(1)}, u32[]{:S(2)}, u32[]{:S(2)}) async-start(bf16[16,16,128]{2,1,0:T(8,128)(2,1)} %bitcast.17), calls=%async_computation.5 | async-start | bytes 131072 | tf_op jit(solution)/shard_map/all_to_all | solution.py:37
  112.6 14.2 %all-to-all-start.4 = ((bf16[8,96,256]{2,1,0:T(8,128)(2,1)}), bf16[8,96,256]{2,1,0:T(8,128)(2,1)S(1)}, u32[]{:S(2)}, u32[]{:S(2)}) async-start(bf16[8,96,256]{2,1,0:T(8,128)(2,1)} %maximum_bitcast_fusion), calls=%async_computation.4 | async-start | bytes 786432 | tf_op jit(solution)/shard_map/all_to_all | solution.py:37
  126.8 19.7 %all-to-all-start.6 = ((bf16[16,256,128]{2,1,0:T(8,128)(2,1)}), bf16[16,256,128]{2,1,0:T(8,128)(2,1)S(1)}, u32[]{:S(2)}, u32[]{:S(2)}) async-start(bf16[16,256,128]{2,1,0:T(8,128)(2,1)} %bitcast_bitcast_fusion), calls=%async_computation.6 | async-start | bytes 2097152 | tf_op jit(solution)/shard_map/all_to_all | solution.py:37
  130.5 2.0 %copy-start.6 = (bf16[128,768]{1,0:T(8,128)(2,1)S(1)}, bf16[128,768]{1,0:T(8,128)(2,1)}, u32[]{:S(2)}) copy-start(bf16[128,768]{1,0:T(8,128)(2,1)} %param.15) | copy-start | bytes 589828
  152.8 22.0 %all-to-all-start.7 = ((bf16[16,304,128]{2,1,0:T(8,128)(2,1)}), bf16[16,304,128]{2,1,0:T(8,128)(2,1)S(1)}, u32[]{:S(2)}, u32[]{:S(2)}) async-start(bf16[16,304,128]{2,1,0:T(8,128)(2,1)} %broadcast_in_dim.20), calls=%async_computation.7 | async-start | bytes 2490368 | tf_op jit(solution)/shard_map/all_to_all | solution.py:37
  175.0 17.3 %copy-start.8 = (bf16[128,128]{1,0:T(8,128)(2,1)S(1)}, bf16[128,128]{1,0:T(8,128)(2,1)}, u32[]{:S(2)}) copy-start(bf16[128,128]{1,0:T(8,128)(2,1)} %param.12) | copy-start | bytes 98308
  175.0 17.3 %copy-start.9 = (bf16[128,128]{1,0:T(8,128)(2,1)S(1)}, bf16[128,128]{1,0:T(8,128)(2,1)}, u32[]{:S(2)}) copy-start(bf16[128,128]{1,0:T(8,128)(2,1)} %param.10) | copy-start | bytes 98308

commit v2 on v1

v2 whole, which is shorter than its diff:
```python
import math

import jax
import jax.numpy as jnp
from jax import lax
from jax.experimental import pallas as pl
from jax.experimental.pallas import tpu as pltpu
from jax.sharding import PartitionSpec as P

HD = 48


EPSILON = 1e-05
BF = jnp.bfloat16
F32 = jnp.float32


def nt(left, right):
    return lax.dot_general(left, right, (((1,), (1,)), ((), ())), preferred_element_type=F32)


def tn(left, right):
    return lax.dot_general(left, right, (((0,), (0,)), ((), ())), preferred_element_type=F32)


def nn(left, right):
    return jnp.dot(left, right, preferred_element_type=F32)


def exchange(blocks, axis):
    return lax.all_to_all(blocks, axis, split_axis=0, concat_axis=0, tiled=True)


def spread(block, axis):
    return exchange(jnp.broadcast_to(block[None], (lax.axis_size(axis),) + block.shape), axis)


def after(value, *others):
    return lax.optimization_barrier((value,) + others)[0]


def high_low(value):
    high = value.astype(BF)
    return [high, (value - high.astype(F32)).astype(BF)]


def norm_kernel(at, cond_ref, pooled_ref, wpool_ref, wt_ref, normed_ref, inv_ref, kv_ref, q_ref, qt_ref):
    single = cond_ref[...].astype(F32) + nn(pooled_ref[...], wpool_ref[...])
    center = single - jnp.mean(single, axis=-1, keepdims=True)
    inverse = lax.rsqrt(jnp.mean(center * center, axis=-1, keepdims=True) + EPSILON)
    normed = (center * inverse).astype(BF)
    normed_ref[...] = normed
    inv_ref[...] = inverse
    kv_ref[...] = nt(wt_ref[HD:], normed).astype(BF)

    @pl.when(pl.program_id(0) == at[0])
    def _():
        q_ref[...] = nt(normed, wt_ref[:HD]).astype(BF)
        qt_ref[...] = nt(wt_ref[:HD], normed).astype(BF)


def norm_tokens(at, cond, pooled, w_pool, w_t, rows):
    tokens, features = cond.shape
    block = tokens // rows
    whole = lambda shape: pl.BlockSpec(shape, lambda b: (0, 0))
    return pl.pallas_call(
        norm_kernel,
        grid=(rows,),
        in_specs=[
            pl.BlockSpec(memory_space=pltpu.SMEM),
            pl.BlockSpec((block, features), lambda b: (b, 0)),
            pl.BlockSpec((block, pooled.shape[1]), lambda b: (b, 0)),
            whole(w_pool.shape),
            whole(w_t.shape),
        ],
        out_specs=[
            pl.BlockSpec((block, features), lambda b: (b, 0)),
            pl.BlockSpec((block, 1), lambda b: (b, 0)),
            pl.BlockSpec((2 * HD, block), lambda b: (0, b)),
            whole((block, HD)),
            whole((HD, block)),
        ],
        out_shape=[
            jax.ShapeDtypeStruct((tokens, features), BF),
            jax.ShapeDtypeStruct((tokens, 1), F32),
            jax.ShapeDtypeStruct((2 * HD, tokens), BF),
            jax.ShapeDtypeStruct((block, HD), BF),
            jax.ShapeDtypeStruct((HD, block), BF),
        ],
        compiler_params=pltpu.CompilerParams(vmem_limit_bytes=24 * 2**20),
        cost_estimate=pl.CostEstimate(
            flops=2 * tokens * features * 272, bytes_accessed=8 * 2**20, transcendentals=0
        ),
    )(at, cond, pooled, w_pool, w_t)


def attend_kernel(
    at, q_ref, qt_ref, kv_ref, bias_ref, wt_ref, normed_ref, inv_ref, wpool_ref, wout_ref, wdec_ref,
    out_ref, s_ref, g_ref, u_ref,
):
    scale = 1.0 / math.sqrt(HD)
    blocks, tokens, columns = s_ref.shape
    half = columns // 2
    cols = 2 * blocks
    tile = tokens // cols
    spans = [slice(b * columns, (b + 1) * columns) for b in range(blocks)]

    queries = q_ref[...]
    top = jnp.full((tokens, 1), -jnp.inf, F32)
    for b in range(blocks):
        bias = jnp.concatenate([bias_ref[2 * b, :tokens], bias_ref[2 * b + 1, :tokens]], axis=1)
        logits = nn(queries, kv_ref[:HD, spans[b]]) * scale + bias.astype(F32)
        s_ref[b] = logits
        top = jnp.maximum(top, jnp.max(logits, axis=-1, keepdims=True))
    total = jnp.zeros((tokens, 1), F32)
    for b in range(blocks):
        shifted = jnp.exp(s_ref[b] - top)
        s_ref[b] = shifted
        total = total + jnp.sum(shifted, axis=-1, keepdims=True)
    share = 1.0 / total

    cots = jnp.concatenate([bias_ref[c, tokens : tokens + tile] for c in range(cols)], axis=0)
    grad_out = nt(cots, wdec_ref[...])
    grad_low = grad_out.astype(BF)
    grad_att = nt(grad_low, wout_ref[...]).astype(BF)
    grad_att_t = nt(wout_ref[...], grad_low).astype(BF)
    attended = jnp.zeros((tokens, HD), F32)
    delta = jnp.zeros((tokens, 1), F32)
    for b in range(blocks):
        probs = s_ref[b] * share
        s_ref[b] = probs
        values = kv_ref[HD:, spans[b]]
        attended = attended + nt(probs.astype(BF), values)
        grad_probs = nn(grad_att, values)
        g_ref[b] = grad_probs
        delta = delta + jnp.sum(probs * grad_probs, axis=-1, keepdims=True)
    update = nn(attended.astype(BF), wout_ref[...]).astype(BF)
    back = nn(update, wdec_ref[...]).astype(BF)
    for c in range(cols):
        out_ref[c, tokens + half : tokens + half + tile] = back[c * tile : (c + 1) * tile]

    grad_queries = jnp.zeros((tokens, HD), F32)
    for b in range(blocks):
        probs = s_ref[b]
        low = (probs * (g_ref[b] - delta)).astype(BF)
        out_ref[2 * b, :tokens] = low[:, :half]
        out_ref[2 * b + 1, :tokens] = low[:, half:]
        grad_queries = grad_queries + nt(low, kv_ref[:HD, spans[b]])
        grad_k = (nn(qt_ref[...], low) * scale).astype(BF)
        grad_v = nn(grad_att_t, probs.astype(BF)).astype(BF)
        u_ref[b] = tn(jnp.concatenate([grad_k, grad_v], axis=0), wt_ref[HD:])
    own = nn((grad_queries * scale).astype(BF), wt_ref[:HD])
    u_ref[at[0]] += own
    first = (at[1] == 0).astype(F32)
    for b in range(blocks):
        upstream = u_ref[b]
        normal = normed_ref[spans[b]].astype(F32)
        part = inv_ref[spans[b]] * (
            upstream
            - jnp.mean(upstream, axis=-1, keepdims=True)
            - normal * jnp.mean(upstream * normal, axis=-1, keepdims=True)
        )
        here = first * (at[0] == b).astype(F32)
        part = nt((part + grad_out * here).astype(BF), wpool_ref[...]).astype(BF)
        out_ref[2 * b, tokens : tokens + half] = part[:half]
        out_ref[2 * b + 1, tokens : tokens + half] = part[half:]


def attend(at, queries, queries_t, kv_t, bias, w_t, normed, inverse, w_pool, w_out, w_dec, rows):
    tokens = queries.shape[0]
    features = w_t.shape[1]
    cols, _, half = bias.shape
    vmem = pl.BlockSpec(memory_space=pltpu.VMEM)
    return pl.pallas_call(
        attend_kernel,
        in_specs=[pl.BlockSpec(memory_space=pltpu.SMEM)] + [vmem] * 10,
        out_specs=vmem,
        out_shape=jax.ShapeDtypeStruct((cols, tokens + half + tokens // cols, half), BF),
        scratch_shapes=[
            pltpu.VMEM((rows, tokens, 2 * half), F32),
            pltpu.VMEM((rows, tokens, 2 * half), F32),
            pltpu.VMEM((rows, tokens, features), F32),
        ],
        compiler_params=pltpu.CompilerParams(vmem_limit_bytes=40 * 2**20),
        cost_estimate=pl.CostEstimate(
            flops=2 * 10**9, bytes_accessed=8 * 2**20, transcendentals=2**19
        ),
    )(at, queries, queries_t, kv_t, bias, w_t, normed, inverse, w_pool, w_out, w_dec)


def on_device(
    atom_single, atom_token, atom_cot, token_cond, pair, w_pool, w_qkv, w_bias, w_out, w_dec
):
    rows, cols = lax.axis_size("row"), lax.axis_size("col")
    row, col = lax.axis_index("row"), lax.axis_index("col")
    tok_rows = token_cond.shape[0]
    total_tokens = tok_rows * rows
    n_atoms, width = atom_single.shape
    tile = tok_rows // cols

    everyone = ("row", "col")
    devices = rows * cols
    cond_all = lax.all_gather(token_cond, "row", axis=0, tiled=True)
    onehot = (
        jnp.arange(total_tokens, dtype=jnp.int32)[:, None] == atom_token[None, :]
    ).astype(BF)
    with_ones = jnp.concatenate([atom_single, atom_cot, jnp.ones_like(atom_single)], axis=1)
    partial = nn(onehot, with_ones).reshape(devices, tile, 3 * width)
    place = jnp.eye(tile, width, dtype=F32)
    partial_counts = jnp.sum(partial[:, :, 2 * width :] * place, axis=1, keepdims=True)
    to_tiles = jnp.concatenate(
        [
            partial[:, :, :width].astype(BF),
            partial[:, :, width : 2 * width].astype(BF),
            jnp.pad(partial_counts.astype(BF), ((0, 0), (0, 7), (0, 0))),
        ],
        axis=1,
    )
    from_all = exchange(to_tiles, everyone)
    bias_local = jnp.einsum("ijc,ch->hij", pair, w_bias, preferred_element_type=F32).astype(BF)
    from_all = after(from_all, bias_local)
    sums = jnp.sum(from_all.astype(F32), axis=0)
    tile_counts = jnp.sum(sums[2 * tile : 2 * tile + 1] * place, axis=1, keepdims=True)
    pooled_tile = (sums[:tile] / tile_counts).astype(BF)
    cot_tile = sums[tile : 2 * tile].astype(BF)
    pooled = spread(pooled_tile, everyone).reshape(total_tokens, width)
    lanes = jnp.arange(width, dtype=jnp.int32)[None]
    seat = jnp.arange(tile, dtype=jnp.int32)[:, None] + tile * (col % (cols // 2))
    count_row = jnp.sum(jnp.where(lanes == seat, tile_counts, 0.0), axis=0, keepdims=True)
    count_row = jnp.where(jnp.arange(tile)[:, None] == col // (cols // 2), count_row, 0.0)
    shared = jnp.broadcast_to(
        jnp.concatenate([cot_tile, count_row.astype(BF)], axis=0)[None], (cols, 2 * tile, width)
    )
    bias_cot = exchange(after(jnp.concatenate([bias_local, shared], axis=1), pooled), "col")

    at = jnp.stack([row, col]).astype(jnp.int32)
    w_t = jnp.transpose(w_qkv, (0, 2, 1)).reshape(3 * HD, -1)
    normed, inverse, kv_t, queries, queries_t = norm_tokens(
        at, cond_all, pooled, w_pool, w_t, rows
    )
    at_tile = row * tok_rows + col * tile
    single_tile = lax.dynamic_slice_in_dim(cond_all, at_tile, tile, 0).astype(F32) + nn(
        pooled_tile, w_pool
    )
    tile_base = nn(single_tile.astype(BF), w_dec)
    bias_cot = after(bias_cot, kv_t, tile_base)
    row_counts = jnp.sum(bias_cot[:, tok_rows + tile : tok_rows + tile + 2].astype(F32), axis=0)
    columns = total_tokens // cols
    block_counts = jnp.where(
        row == col // 2, lax.dynamic_slice_in_dim(row_counts, col % 2, 1, 0), 0.0
    ).astype(BF)

    hop = attend(
        at, queries, queries_t, kv_t, bias_cot, w_t, normed, inverse, w_pool, w_out, w_dec, rows
    )
    hop = exchange(hop, "col")
    bias_back = hop[:, :tok_rows]
    rest = jnp.sum(hop[:, tok_rows:].astype(F32), axis=0)
    weight_part = jnp.einsum("ijc,hij->hc", pair, bias_back, preferred_element_type=F32)
    heads = weight_part.shape[0]
    hop = spread(
        jnp.concatenate(
            [rest[:columns].astype(BF), (tile_base + rest[columns:]).astype(BF)]
            + high_low(weight_part)
            + [jnp.pad(block_counts, ((0, 15), (0, 0)))],
            axis=0,
        ),
        "row",
    )
    at_counts = columns + tile + 2 * heads
    count_row = jnp.sum(hop[:, at_counts : at_counts + 1].astype(F32), axis=0)
    own_counts = jnp.sum(count_row * jnp.eye(columns, dtype=F32), axis=1, keepdims=True)
    token_grad = (jnp.sum(hop[:, :columns].astype(F32), axis=0) / own_counts).astype(BF)
    token_back = hop[:, columns : columns + tile].reshape(columns, width)
    weight_col = jnp.sum(hop[:, columns + tile : at_counts].astype(F32), axis=0)
    hop = spread(
        jnp.concatenate(
            [token_grad, token_back] + high_low(weight_col[:heads] + weight_col[heads:]), axis=0
        ),
        "col",
    )
    grad_table = hop[:, :columns].reshape(total_tokens, width)
    back_table = hop[:, columns : 2 * columns].reshape(total_tokens, width)
    weight = jnp.sum(hop[:, 2 * columns :].astype(F32), axis=0)
    of_row, rest = atom_token // tok_rows, atom_token % tok_rows
    back_ids = (rest // tile) * columns + of_row * tile + rest % tile
    slots = jnp.arange(total_tokens, dtype=jnp.int32)[None, :]
    grad_atom = atom_cot.astype(F32) + nn((atom_token[:, None] == slots).astype(BF), grad_table)
    atom_out = (
        atom_single.astype(F32) + nn((back_ids[:, None] == slots).astype(BF), back_table)
    ).astype(BF)
    grad_bias = jnp.transpose(weight[:heads] + weight[heads:])
    return (atom_out, grad_atom, grad_bias)


def solution(mesh):
    return jax.shard_map(
        on_device,
        mesh=mesh,
        in_specs=(
            P(("row", "col"), None),
            P(("row", "col")),
            P(("row", "col"), None),
            P("row", None),
            P("row", "col", None),
            P(),
            P(None, None, "col"),
            P(),
            P("col", None),
            P(),
        ),
        out_specs=(P(("row", "col"), None), P(("row", "col"), None), P()),
        check_vma=False,
    )
```

time: 194 us -> 180 us (0.928)
  waiting for transfers between devices: 92.1 us -> 74 us
  Pallas kernels: 0 us -> 16.6 us
  starting transfers between devices: 42.7 us -> 28.9 us
  between operations: 1.06 us -> 14.4 us
  matrix products: 24.8 us -> 15.4 us
  other arithmetic: 8.97 us -> 4.34 us
  local copies, waits for them, and re-layouts: 7.09 us -> 10.1 us
  blocking collectives: 16.1 us -> 13.7 us
    all_to_all x8 -> x5, waiting for transfers between devices: 92.1 us -> 73.3 us  [exchange(): return lax.all_to_all(blocks, axis, split_axis=0, concat_axis=0, tiled=True)]
    pallas_call x0 -> x2, Pallas kernels: none -> 16.6 us  [the longest x1 9.69 us: attend(): pl.pallas_call(attend_kernel, in_specs=[pl.BlockSpec(memory_space=pltpu.S...]
    all_to_all x8 -> x5, starting transfers between devices: 42.7 us -> 28.9 us  [exchange(): return lax.all_to_all(blocks, axis, split_axis=0, concat_axis=0, tiled=True)]
    unnamed x27 -> x28, local copies, waits for them, and re-layouts: 1.13 us -> 7.31 us
    dot_general x10 -> x0, matrix products: 5.95 us -> none  [the longest x4 3.2 us: tn(): lax.dot_general(left, right, (((0,), (0,)), ((), ())), preferred_element_...]
    dot_general x8 -> x4, matrix products: 8.2 us -> 4.31 us  [nn(): return jnp.dot(left, right, preferred_element_type=F32)]
    all_to_all x1, blocking collectives: 16.1 us -> 13.7 us  [exchange(): return lax.all_to_all(blocks, axis, split_axis=0, concat_axis=0, tiled=True)]
  transfers between devices with their start and end apart: 8 -> 6, of which waited for: 8 -> 5; matrix products, arithmetic and copies ran while one was open for 7% -> 7% of each run, Pallas kernels for 0% -> 4%
where the time goes in v2:
time: 180 us; the launch traced here: 177 us
  waiting for transfers between devices  74 us (41%)
  starting transfers between devices  28.9 us (16%)
  Pallas kernels  16.6 us (9%)
  matrix products  15.4 us (9%)
  between operations  14.4 us (8%)
  blocking collectives  13.7 us (8%)
  local copies, waits for them, and re-layouts  10.1 us (6%)
  other arithmetic  4.34 us (2%)
    all_to_all x5, waiting for transfers between devices, exchange(): return lax.all_to_all(blocks, axis, split_axis=0, concat_axis=0, tiled=True)  73.3 us
    all_to_all x5, starting transfers between devices, exchange(): return lax.all_to_all(blocks, axis, split_axis=0, concat_axis=0, tiled=True)  28.9 us
    all_to_all x1, blocking collectives, exchange(): return lax.all_to_all(blocks, axis, split_axis=0, concat_axis=0, tiled=True)  13.7 us
    pallas_call x1, Pallas kernels, attend(): pl.pallas_call(attend_kernel, in_specs=[pl.BlockSpec(memory_space=pltpu.S...  9.69 us
    unnamed x28, local copies, waits for them, and re-layouts  7.31 us
    pallas_call x1, Pallas kernels, norm_tokens(): pl.pallas_call(norm_kernel, grid=(rows,), in_specs=[pl.BlockSpec(memory_s...  6.88 us
    dot_general x1, matrix products, on_device(): jnp.einsum('ijc,ch->hij', pair, w_bias, preferred_element_type=F32)  5.93 us
    dot_general x1, matrix products, on_device(): jnp.einsum('ijc,hij->hc', pair, bias_back, preferred_element_type=F32)  5.14 us
  transfers between devices with their start and end apart: 6, of which 5 were waited for; matrix products, arithmetic and copies ran while one was open for 7% of the time, Pallas kernels for 4%

profile of v2, /device:TPU:1, one launch (start us, length us, event | category | flops | bytes accessed | tf_op | source)
XLA Modules:
  0.0 177.5 jit_solution(12885990756644023148)
XLA Ops:
  8.0 1.4 bitcast_convert_fusion
  9.8 1.3 fusion.1
  11.1 11.5 %all-to-all-start = ((bf16[128,40,128]{2,1,0:T(8,128)(2,1)}), bf16[128,40,128]{2,1,0:T(8,128)(2,1)S(1)}, u32[]{:S(2)}, u32[]{:S(2)}) async-start(bf16[128,40,128]{2,1,0:T(8,128)(2,1)} %fusion.1), calls=%async_computation | async-start | bytes 2621440 | tf_op jit(solution)/shard_map/all_to_all | solution.py:31
  22.6 5.9 %fusion.23 = bf16[16,256,128]{2,0,1:T(8,128)(2,1)S(1)} fusion(bf16[256,128,128]{2,1,0:T(8,128)(2,1)} %param.14, bf16[128,16]{0,1:T(8,128)(2,1)S(1)} %copy-done), kind=kOutput, calls=%fused_computation.63 | convolution fusion | flops 134217728 | bytes 9441280 | tf_op jit(solution)/shard_map/ijc,ch->hij/dot_general | solution.py:220
  28.9 15.2 %all-to-all-done = bf16[128,40,128]{2,1,0:T(8,128)(2,1)S(1)} async-done(((bf16[128,40,128]{2,1,0:T(8,128)(2,1)}), bf16[128,40,128]{2,1,0:T(8,128)(2,1)S(1)}, u32[]{:S(2)}, u32[]{:S(2)}) %all-to-all-start) | async-done | bytes 1310752 | tf_op jit(solution)/shard_map/all_to_all | solution.py:31
  45.4 4.9 %all-to-all-start.1 = ((bf16[128,16,128]{2,1,0:T(8,128)(2,1)}), bf16[128,16,128]{2,1,0:T(8,128)(2,1)S(1)}, u32[]{:S(2)}, u32[]{:S(2)}) async-start(bf16[128,16,128]{2,1,0:T(8,128)(2,1)} %broadcast_in_dim.40), calls=%async_computation.1 | async-start | bytes 1048576 | tf_op jit(solution)/shard_map/all_to_all | solution.py:31
  50.4 1.1 pad_maximum_fusion
  51.5 12.8 %all-to-all-done.1 = bf16[128,16,128]{2,1,0:T(8,128)(2,1)S(1)} async-done(((bf16[128,16,128]{2,1,0:T(8,128)(2,1)}), bf16[128,16,128]{2,1,0:T(8,128)(2,1)S(1)}, u32[]{:S(2)}, u32[]{:S(2)}) %all-to-all-start.1) | async-done | bytes 524320 | tf_op jit(solution)/shard_map/all_to_all | solution.py:31
  64.3 3.9 %all-to-all-start.2 = ((bf16[16,288,128]{2,1,0:T(8,128)(2,1)}), bf16[16,288,128]{2,1,0:T(8,128)(2,1)S(1)}, u32[]{:S(2)}, u32[]{:S(2)}) async-start(bf16[16,288,128]{2,1,0:T(8,128)(2,1)} %pad_maximum_fusion), calls=%async_computation.2 | async-start | bytes 2359296 | tf_op jit(solution)/shard_map/all_to_all | solution.py:31
  68.3 1.9 %copy-done.1 = bf16[2048,768]{1,0:T(8,128)(2,1)S(1)} copy-done((bf16[2048,768]{1,0:T(8,128)(2,1)S(1)}, bf16[2048,768]{1,0:T(8,128)(2,1)}, u32[]{:S(2)}) %copy-start.1) | copy-done | bytes 3145752
  70.2 6.9 %shard_map.121 = (bf16[2048,768]{1,0:T(8,128)(2,1)S(1)}, f32[2048,1]{1,0:T(8,128)S(1)}, bf16[96,2048]{1,0:T(8,128)(2,1)S(1)}, bf16[256,48]{1,0:T(8,128)(2,1)S(1)}, bf16[48,256]{1,0:T(8,128)(2,1)S(1)}) custom-call(s32[2]{0:T(128)S(1)} %pad_add_fusion.at, bf16[2048,768]{1,0:T(8,128)(2,1)S(1)} %copy-done.1, bf16[2048,128]{1,0:T(8,128)(2,1)S(1)} %bitcast.30, ...), custom_call_target="tpu_custom_call" | custom-call | flops 855638016 | bytes 8388608 | tf_op jit(solution)/shard_map/pallas_call | solution.py:66
  77.1 1.7 copy-done.2
  79.5 1.0 fusion.4
  80.5 5.1 %all-to-all-done.2.bias_ref = bf16[16,288,128]{2,1,0:T(8,128)(2,1)S(1)} async-done(((bf16[16,288,128]{2,1,0:T(8,128)(2,1)}), bf16[16,288,128]{2,1,0:T(8,128)(2,1)S(1)}, u32[]{:S(2)}, u32[]{:S(2)}) %all-to-all-start.2) | async-done | bytes 1179680 | tf_op jit(solution)/shard_map/all_to_all | solution.py:31
  85.6 1.9 %copy-done.3 = bf16[2048,768]{1,0:T(8,128)(2,1)S(1)} copy-done((bf16[2048,768]{1,0:T(8,128)(2,1)S(1)}, bf16[2048,768]{1,0:T(8,128)(2,1)}, u32[]{:S(2)}) %copy-start.3) | copy-done | bytes 3145752
  87.5 1.0 copy-done.8
  88.5 9.7 %shard_map.122 = bf16[16,400,128]{2,1,0:T(8,128)(2,1)} custom-call(s32[2]{0:T(128)S(1)} %pad_add_fusion.at, bf16[256,48]{1,0:T(8,128)(2,1)S(1)} %get-tuple-element.12.q_ref, bf16[48,256]{1,0:T(8,128)(2,1)S(1)} %get-tuple-element.13.qt_ref, bf16[96,2048]{1,0:T(8,128)(2,1)S(1)} %copy-done.8, bf16[16,288,128]{2,1,0:T(8,128)(2,1)S(1)} %all-to-all-done.2.bias_ref, ...), custom_call_target="tpu_custom_call" | custom-call | flops 2000000000 | bytes 8388608 | tf_op jit(solution)/shard_map/pallas_call | solution.py:174
  98.2 5.0 %all-to-all-start.3 = ((bf16[16,400,128]{2,1,0:T(8,128)(2,1)}), bf16[16,400,128]{2,1,0:T(8,128)(2,1)S(1)}, u32[]{:S(2)}, u32[]{:S(2)}) async-start(bf16[16,400,128]{2,1,0:T(8,128)(2,1)} %shard_map.122), calls=%async_computation.3 | async-start | bytes 3276800 | tf_op jit(solution)/shard_map/all_to_all | solution.py:31
  103.3 22.8 %all-to-all-done.3 = bf16[16,400,128]{2,1,0:T(8,128)(2,1)S(1)} async-done(((bf16[16,400,128]{2,1,0:T(8,128)(2,1)}), bf16[16,400,128]{2,1,0:T(8,128)(2,1)S(1)}, u32[]{:S(2)}, u32[]{:S(2)}) %all-to-all-start.3) | async-done | bytes 1638432 | tf_op jit(solution)/shard_map/all_to_all | solution.py:31
  126.3 5.1 %constant_dynamic-update-slice_fusion.2 = (bf16[192,128]{1,0:T(8,128)(2,1)S(1)}, f32[16,128]{1,0:T(8,128)S(1)}) fusion(bf16[192,128]{1,0:T(8,128)(2,1)S(1)} %constant_dynamic-update-slice_fusion.3, bf16[256,128,128]{2,1,0:T(8,128)(2,1)} %param.14, bf16[16,256,128]{2,1,0:T(8,128)(2,1)S(1)} %slice.101), kind=kOutput, calls=%fused_computation.44 | convolution fusion | flops 134219776 | bytes 9449472 | tf_op jit(solution)/shard_map/ijc,hij->hc/dot_general | solution.py:259
  131.5 13.7 %all_to_all.30 = bf16[8,192,128]{2,1,0:T(8,128)(2,1)S(1)} all-to-all(bf16[8,192,128]{2,1,0:T(8,128)(2,1)S(1)} %broadcast_in_dim.46), channel_id=1, replica_groups=mesh['row'=8,'col'=16] {'row'}, dimensions={0} | all-to-all | bytes 786432 | tf_op jit(solution)/shard_map/all_to_all | solution.py:31
  145.6 1.2 broadcast_in_dim.47
  146.7 3.7 %all-to-all-start.5 = ((bf16[16,288,128]{2,1,0:T(8,128)(2,1)}), bf16[16,288,128]{2,1,0:T(8,128)(2,1)S(1)}, u32[]{:S(2)}, u32[]{:S(2)}) async-start(bf16[16,288,128]{2,1,0:T(8,128)(2,1)} %broadcast_in_dim.47), calls=%async_computation.5 | async-start | bytes 2359296 | tf_op jit(solution)/shard_map/all_to_all | solution.py:31
  150.5 17.4 %all-to-all-done.5 = bf16[16,288,128]{2,1,0:T(8,128)(2,1)S(1)} async-done(((bf16[16,288,128]{2,1,0:T(8,128)(2,1)}), bf16[16,288,128]{2,1,0:T(8,128)(2,1)S(1)}, u32[]{:S(2)}, u32[]{:S(2)}) %all-to-all-start.5) | async-done | bytes 1179680 | tf_op jit(solution)/shard_map/all_to_all | solution.py:31
  (68 shorter events, 7.1 us)
Async XLA Ops:
  7.2 15.5 %copy-start = (bf16[128,16]{0,1:T(8,128)(2,1)S(1)}, bf16[128,16]{0,1:T(8,128)(2,1)}, u32[]{:S(2)}) copy-start(bf16[128,16]{0,1:T(8,128)(2,1)} %param.17) | copy-start | bytes 12292
  7.2 61.1 %all-gather.2.cloned.1.call-start = ((), (), s32[]{:S(2)}) async-start(), calls=%async_computation.6 | async-start | bytes 3538944 | tf_op jit(solution)/shard_map/all_gather | solution.py:203
  11.1 33.0 %all-to-all-start = ((bf16[128,40,128]{2,1,0:T(8,128)(2,1)}), bf16[128,40,128]{2,1,0:T(8,128)(2,1)S(1)}, u32[]{:S(2)}, u32[]{:S(2)}) async-start(bf16[128,40,128]{2,1,0:T(8,128)(2,1)} %fusion.1), calls=%async_computation | async-start | bytes 2621440 | tf_op jit(solution)/shard_map/all_to_all | solution.py:31
  45.4 18.9 %all-to-all-start.1 = ((bf16[128,16,128]{2,1,0:T(8,128)(2,1)}), bf16[128,16,128]{2,1,0:T(8,128)(2,1)S(1)}, u32[]{:S(2)}, u32[]{:S(2)}) async-start(bf16[128,16,128]{2,1,0:T(8,128)(2,1)} %broadcast_in_dim.40), calls=%async_computation.1 | async-start | bytes 1048576 | tf_op jit(solution)/shard_map/all_to_all | solution.py:31
  51.5 16.8 %copy-start.4 = (bf16[128,768]{1,0:T(8,128)(2,1)S(1)}, bf16[128,768]{1,0:T(8,128)(2,1)}, u32[]{:S(2)}) copy-start(bf16[128,768]{1,0:T(8,128)(2,1)} %wpool_ref.3) | copy-start | bytes 589828
  51.5 16.8 %copy-start.5 = (bf16[3,768,48]{1,2,0:T(8,128)(2,1)S(1)}, bf16[3,768,48]{1,2,0:T(8,128)(2,1)}, u32[]{:S(2)}) copy-start(bf16[3,768,48]{1,2,0:T(8,128)(2,1)} %param.16) | copy-start | bytes 663556
  64.3 21.3 %all-to-all-start.2 = ((bf16[16,288,128]{2,1,0:T(8,128)(2,1)}), bf16[16,288,128]{2,1,0:T(8,128)(2,1)S(1)}, u32[]{:S(2)}, u32[]{:S(2)}) async-start(bf16[16,288,128]{2,1,0:T(8,128)(2,1)} %pad_maximum_fusion), calls=%async_computation.2 | async-start | bytes 2359296 | tf_op jit(solution)/shard_map/all_to_all | solution.py:31
  68.3 1.9 %copy-start.1 = (bf16[2048,768]{1,0:T(8,128)(2,1)S(1)}, bf16[2048,768]{1,0:T(8,128)(2,1)}, u32[]{:S(2)}) copy-start(bf16[2048,768]{1,0:T(8,128)(2,1)} %all-gather.2.cloned.1.call-done.cond_ref) | copy-start | bytes 9437188
  70.2 9.3 %copy-start.6 = (bf16[768,128]{1,0:T(8,128)(2,1)S(1)}, bf16[768,128]{1,0:T(8,128)(2,1)}, u32[]{:S(2)}) copy-start(bf16[768,128]{1,0:T(8,128)(2,1)} %wdec_ref.1) | copy-start | bytes 589828
  70.2 15.4 %copy-start.9 = (bf16[48,768]{1,0:T(8,128)(2,1)S(1)}, bf16[48,768]{1,0:T(8,128)(2,1)}, u32[]{:S(2)}) copy-start(bf16[48,768]{1,0:T(8,128)(2,1)} %wout_ref.1) | copy-start | bytes 221188
  77.1 1.7 copy-start.2
  78.8 0.7 copy-start.7
  85.6 1.9 %copy-start.3 = (bf16[2048,768]{1,0:T(8,128)(2,1)S(1)}, bf16[2048,768]{1,0:T(8,128)(2,1)}, u32[]{:S(2)}) copy-start(bf16[2048,768]{1,0:T(8,128)(2,1)} %copy-done.2) | copy-start | bytes 9437188
  87.5 1.0 copy-start.8
  98.2 27.9 %all-to-all-start.3 = ((bf16[16,400,128]{2,1,0:T(8,128)(2,1)}), bf16[16,400,128]{2,1,0:T(8,128)(2,1)S(1)}, u32[]{:S(2)}, u32[]{:S(2)}) async-start(bf16[16,400,128]{2,1,0:T(8,128)(2,1)} %shard_map.122), calls=%async_computation.3 | async-start | bytes 3276800 | tf_op jit(solution)/shard_map/all_to_all | solution.py:31
  145.6 4.9 %copy-start.12 = (s32[128]{0:T(128)S(1)}, s32[128]{0:T(128)}, u32[]{:S(2)}) copy-start(s32[128]{0:T(128)} %param.11) | copy-start | bytes 1540
  146.7 21.2 %all-to-all-start.5 = ((bf16[16,288,128]{2,1,0:T(8,128)(2,1)}), bf16[16,288,128]{2,1,0:T(8,128)(2,1)S(1)}, u32[]{:S(2)}, u32[]{:S(2)}) async-start(bf16[16,288,128]{2,1,0:T(8,128)(2,1)} %broadcast_in_dim.47), calls=%async_computation.5 | async-start | bytes 2359296 | tf_op jit(solution)/shard_map/all_to_all | solution.py:31
  150.5 17.6 %copy-start.10 = (bf16[128,128]{1,0:T(8,128)(2,1)S(1)}, bf16[128,128]{1,0:T(8,128)(2,1)}, u32[]{:S(2)}) copy-start(bf16[128,128]{1,0:T(8,128)(2,1)} %param.12) | copy-start | bytes 98308
  150.5 19.2 %copy-start.11 = (bf16[128,128]{1,0:T(8,128)(2,1)S(1)}, bf16[128,128]{1,0:T(8,128)(2,1)}, u32[]{:S(2)}) copy-start(bf16[128,128]{1,0:T(8,128)(2,1)} %param.10) | copy-start | bytes 98308
Sparse Core Ops, SparseCore 0:
  9.7 45.4 all-gather.1

commit v3 on v2

v3 whole, which is shorter than its diff:
```python
import math

import jax
import jax.numpy as jnp
from jax import lax
from jax.experimental import pallas as pl
from jax.experimental.pallas import tpu as pltpu
from jax.sharding import Mesh
from jax.sharding import PartitionSpec as P

HD = 48


EPSILON = 1e-05
BF = jnp.bfloat16
F32 = jnp.float32


def nt(left, right):
    return lax.dot_general(left, right, (((1,), (1,)), ((), ())), preferred_element_type=F32)


def tn(left, right):
    return lax.dot_general(left, right, (((0,), (0,)), ((), ())), preferred_element_type=F32)


def nn(left, right):
    return jnp.dot(left, right, preferred_element_type=F32)


def exchange(blocks, axis):
    return lax.all_to_all(blocks, axis, split_axis=0, concat_axis=0, tiled=True)


def spread(block, axis):
    return exchange(jnp.broadcast_to(block[None], (lax.axis_size(axis),) + block.shape), axis)


def after(value, *others):
    return lax.optimization_barrier((value,) + others)[0]


def high_low(value):
    high = value.astype(BF)
    return [high, (value - high.astype(F32)).astype(BF)]


def norm_kernel(
    at, cond0, cond1, cond2, cond3, cond4, cond5, cond6, cond7, pooled_ref, pooled_other, wt_ref,
    wpool_ref, normed_ref, inv_ref, kv_ref, q_ref, qt_ref,
):
    cols, half, _ = normed_ref.shape
    conds = (cond0, cond1, cond2, cond3, cond4, cond5, cond6, cond7)
    for step in range(cols // 2):
        at_z = jnp.bitwise_xor(at[2], step // 2)
        b = 2 * at_z + jnp.bitwise_xor(at[3], step % 2)
        pools = pooled_other if step % 2 else pooled_ref
        single = conds[step][...].astype(F32) + nn(pools[at_z], wpool_ref[...])
        center = single - jnp.mean(single, axis=-1, keepdims=True)
        inverse = lax.rsqrt(jnp.mean(center * center, axis=-1, keepdims=True) + EPSILON)
        normed = (center * inverse).astype(BF)
        kv = nt(wt_ref[HD:], normed).astype(BF)
        for i in range(2):
            part = slice(i * half, (i + 1) * half)
            normed_ref[2 * b + i] = normed[part]
            inv_ref[2 * b + i] = inverse[part]
            kv_ref[2 * b + i] = kv[:, part]
        if step == 0:
            q_ref[...] = nt(normed, wt_ref[:HD]).astype(BF)
            qt_ref[...] = nt(wt_ref[:HD], normed).astype(BF)


def attend_kernel(
    q_ref, qt_ref, kv_ref, bias_ref, wout_ref, wdec_ref,
    out_ref, gkv_ref, gq_ref, att_ref, gout_ref, s_ref, g_ref,
):
    scale = 1.0 / math.sqrt(HD)
    blocks, tokens, columns = s_ref.shape
    half = columns // 2
    cols = 2 * blocks
    tile = tokens // cols

    def pair(ref, b, rows):
        return jnp.concatenate([ref[2 * b, rows], ref[2 * b + 1, rows]], axis=1)

    keys, values = slice(0, HD), slice(HD, 2 * HD)
    queries = q_ref[...]
    top = jnp.full((tokens, 1), -jnp.inf, F32)
    for b in range(blocks):
        bias = pair(bias_ref, b, slice(0, tokens))
        logits = nn(queries, pair(kv_ref, b, keys)) * scale + bias.astype(F32)
        s_ref[b] = logits
        top = jnp.maximum(top, jnp.max(logits, axis=-1, keepdims=True))
    total = jnp.zeros((tokens, 1), F32)
    for b in range(blocks):
        shifted = jnp.exp(s_ref[b] - top)
        s_ref[b] = shifted
        total = total + jnp.sum(shifted, axis=-1, keepdims=True)
    share = 1.0 / total

    cots = jnp.concatenate([bias_ref[c, tokens : tokens + tile] for c in range(cols)], axis=0)
    grad_out = nt(cots, wdec_ref[...])
    gout_ref[...] = grad_out
    grad_low = grad_out.astype(BF)
    grad_att = nt(grad_low, wout_ref[...]).astype(BF)
    grad_att_t = nt(wout_ref[...], grad_low).astype(BF)
    attended = jnp.zeros((tokens, HD), F32)
    delta = jnp.zeros((tokens, 1), F32)
    for b in range(blocks):
        probs = s_ref[b] * share
        s_ref[b] = probs
        block = pair(kv_ref, b, values)
        attended = attended + nt(probs.astype(BF), block)
        grad_probs = nn(grad_att, block)
        g_ref[b] = grad_probs
        delta = delta + jnp.sum(probs * grad_probs, axis=-1, keepdims=True)
    att_ref[...] = attended.astype(BF)

    grad_queries = jnp.zeros((tokens, HD), F32)
    for b in range(blocks):
        probs = s_ref[b]
        low = (probs * (g_ref[b] - delta)).astype(BF)
        out_ref[2 * b] = low[:, :half]
        out_ref[2 * b + 1] = low[:, half:]
        grad_queries = grad_queries + nt(low, pair(kv_ref, b, keys))
        grad_k = (nn(qt_ref[...], low) * scale).astype(BF)
        grad_v = nn(grad_att_t, probs.astype(BF)).astype(BF)
        gkv_ref[:, b * columns : (b + 1) * columns] = jnp.concatenate([grad_k, grad_v], axis=0)
    gq_ref[...] = (grad_queries * scale).astype(BF)


def token_grad_kernel(
    at, gkv_ref, gq_ref, att_ref, gout_ref, normed_ref, inv_ref, wt_ref, wpool_ref, wout_ref,
    wdec_ref, mine_ref, other_ref, back_ref, u_ref,
):
    cols, half, _ = normed_ref.shape
    tile, short = back_ref.shape[1], half // 2
    row, col, core = at[0], at[1], at[3]
    update = nn(att_ref[...], wout_ref[...]).astype(BF)
    back = nn(update, wdec_ref[...]).astype(BF)
    for c in range(cols):
        back_ref[c] = back[c * tile : (c + 1) * tile]
    for b in range(cols // 2):
        columns = slice(2 * b * half, 2 * (b + 1) * half)
        upstream = tn(gkv_ref[:, columns], wt_ref[HD:])
        u_ref[2 * b] = upstream[:half]
        u_ref[2 * b + 1] = upstream[half:]
    own = nn(gq_ref[...], wt_ref[:HD])
    u_ref[2 * row] += own[:half]
    u_ref[2 * row + 1] += own[half:]
    head = (col == 0).astype(F32)
    for c in range(cols):
        upstream = u_ref[c]
        normal = normed_ref[c].astype(F32)
        part = inv_ref[c] * (
            upstream
            - jnp.mean(upstream, axis=-1, keepdims=True)
            - normal * jnp.mean(upstream * normal, axis=-1, keepdims=True)
        )
        here = head * (row == c // 2).astype(F32)
        at_half = (c % 2) * half
        part = part + gout_ref[at_half : at_half + half] * here
        grad = nt(part.astype(BF), wpool_ref[...])
        mine_ref[c] = jnp.where(core == 0, grad[:short], grad[short:])
        other_ref[c] = jnp.where(core == 0, grad[short:], grad[:short]).astype(BF)


def call(body, outs, scratch, cost, *args, scalars=None):
    n_in, n_out, n_at = len(args), len(outs), int(scalars is not None)

    def kernel(*refs):
        at, refs = refs[:n_at], refs[n_at:]
        sources, results = refs[:n_in], refs[n_in : n_in + n_out]
        held = refs[n_in + n_out : 2 * (n_in + n_out)]
        sems, rest = refs[2 * (n_in + n_out)], refs[2 * (n_in + n_out) + 1 :]
        incoming = [
            pltpu.make_async_copy(src, dst, sems.at[i])
            for i, (src, dst) in enumerate(zip(sources, held[:n_in]))
        ]
        for copy in incoming:
            copy.start()
        for copy in incoming:
            copy.wait()
        body(*at, *held, *rest)
        outgoing = [
            pltpu.make_async_copy(src, dst, sems.at[n_in + i])
            for i, (src, dst) in enumerate(zip(held[n_in:], results))
        ]
        for copy in outgoing:
            copy.start()
        for copy in outgoing:
            copy.wait()

    anywhere = pl.BlockSpec(memory_space=pl.ANY)
    specs = [pl.BlockSpec(memory_space=pltpu.SMEM)] * n_at + [anywhere] * n_in
    return pl.pallas_call(
        kernel,
        in_specs=specs,
        out_specs=[anywhere] * n_out,
        out_shape=[jax.ShapeDtypeStruct(*out) for out in outs],
        scratch_shapes=[pltpu.VMEM(arg.shape, arg.dtype) for arg in args]
        + [pltpu.VMEM(*out) for out in outs]
        + [pltpu.SemaphoreType.DMA((n_in + n_out,))]
        + [pltpu.VMEM(*item) for item in scratch],
        compiler_params=pltpu.CompilerParams(vmem_limit_bytes=56 * 2**20),
        cost_estimate=pl.CostEstimate(
            flops=cost, bytes_accessed=8 * 2**20, transcendentals=2**19
        ),
    )(*([scalars] * n_at), *args)


ROW, COL, SAME_CORE = ("z", "k"), ("y", "x"), ("z", "y", "x")
SWAP = [(0, 1), (1, 0)]


def turn(value, axis, by):
    size = lax.axis_size(axis)
    return lax.ppermute(value, axis, [(i, i ^ by) for i in range(size)])


def take(value, start, size, axis=0):
    return lax.dynamic_slice_in_dim(value, start, size, axis)


def on_device(
    atom_single, atom_token, atom_cot, token_cond, pair, w_pool, w_qkv, w_bias, w_out, w_dec
):
    side = lax.axis_size("x")
    rows, cols = lax.axis_size("z") * 2, lax.axis_size("y") * side
    z, core, y, x = [lax.axis_index(name) for name in ("z", "k", "y", "x")]
    row, col = z * 2 + core, y * side + x
    tok_rows = token_cond.shape[0]
    total_tokens = tok_rows * rows
    n_atoms, width = atom_single.shape
    tile, columns = tok_rows // cols, total_tokens // cols
    peers = rows * cols // 2
    at = jnp.stack([row, col, z, core]).astype(jnp.int32)
    w_t = jnp.transpose(w_qkv, (0, 2, 1)).reshape(3 * HD, -1)

    own_atoms = jnp.concatenate([atom_single, atom_cot], axis=1)
    atoms = jnp.concatenate([own_atoms, lax.ppermute(own_atoms, "k", SWAP)], axis=0)
    ids = jnp.concatenate([atom_token, lax.ppermute(atom_token, "k", SWAP)])
    slots = jnp.arange(total_tokens // 2, dtype=jnp.int32)
    slots = (slots // tok_rows * 2 + core) * tok_rows + slots % tok_rows
    onehot = (slots[:, None] == ids[None, :]).astype(BF)
    with_ones = jnp.concatenate([atoms, jnp.ones((2 * n_atoms, width), BF)], axis=1)
    partial = nn(onehot, with_ones).reshape(peers, tile, 3 * width)
    place = jnp.eye(tile, width, dtype=F32)
    partial_counts = jnp.sum(partial[:, :, 2 * width :] * place, axis=1, keepdims=True)
    to_tiles = jnp.concatenate(
        [
            partial[:, :, :width].astype(BF),
            partial[:, :, width : 2 * width].astype(BF),
            jnp.pad(partial_counts.astype(BF), ((0, 0), (0, 7), (0, 0))),
        ],
        axis=1,
    )

    bias = jnp.einsum("ijc,ch->hij", pair, w_bias, preferred_element_type=F32).astype(BF)
    from_all = exchange(to_tiles, SAME_CORE)
    late_cond = after(token_cond, to_tiles)
    cond = [token_cond] + [turn(late_cond, "z", d) for d in (1, 2, 3)]
    from_all = after(from_all, bias)
    sums = jnp.sum(from_all.astype(F32), axis=0)
    tile_counts = jnp.sum(sums[2 * tile : 2 * tile + 1] * place, axis=1, keepdims=True)
    pooled_tile = (sums[:tile] / tile_counts).astype(BF)
    lanes = jnp.arange(width, dtype=jnp.int32)[None]
    seat = jnp.arange(tile, dtype=jnp.int32)[:, None] + tile * (col % (cols // 2))
    count_row = jnp.sum(jnp.where(lanes == seat, tile_counts, 0.0), axis=0, keepdims=True)
    count_row = jnp.where(jnp.arange(8)[:, None] == col // (cols // 2), count_row, 0.0)
    count_row = jnp.pad(count_row[:2], ((0, tile - 2), (0, 0)))
    shared = jnp.concatenate([sums[tile : 2 * tile], count_row], axis=0).astype(BF)
    shared = jnp.broadcast_to(shared[None], (cols, 2 * tile, width))
    pooled = spread(pooled_tile, SAME_CORE)
    conds = []
    for piece in cond:
        conds += [piece, lax.ppermute(piece, "k", SWAP)]
    pooled = after(pooled, *conds).reshape(rows // 2, tok_rows, width)
    bias_cot = exchange(after(jnp.concatenate([bias, shared], axis=1), pooled), COL)
    other_pooled = lax.ppermute(pooled, "k", SWAP)
    single_tile = take(token_cond, col * tile, tile).astype(F32) + nn(pooled_tile, w_pool)
    tile_base = nn(single_tile.astype(BF), w_dec)
    features = w_t.shape[1]
    normed, inverse, kv, queries, queries_t = call(
        norm_kernel,
        [
            ((cols, columns, features), BF),
            ((cols, columns, 1), F32),
            ((cols, 2 * HD, columns), BF),
            ((tok_rows, HD), BF),
            ((HD, tok_rows), BF),
        ],
        [], 10**9, *conds, pooled, other_pooled, w_t, w_pool, scalars=at,
    )
    bias_cot = after(bias_cot, kv, tile_base)
    row_counts = jnp.sum(bias_cot[:, tok_rows + tile : tok_rows + tile + 2].astype(F32), axis=0)
    block_counts = jnp.where(row == col // 2, take(row_counts, col % 2, 1), 0.0).astype(BF)

    spread_logits = (rows, tok_rows, 2 * columns)
    grad_logits, grad_kv, grad_queries, attended, grad_out = call(
        attend_kernel,
        [
            ((cols, tok_rows, columns), BF),
            ((2 * HD, total_tokens), BF),
            ((tok_rows, HD), BF),
            ((tok_rows, HD), BF),
            ((tok_rows, features), F32),
        ],
        [(spread_logits, F32), (spread_logits, F32)],
        2 * 10**9, queries, queries_t, kv, bias_cot, w_out, w_dec,
    )
    bias_back = exchange(grad_logits, COL)
    mine, other, back = call(
        token_grad_kernel,
        [
            ((cols, columns // 2, width), F32),
            ((cols, columns // 2, width), BF),
            ((cols, tile, width), BF),
        ],
        [((cols, columns, features), F32)],
        10**9,
        grad_kv, grad_queries, attended, grad_out, normed, inverse, w_t, w_pool, w_out, w_dec,
        scalars=at,
    )
    grad_part = (mine + lax.ppermute(other, "k", SWAP).astype(F32)).astype(BF)
    to_col = jnp.concatenate([grad_part, back], axis=1)
    bias_back = after(bias_back, to_col)
    hop = exchange(after(to_col, bias_back), COL)
    weight_part = jnp.einsum("ijc,hij->hc", pair, bias_back, preferred_element_type=F32)
    hop = after(hop, weight_part)
    rest = jnp.sum(hop.astype(F32), axis=0)
    heads = weight_part.shape[0]
    hop = spread(
        jnp.concatenate(
            [rest[: columns // 2].astype(BF), (tile_base + rest[columns // 2 :]).astype(BF)]
            + high_low(weight_part)
            + [jnp.pad(block_counts, ((0, 15), (0, 0)))],
            axis=0,
        ),
        ROW,
    )
    at_back = columns // 2
    at_weight = at_back + tile
    at_counts = at_weight + 2 * heads
    count_row = jnp.sum(hop[:, at_counts : at_counts + 1].astype(F32), axis=0)
    own_counts = jnp.sum(count_row * jnp.eye(columns, dtype=F32), axis=1, keepdims=True)
    halves = hop[:, :at_back].reshape(rows // 2, columns, width)
    token_grad = (jnp.sum(halves.astype(F32), axis=0) / own_counts).astype(BF)
    token_back = hop[:, at_back:at_weight].reshape(columns, width)
    weight_col = jnp.sum(hop[:, at_weight:at_counts].astype(F32), axis=0)
    table = jnp.where(core == 0, token_grad, token_back)
    hop = spread(
        jnp.concatenate([table] + high_low(weight_col[:heads] + weight_col[heads:]), axis=0), COL
    )
    table = hop[:, :columns].reshape(total_tokens, width)
    weight = jnp.sum(hop[:, columns:].astype(F32), axis=0)
    of_row, rest = ids // tok_rows, ids % tok_rows
    back_ids = (rest // tile) * columns + of_row * tile + rest % tile
    picks = jnp.where(core == 0, ids, back_ids)
    slots = jnp.arange(total_tokens, dtype=jnp.int32)[None, :]
    picked = nn((picks[:, None] == slots).astype(BF), table).astype(BF)
    mine, other = picked[:n_atoms], lax.ppermute(picked[n_atoms:], "k", SWAP)
    grad_atom = atom_cot.astype(F32) + jnp.where(core == 0, mine, other).astype(F32)
    atom_out = (
        atom_single.astype(F32) + jnp.where(core == 0, other, mine).astype(F32)
    ).astype(BF)
    grad_bias = jnp.transpose(weight[:heads] + weight[heads:])
    return (atom_out, grad_atom, grad_bias)


def solution(mesh):
    rows, cols = mesh.devices.shape
    side = math.isqrt(cols)
    devices = mesh.devices.reshape(rows // 2, 2, side, side)
    everyone = ROW + COL
    return jax.shard_map(
        on_device,
        mesh=Mesh(devices, everyone),
        in_specs=(
            P(everyone, None),
            P(everyone),
            P(everyone, None),
            P(ROW, None),
            P(ROW, COL, None),
            P(),
            P(None, None, COL),
            P(),
            P(COL, None),
            P(),
        ),
        out_specs=(P(everyone, None), P(everyone, None), P()),
        check_vma=False,
    )
```

time: 180 us -> 155 us (0.86)
  starting transfers between devices: 28.9 us -> 60.2 us
  waiting for transfers between devices: 74 us -> 44.6 us
  blocking collectives: 13.7 us -> 0 us
  between operations: 14.4 us -> 1.03 us
  Pallas kernels: 16.6 us -> 21.5 us
  other arithmetic: 4.34 us -> 8.39 us
  local copies, waits for them, and re-layouts: 10.1 us -> 6.23 us
  matrix products: 15.4 us -> 12 us
    all_to_all x5 -> x7, waiting for transfers between devices: 73.3 us -> 36.5 us  [exchange(): return lax.all_to_all(blocks, axis, split_axis=0, concat_axis=0, tiled=True)]
    ppermute x0 -> x12, starting transfers between devices: none -> 19 us  [the longest x4 6.96 us: on_device(): conds += [piece, lax.ppermute(piece, 'k', SWAP)]]
    all_to_all x1 -> x0, blocking collectives: 13.7 us -> none  [exchange(): return lax.all_to_all(blocks, axis, split_axis=0, concat_axis=0, tiled=True)]
    all_to_all x5 -> x7, starting transfers between devices: 28.9 us -> 41.1 us  [exchange(): return lax.all_to_all(blocks, axis, split_axis=0, concat_axis=0, tiled=True)]
    ppermute x0 -> x12, waiting for transfers between devices: none -> 8.09 us  [the longest x3 6.64 us: turn(): return lax.ppermute(value, axis, [(i, i ^ by) for i in range(size)])]
    pallas_call x2 -> x3, Pallas kernels: 16.6 us -> 21.5 us  [call(): pl.pallas_call(kernel, in_specs=specs, out_specs=[anywhere] * n_out, out_...]
    unnamed x28 -> x26, local copies, waits for them, and re-layouts: 7.31 us -> 2.55 us
    dot_general x4 -> x3, matrix products: 4.31 us -> 1.23 us  [nn(): return jnp.dot(left, right, preferred_element_type=F32)]
  transfers between devices with their start and end apart: 6 -> 19, of which waited for: 5 -> 11; matrix products, arithmetic and copies ran while one was open for 7% -> 14% of each run, Pallas kernels for 4% -> 11%
where the time goes in v3:
time: 155 us; the launch traced here: 154 us
  starting transfers between devices  60.2 us (39%)
  waiting for transfers between devices  44.6 us (29%)
  Pallas kernels  21.5 us (14%)
  matrix products  12 us (8%)
  other arithmetic  8.39 us (5%)
  local copies, waits for them, and re-layouts  6.23 us (4%)
    all_to_all x7, starting transfers between devices, exchange(): return lax.all_to_all(blocks, axis, split_axis=0, concat_axis=0, tiled=True)  41.1 us
    all_to_all x7, waiting for transfers between devices, exchange(): return lax.all_to_all(blocks, axis, split_axis=0, concat_axis=0, tiled=True)  36.5 us
    pallas_call x3, Pallas kernels, call(): pl.pallas_call(kernel, in_specs=specs, out_specs=[anywhere] * n_out, out_...  21.5 us
    ppermute x4, starting transfers between devices, on_device(): conds += [piece, lax.ppermute(piece, 'k', SWAP)]  6.96 us
    ppermute x3, waiting for transfers between devices, turn(): return lax.ppermute(value, axis, [(i, i ^ by) for i in range(size)])  6.64 us
    dot_general x1, matrix products, on_device(): jnp.einsum('ijc,ch->hij', pair, w_bias, preferred_element_type=F32)  5.66 us
    dot_general x1, matrix products, on_device(): jnp.einsum('ijc,hij->hc', pair, bias_back, preferred_element_type=F32)  5.12 us
    ppermute x3, starting transfers between devices, turn(): return lax.ppermute(value, axis, [(i, i ^ by) for i in range(size)])  5.03 us
  transfers between devices with their start and end apart: 19, of which 11 were waited for; matrix products, arithmetic and copies ran while one was open for 14% of the time, Pallas kernels for 11%

profile of v3, /device:TPU:1, one launch (start us, length us, event | category | flops | bytes accessed | tf_op | source)
XLA Modules:
  0.0 153.9 jit_solution(14528047707592711744)
XLA Ops:
  6.9 1.7 %collective-permute-start.3 = (bf16[256,768]{1,0:T(8,128)(2,1)S(1)}, bf16[256,768]{1,0:T(8,128)(2,1)}, u32[]{:S(2)}, u32[]{:S(2)}) collective-permute-start(bf16[256,768]{1,0:T(8,128)(2,1)S(1)} %copy-done.5), channel_id=1, source_target_pairs={{0,32},{32,0},{64,96},{96,64},{1,33},{33,1},{65,97},{97,65},{2,34}... | collective-permute-start | bytes 1179656 | tf_op jit(solution)/shard_map/ppermute | solution.py:218
  8.6 3.3 %collective-permute-start.5 = (bf16[256,768]{1,0:T(8,128)(2,1)S(1)}, bf16[256,768]{1,0:T(8,128)(2,1)}, u32[]{:S(2)}, u32[]{:S(2)}) collective-permute-start(bf16[256,768]{1,0:T(8,128)(2,1)S(1)} %copy-done.5), channel_id=1, source_target_pairs={{0,64},{32,96},{64,0},{96,32},{1,65},{33,97},{65,1},{97,33},{2,66}... | collective-permute-start | bytes 1179656 | tf_op jit(solution)/shard_map/ppermute | solution.py:218
  11.9 10.1 %all-to-all-start = ((bf16[64,40,128]{2,1,0:T(8,128)(2,1)}), bf16[64,40,128]{2,1,0:T(8,128)(2,1)S(1)}, u32[]{:S(2)}, u32[]{:S(2)}) async-start(bf16[64,40,128]{2,1,0:T(8,128)(2,1)} %fusion.9), calls=%async_computation | async-start | bytes 1310720 | tf_op jit(solution)/shard_map/all_to_all | solution.py:32
  22.0 5.7 %fusion.43 = bf16[16,256,128]{2,0,1:T(8,128)(2,1)S(1)} fusion(bf16[256,128,128]{2,1,0:T(8,128)(2,1)} %param.14, bf16[128,16]{0,1:T(8,128)(2,1)S(1)} %copy-done), kind=kOutput, calls=%fused_computation.91 | convolution fusion | flops 134217728 | bytes 9441280 | tf_op jit(solution)/shard_map/ijc,ch->hij/dot_general | solution.py:259
  29.5 5.6 %collective-permute-done.5.refs_5_ = bf16[256,768]{1,0:T(8,128)(2,1)} collective-permute-done((bf16[256,768]{1,0:T(8,128)(2,1)S(1)}, bf16[256,768]{1,0:T(8,128)(2,1)}, u32[]{:S(2)}, u32[]{:S(2)}) %collective-permute-start.5) | collective-permute-done | bytes 393248 | tf_op jit(solution)/shard_map/ppermute | solution.py:218
  35.1 2.1 %collective-permute-start.6 = (bf16[256,768]{1,0:T(8,128)(2,1)}, bf16[256,768]{1,0:T(8,128)(2,1)S(1)}, u32[]{:S(2)}, u32[]{:S(2)}) collective-permute-start(bf16[256,768]{1,0:T(8,128)(2,1)} %collective-permute-done.5.refs_5_), channel_id=1, source_target_pairs={{0,16},{16,0},{1,17},{17,1},{2,18},{18,2},{3,19},{19,3},{4,20},{20... | collective-permute-start | bytes 1179656 | tf_op jit(solution)/shard_map/ppermute | solution.py:277
  38.2 1.9 %collective-permute-start.8 = (bf16[256,768]{1,0:T(8,128)(2,1)}, bf16[256,768]{1,0:T(8,128)(2,1)}, u32[]{:S(2)}, u32[]{:S(2)}) collective-permute-start(bf16[256,768]{1,0:T(8,128)(2,1)} %collective-permute-done.7.refs_7_), channel_id=1, source_target_pairs={{0,16},{16,0},{1,17},{17,1},{2,18},{18,2},{3,19},{19,3},{4,20},{20... | collective-permute-start | bytes 1179656 | tf_op jit(solution)/shard_map/ppermute | solution.py:277
  41.2 7.7 %all-to-all-start.1 = ((bf16[64,16,128]{2,1,0:T(8,128)(2,1)}), bf16[64,16,128]{2,1,0:T(8,128)(2,1)S(1)}, u32[]{:S(2)}, u32[]{:S(2)}) async-start(bf16[64,16,128]{2,1,0:T(8,128)(2,1)} %broadcast_in_dim.39), calls=%async_computation.1 | async-start | bytes 524288 | tf_op jit(solution)/shard_map/all_to_all | solution.py:32
  50.2 8.8 %all-to-all-done.1 = bf16[64,16,128]{2,1,0:T(8,128)(2,1)S(1)} async-done(((bf16[64,16,128]{2,1,0:T(8,128)(2,1)}), bf16[64,16,128]{2,1,0:T(8,128)(2,1)S(1)}, u32[]{:S(2)}, u32[]{:S(2)}) %all-to-all-start.1) | async-done | bytes 262176 | tf_op jit(solution)/shard_map/all_to_all | solution.py:32
  59.0 3.7 %all-to-all-start.2 = ((bf16[16,288,128]{2,1,0:T(8,128)(2,1)}), bf16[16,288,128]{2,1,0:T(8,128)(2,1)S(1)}, u32[]{:S(2)}, u32[]{:S(2)}) async-start(bf16[16,288,128]{2,1,0:T(8,128)(2,1)} %pad_maximum_fusion), calls=%async_computation.2 | async-start | bytes 2359296 | tf_op jit(solution)/shard_map/all_to_all | solution.py:32
  65.7 8.0 %shard_map.121 = (bf16[16,128,768]{2,1,0:T(8,128)(2,1)}, f32[16,128,1]{2,1,0:T(8,128)}, bf16[16,96,128]{2,1,0:T(8,128)(2,1)}, bf16[256,48]{1,0:T(8,128)(2,1)}, bf16[48,256]{1,0:T(8,128)(2,1)}) custom-call(s32[4]{0:T(128)} %pad_add_fusion.refs_0_, bf16[256,768]{1,0:T(8,128)(2,1)} %refs_1_.1, bf16[256,768]{1,0:T(8,128)(2,1)} %copy-done.6, ...), custom_call_target="tpu_custom_call" | custom-call | flops 1000000000 | bytes 8388608 | tf_op jit(solution)/shard_map/pallas_call | solution.py:196
  73.7 5.9 %all-to-all-done.2.refs_3_ = bf16[16,288,128]{2,1,0:T(8,128)(2,1)S(1)} async-done(((bf16[16,288,128]{2,1,0:T(8,128)(2,1)}), bf16[16,288,128]{2,1,0:T(8,128)(2,1)S(1)}, u32[]{:S(2)}, u32[]{:S(2)}) %all-to-all-start.2) | async-done | bytes 1179680 | tf_op jit(solution)/shard_map/all_to_all | solution.py:32
  80.6 4.8 %shard_map.122 = (bf16[16,256,128]{2,1,0:T(8,128)(2,1)}, bf16[96,2048]{1,0:T(8,128)(2,1)}, bf16[256,48]{1,0:T(8,128)(2,1)}, bf16[256,48]{1,0:T(8,128)(2,1)}, f32[256,768]{1,0:T(8,128)}) custom-call(bf16[256,48]{1,0:T(8,128)(2,1)} %get-tuple-element.27.refs_0_, bf16[48,256]{1,0:T(8,128)(2,1)} %get-tuple-element.28.refs_1_, ...), custom_call_target="tpu_custom_call" | custom-call | flops 2000000000 | bytes 8388608 | tf_op jit(solution)/shard_map/pallas_call | solution.py:196
  85.4 4.4 %all-to-all-start.3 = ((bf16[16,256,128]{2,1,0:T(8,128)(2,1)}), bf16[16,256,128]{2,1,0:T(8,128)(2,1)S(1)}, u32[]{:S(2)}, u32[]{:S(2)}) async-start(bf16[16,256,128]{2,1,0:T(8,128)(2,1)} %get-tuple-element.41), calls=%async_computation.3 | async-start | bytes 2097152 | tf_op jit(solution)/shard_map/all_to_all | solution.py:32
  89.8 8.7 %shard_map.123 = (f32[16,64,128]{2,1,0:T(8,128)}, bf16[16,64,128]{2,1,0:T(8,128)(2,1)}, bf16[16,16,128]{2,1,0:T(8,128)(2,1)}) custom-call(s32[4]{0:T(128)} %pad_add_fusion.refs_0_, bf16[96,2048]{1,0:T(8,128)(2,1)} %get-tuple-element.32.refs_1_, bf16[256,48]{1,0:T(8,128)(2,1)} %get-tuple-element.33.refs_2_, bf16[256,48]{1,0:T(8,128)(2,1)} %get-tuple-element.34.refs_3_, ...), custom_call_target="tpu_custom_call" | custom-call | flops 1000000000 | bytes 8388608 | tf_op jit(solution)/shard_map/pallas_call | solution.py:196
  98.5 2.5 %collective-permute-start.10 = (bf16[16,64,128]{2,1,0:T(8,128)(2,1)}, bf16[16,64,128]{2,1,0:T(8,128)(2,1)S(1)}, u32[]{:S(2)}, u32[]{:S(2)}) collective-permute-start(bf16[16,64,128]{2,1,0:T(8,128)(2,1)} %get-tuple-element.39), channel_id=1, source_target_pairs={{0,16},{16,0},{1,17},{17,1},{2,18},{18,2},{3,19},{19,3},{4,20},{20... | collective-permute-start | bytes 786440 | tf_op jit(solution)/shard_map/ppermute | solution.py:325
  105.1 6.9 %all-to-all-start.4 = ((bf16[16,80,128]{2,1,0:T(8,128)(2,1)}), bf16[16,80,128]{2,1,0:T(8,128)(2,1)S(1)}, u32[]{:S(2)}, u32[]{:S(2)}) async-start(bf16[16,80,128]{2,1,0:T(8,128)(2,1)} %pad_maximum_fusion.1), calls=%async_computation.4 | async-start | bytes 655360 | tf_op jit(solution)/shard_map/all_to_all | solution.py:32
  112.0 5.1 %convolution_bitcast_fusion = f32[16,128]{1,0:T(8,128)S(1)} fusion(bf16[256,128,128]{2,1,0:T(8,128)(2,1)} %param.14, bf16[16,256,128]{2,1,0:T(8,128)(2,1)S(1)} %all-to-all-done.3), kind=kOutput, calls=%fused_computation.11 | convolution fusion | flops 134217728 | bytes 9445376 | tf_op jit(solution)/shard_map/ijc,hij->hc/dot_general | solution.py:329
  117.1 3.7 %all-to-all-done.4 = bf16[16,80,128]{2,1,0:T(8,128)(2,1)S(1)} async-done(((bf16[16,80,128]{2,1,0:T(8,128)(2,1)}), bf16[16,80,128]{2,1,0:T(8,128)(2,1)S(1)}, u32[]{:S(2)}, u32[]{:S(2)}) %all-to-all-start.4) | async-done | bytes 327712 | tf_op jit(solution)/shard_map/all_to_all | solution.py:32
  121.6 4.8 %all-to-all-start.5 = ((bf16[8,128,128]{2,1,0:T(8,128)(2,1)}), bf16[8,128,128]{2,1,0:T(8,128)(2,1)S(1)}, u32[]{:S(2)}, u32[]{:S(2)}) async-start(bf16[8,128,128]{2,1,0:T(8,128)(2,1)} %broadcast_in_dim.46), calls=%async_computation.5 | async-start | bytes 524288 | tf_op jit(solution)/shard_map/all_to_all | solution.py:32
  126.5 6.5 %all-to-all-done.5 = bf16[8,128,128]{2,1,0:T(8,128)(2,1)S(1)} async-done(((bf16[8,128,128]{2,1,0:T(8,128)(2,1)}), bf16[8,128,128]{2,1,0:T(8,128)(2,1)S(1)}, u32[]{:S(2)}, u32[]{:S(2)}) %all-to-all-start.5) | async-done | bytes 262176 | tf_op jit(solution)/shard_map/all_to_all | solution.py:32
  134.3 3.6 %all-to-all-start.6 = ((bf16[16,160,128]{2,1,0:T(8,128)(2,1)}), bf16[16,160,128]{2,1,0:T(8,128)(2,1)S(1)}, u32[]{:S(2)}, u32[]{:S(2)}) async-start(bf16[16,160,128]{2,1,0:T(8,128)(2,1)} %broadcast_in_dim.47), calls=%async_computation.6 | async-start | bytes 1310720 | tf_op jit(solution)/shard_map/all_to_all | solution.py:32
  137.9 11.6 %all-to-all-done.6 = bf16[16,160,128]{2,1,0:T(8,128)(2,1)S(1)} async-done(((bf16[16,160,128]{2,1,0:T(8,128)(2,1)}), bf16[16,160,128]{2,1,0:T(8,128)(2,1)S(1)}, u32[]{:S(2)}, u32[]{:S(2)}) %all-to-all-start.6) | async-done | bytes 655392 | tf_op jit(solution)/shard_map/all_to_all | solution.py:32
  150.1 2.3 %collective-permute-start.11 = (bf16[128,128]{1,0:T(8,128)(2,1)S(1)}, bf16[128,128]{1,0:T(8,128)(2,1)S(1)}, u32[]{:S(2)}, u32[]{:S(2)}) collective-permute-start(bf16[128,128]{1,0:T(8,128)(2,1)S(1)} %slice.108), channel_id=1, source_target_pairs={{0,16},{16,0},{1,17},{17,1},{2,18},{18,2},{3,19},{19,3},{4,20},{20... | collective-permute-start | bytes 98312 | tf_op jit(solution)/shard_map/ppermute | solution.py:362
  (97 shorter events, 23.6 us)
Async XLA Ops:
  0.6 21.4 %copy-start = (bf16[128,16]{0,1:T(8,128)(2,1)S(1)}, bf16[128,16]{0,1:T(8,128)(2,1)}, u32[]{:S(2)}) copy-start(bf16[128,16]{0,1:T(8,128)(2,1)} %param.17) | copy-start | bytes 12292
  0.6 49.5 %collective-permute-start.1 = (bf16[256,768]{1,0:T(8,128)(2,1)}, bf16[256,768]{1,0:T(8,128)(2,1)S(1)}, u32[]{:S(2)}, u32[]{:S(2)}) collective-permute-start(bf16[256,768]{1,0:T(8,128)(2,1)} %refs_1_.1), channel_id=1, source_target_pairs={{0,16},{16,0},{1,17},{17,1},{2,18},{18,2},{3,19},{19,3},{4,20},{20... | collective-permute-start | bytes 1179656 | tf_op jit(solution)/shard_map/ppermute | solution.py:277
  3.7 1.6 %collective-permute-start.2 = (bf16[128,256]{1,0:T(8,128)(2,1)S(1)}, bf16[128,256]{1,0:T(8,128)(2,1)S(1)}, u32[]{:S(2)}, u32[]{:S(2)}) collective-permute-start(bf16[128,256]{1,0:T(8,128)(2,1)S(1)} %constant_dynamic-update-slice_fusion.1), channel_id=1, source_target_pairs={{0,16},{16,0},{1,17},{17,1},{2,18},{18,2},{3,19},{19,3},{4,20},{20... | collective-permute-start | bytes 196616 | tf_op jit(solution)/shard_map/ppermute | solution.py:241
  3.8 1.4 collective-permute-start
  6.9 21.1 %collective-permute-start.3 = (bf16[256,768]{1,0:T(8,128)(2,1)S(1)}, bf16[256,768]{1,0:T(8,128)(2,1)}, u32[]{:S(2)}, u32[]{:S(2)}) collective-permute-start(bf16[256,768]{1,0:T(8,128)(2,1)S(1)} %copy-done.5), channel_id=1, source_target_pairs={{0,32},{32,0},{64,96},{96,64},{1,33},{33,1},{65,97},{97,65},{2,34}... | collective-permute-start | bytes 1179656 | tf_op jit(solution)/shard_map/ppermute | solution.py:218
  8.6 26.5 %collective-permute-start.5 = (bf16[256,768]{1,0:T(8,128)(2,1)S(1)}, bf16[256,768]{1,0:T(8,128)(2,1)}, u32[]{:S(2)}, u32[]{:S(2)}) collective-permute-start(bf16[256,768]{1,0:T(8,128)(2,1)S(1)} %copy-done.5), channel_id=1, source_target_pairs={{0,64},{32,96},{64,0},{96,32},{1,65},{33,97},{65,1},{97,33},{2,66}... | collective-permute-start | bytes 1179656 | tf_op jit(solution)/shard_map/ppermute | solution.py:218
  11.9 26.3 %collective-permute-start.7 = (bf16[256,768]{1,0:T(8,128)(2,1)S(1)}, bf16[256,768]{1,0:T(8,128)(2,1)}, u32[]{:S(2)}, u32[]{:S(2)}) collective-permute-start(bf16[256,768]{1,0:T(8,128)(2,1)S(1)} %copy-done.5), channel_id=1, source_target_pairs={{0,96},{32,64},{64,32},{96,0},{1,97},{33,65},{65,33},{97,1},{2,98}... | collective-permute-start | bytes 1179656 | tf_op jit(solution)/shard_map/ppermute | solution.py:218
  11.9 28.2 %all-to-all-start = ((bf16[64,40,128]{2,1,0:T(8,128)(2,1)}), bf16[64,40,128]{2,1,0:T(8,128)(2,1)S(1)}, u32[]{:S(2)}, u32[]{:S(2)}) async-start(bf16[64,40,128]{2,1,0:T(8,128)(2,1)} %fusion.9), calls=%async_computation | async-start | bytes 1310720 | tf_op jit(solution)/shard_map/all_to_all | solution.py:32
  28.0 22.1 %collective-permute-start.4 = (bf16[256,768]{1,0:T(8,128)(2,1)}, bf16[256,768]{1,0:T(8,128)(2,1)S(1)}, u32[]{:S(2)}, u32[]{:S(2)}) collective-permute-start(bf16[256,768]{1,0:T(8,128)(2,1)} %collective-permute-done.3.refs_3_), channel_id=1, source_target_pairs={{0,16},{16,0},{1,17},{17,1},{2,18},{18,2},{3,19},{19,3},{4,20},{20... | collective-permute-start | bytes 1179656 | tf_op jit(solution)/shard_map/ppermute | solution.py:277
  35.1 15.0 %collective-permute-start.6 = (bf16[256,768]{1,0:T(8,128)(2,1)}, bf16[256,768]{1,0:T(8,128)(2,1)S(1)}, u32[]{:S(2)}, u32[]{:S(2)}) collective-permute-start(bf16[256,768]{1,0:T(8,128)(2,1)} %collective-permute-done.5.refs_5_), channel_id=1, source_target_pairs={{0,16},{16,0},{1,17},{17,1},{2,18},{18,2},{3,19},{19,3},{4,20},{20... | collective-permute-start | bytes 1179656 | tf_op jit(solution)/shard_map/ppermute | solution.py:277
  38.2 11.9 %collective-permute-start.8 = (bf16[256,768]{1,0:T(8,128)(2,1)}, bf16[256,768]{1,0:T(8,128)(2,1)}, u32[]{:S(2)}, u32[]{:S(2)}) collective-permute-start(bf16[256,768]{1,0:T(8,128)(2,1)} %collective-permute-done.7.refs_7_), channel_id=1, source_target_pairs={{0,16},{16,0},{1,17},{17,1},{2,18},{18,2},{3,19},{19,3},{4,20},{20... | collective-permute-start | bytes 1179656 | tf_op jit(solution)/shard_map/ppermute | solution.py:277
  41.2 17.8 %all-to-all-start.1 = ((bf16[64,16,128]{2,1,0:T(8,128)(2,1)}), bf16[64,16,128]{2,1,0:T(8,128)(2,1)S(1)}, u32[]{:S(2)}, u32[]{:S(2)}) async-start(bf16[64,16,128]{2,1,0:T(8,128)(2,1)} %broadcast_in_dim.39), calls=%async_computation.1 | async-start | bytes 524288 | tf_op jit(solution)/shard_map/all_to_all | solution.py:32
  50.1 15.6 %copy-start.6 = (bf16[256,768]{1,0:T(8,128)(2,1)}, bf16[256,768]{1,0:T(8,128)(2,1)S(1)}, u32[]{:S(2)}) copy-start(bf16[256,768]{1,0:T(8,128)(2,1)S(1)} %collective-permute-done.1.refs_2_) | copy-start | bytes 1179652
  50.1 15.6 %copy-start.7 = (bf16[256,768]{1,0:T(8,128)(2,1)}, bf16[256,768]{1,0:T(8,128)(2,1)S(1)}, u32[]{:S(2)}) copy-start(bf16[256,768]{1,0:T(8,128)(2,1)S(1)} %collective-permute-done.4.refs_4_) | copy-start | bytes 1179652
  50.1 15.6 %copy-start.8 = (bf16[256,768]{1,0:T(8,128)(2,1)}, bf16[256,768]{1,0:T(8,128)(2,1)S(1)}, u32[]{:S(2)}) copy-start(bf16[256,768]{1,0:T(8,128)(2,1)S(1)} %collective-permute-done.6.refs_6_) | copy-start | bytes 1179652
  59.0 20.6 %all-to-all-start.2 = ((bf16[16,288,128]{2,1,0:T(8,128)(2,1)}), bf16[16,288,128]{2,1,0:T(8,128)(2,1)S(1)}, u32[]{:S(2)}, u32[]{:S(2)}) async-start(bf16[16,288,128]{2,1,0:T(8,128)(2,1)} %pad_maximum_fusion), calls=%async_computation.2 | async-start | bytes 2359296 | tf_op jit(solution)/shard_map/all_to_all | solution.py:32
  62.7 3.0 %collective-permute-start.9 = (bf16[4,256,128]{2,1,0:T(8,128)(2,1)S(1)}, bf16[4,256,128]{2,1,0:T(8,128)(2,1)}, u32[]{:S(2)}, u32[]{:S(2)}) collective-permute-start(bf16[4,256,128]{2,1,0:T(8,128)(2,1)S(1)} %bitcast.36), channel_id=1, source_target_pairs={{0,16},{16,0},{1,17},{17,1},{2,18},{18,2},{3,19},{19,3},{4,20},{20... | collective-permute-start | bytes 786440 | tf_op jit(solution)/shard_map/ppermute | solution.py:280
  85.4 19.7 %all-to-all-start.3 = ((bf16[16,256,128]{2,1,0:T(8,128)(2,1)}), bf16[16,256,128]{2,1,0:T(8,128)(2,1)S(1)}, u32[]{:S(2)}, u32[]{:S(2)}) async-start(bf16[16,256,128]{2,1,0:T(8,128)(2,1)} %get-tuple-element.41), calls=%async_computation.3 | async-start | bytes 2097152 | tf_op jit(solution)/shard_map/all_to_all | solution.py:32
  98.5 3.9 %collective-permute-start.10 = (bf16[16,64,128]{2,1,0:T(8,128)(2,1)}, bf16[16,64,128]{2,1,0:T(8,128)(2,1)S(1)}, u32[]{:S(2)}, u32[]{:S(2)}) collective-permute-start(bf16[16,64,128]{2,1,0:T(8,128)(2,1)} %get-tuple-element.39), channel_id=1, source_target_pairs={{0,16},{16,0},{1,17},{17,1},{2,18},{18,2},{3,19},{19,3},{4,20},{20... | collective-permute-start | bytes 786440 | tf_op jit(solution)/shard_map/ppermute | solution.py:325
  105.1 15.7 %all-to-all-start.4 = ((bf16[16,80,128]{2,1,0:T(8,128)(2,1)}), bf16[16,80,128]{2,1,0:T(8,128)(2,1)S(1)}, u32[]{:S(2)}, u32[]{:S(2)}) async-start(bf16[16,80,128]{2,1,0:T(8,128)(2,1)} %pad_maximum_fusion.1), calls=%async_computation.4 | async-start | bytes 655360 | tf_op jit(solution)/shard_map/all_to_all | solution.py:32
  121.6 11.4 %all-to-all-start.5 = ((bf16[8,128,128]{2,1,0:T(8,128)(2,1)}), bf16[8,128,128]{2,1,0:T(8,128)(2,1)S(1)}, u32[]{:S(2)}, u32[]{:S(2)}) async-start(bf16[8,128,128]{2,1,0:T(8,128)(2,1)} %broadcast_in_dim.46), calls=%async_computation.5 | async-start | bytes 524288 | tf_op jit(solution)/shard_map/all_to_all | solution.py:32
  134.3 15.2 %all-to-all-start.6 = ((bf16[16,160,128]{2,1,0:T(8,128)(2,1)}), bf16[16,160,128]{2,1,0:T(8,128)(2,1)S(1)}, u32[]{:S(2)}, u32[]{:S(2)}) async-start(bf16[16,160,128]{2,1,0:T(8,128)(2,1)} %broadcast_in_dim.47), calls=%async_computation.6 | async-start | bytes 1310720 | tf_op jit(solution)/shard_map/all_to_all | solution.py:32
  137.9 15.4 %copy-start.9 = (bf16[128,128]{1,0:T(8,128)(2,1)S(1)}, bf16[128,128]{1,0:T(8,128)(2,1)}, u32[]{:S(2)}) copy-start(bf16[128,128]{1,0:T(8,128)(2,1)} %param.12) | copy-start | bytes 98308
  150.1 3.2 %collective-permute-start.11 = (bf16[128,128]{1,0:T(8,128)(2,1)S(1)}, bf16[128,128]{1,0:T(8,128)(2,1)S(1)}, u32[]{:S(2)}, u32[]{:S(2)}) collective-permute-start(bf16[128,128]{1,0:T(8,128)(2,1)S(1)} %slice.108), channel_id=1, source_target_pairs={{0,16},{16,0},{1,17},{17,1},{2,18},{18,2},{3,19},{19,3},{4,20},{20... | collective-permute-start | bytes 98312 | tf_op jit(solution)/shard_map/ppermute | solution.py:362
  (6 other events, 54.2 us)

commit v4 on v3

--- a/solution.py
+++ b/solution.py
@@ -237,13 +237,13 @@
     at = jnp.stack([row, col, z, core]).astype(jnp.int32)
     w_t = jnp.transpose(w_qkv, (0, 2, 1)).reshape(3 * HD, -1)
 
-    own_atoms = jnp.concatenate([atom_single, atom_cot], axis=1)
-    atoms = jnp.concatenate([own_atoms, lax.ppermute(own_atoms, "k", SWAP)], axis=0)
     ids = jnp.concatenate([atom_token, lax.ppermute(atom_token, "k", SWAP)])
+    singles = jnp.concatenate([atom_single, lax.ppermute(atom_single, "k", SWAP)], axis=0)
+    cots = jnp.concatenate([atom_cot, lax.ppermute(atom_cot, "k", SWAP)], axis=0)
     slots = jnp.arange(total_tokens // 2, dtype=jnp.int32)
     slots = (slots // tok_rows * 2 + core) * tok_rows + slots % tok_rows
     onehot = (slots[:, None] == ids[None, :]).astype(BF)
-    with_ones = jnp.concatenate([atoms, jnp.ones((2 * n_atoms, width), BF)], axis=1)
+    with_ones = jnp.concatenate([singles, cots, jnp.ones_like(singles)], axis=1)
     partial = nn(onehot, with_ones).reshape(peers, tile, 3 * width)
     place = jnp.eye(tile, width, dtype=F32)
     partial_counts = jnp.sum(partial[:, :, 2 * width :] * place, axis=1, keepdims=True)
@@ -258,8 +258,6 @@
 
     bias = jnp.einsum("ijc,ch->hij", pair, w_bias, preferred_element_type=F32).astype(BF)
     from_all = exchange(to_tiles, SAME_CORE)
-    late_cond = after(token_cond, to_tiles)
-    cond = [token_cond] + [turn(late_cond, "z", d) for d in (1, 2, 3)]
     from_all = after(from_all, bias)
     sums = jnp.sum(from_all.astype(F32), axis=0)
     tile_counts = jnp.sum(sums[2 * tile : 2 * tile + 1] * place, axis=1, keepdims=True)
@@ -272,11 +270,15 @@
     shared = jnp.concatenate([sums[tile : 2 * tile], count_row], axis=0).astype(BF)
     shared = jnp.broadcast_to(shared[None], (cols, 2 * tile, width))
     pooled = spread(pooled_tile, SAME_CORE)
+    late_cond = after(token_cond, bias)
+    pieces = [turn(late_cond, "z", d) for d in (1, 2, 3)]
+    pooled = pooled.reshape(rows // 2, tok_rows, width)
+    to_col = after(jnp.concatenate([bias, shared], axis=1), pooled, *pieces)
+    bias_cot = exchange(to_col, COL)
     conds = []
-    for piece in cond:
+    for piece in [token_cond] + pieces:
+        piece = after(piece, to_col)
         conds += [piece, lax.ppermute(piece, "k", SWAP)]
-    pooled = after(pooled, *conds).reshape(rows // 2, tok_rows, width)
-    bias_cot = exchange(after(jnp.concatenate([bias, shared], axis=1), pooled), COL)
     other_pooled = lax.ppermute(pooled, "k", SWAP)
     single_tile = take(token_cond, col * tile, tile).astype(F32) + nn(pooled_tile, w_pool)
     tile_base = nn(single_tile.astype(BF), w_dec)
@@ -328,6 +330,7 @@
     hop = exchange(after(to_col, bias_back), COL)
     weight_part = jnp.einsum("ijc,hij->hc", pair, bias_back, preferred_element_type=F32)
     hop = after(hop, weight_part)
+    block_counts = block_counts + lax.ppermute(block_counts, "k", SWAP)
     rest = jnp.sum(hop.astype(F32), axis=0)
     heads = weight_part.shape[0]
     hop = spread(
@@ -337,34 +340,45 @@
             + [jnp.pad(block_counts, ((0, 15), (0, 0)))],
             axis=0,
         ),
-        ROW,
+        "z",
     )
     at_back = columns // 2
     at_weight = at_back + tile
     at_counts = at_weight + 2 * heads
     count_row = jnp.sum(hop[:, at_counts : at_counts + 1].astype(F32), axis=0)
-    own_counts = jnp.sum(count_row * jnp.eye(columns, dtype=F32), axis=1, keepdims=True)
-    halves = hop[:, :at_back].reshape(rows // 2, columns, width)
-    token_grad = (jnp.sum(halves.astype(F32), axis=0) / own_counts).astype(BF)
-    token_back = hop[:, at_back:at_weight].reshape(columns, width)
+    seats = core * at_back + jnp.arange(at_back, dtype=jnp.int32)[:, None]
+    own_counts = jnp.sum(jnp.where(lanes == seats, count_row, 0.0), axis=1, keepdims=True)
+    token_grad = (jnp.sum(hop[:, :at_back].astype(F32), axis=0) / own_counts).astype(BF)
+    token_back = hop[:, at_back:at_weight].reshape(at_back, width)
     weight_col = jnp.sum(hop[:, at_weight:at_counts].astype(F32), axis=0)
-    table = jnp.where(core == 0, token_grad, token_back)
     hop = spread(
-        jnp.concatenate([table] + high_low(weight_col[:heads] + weight_col[heads:]), axis=0), COL
-    )
-    table = hop[:, :columns].reshape(total_tokens, width)
+        jnp.concatenate(
+            [token_grad, token_back] + high_low(weight_col[:heads] + weight_col[heads:]), axis=0
+        ),
+        COL,
+    )
     weight = jnp.sum(hop[:, columns:].astype(F32), axis=0)
+    weight = weight[:heads] + weight[heads:]
+    grad_table = hop[:, :at_back].reshape(cols * at_back, width)
+    back_table = hop[:, at_back:columns].reshape(cols * at_back, width)
+    slots = jnp.arange(cols * at_back, dtype=jnp.int32)[None, :]
     of_row, rest = ids // tok_rows, ids % tok_rows
-    back_ids = (rest // tile) * columns + of_row * tile + rest % tile
-    picks = jnp.where(core == 0, ids, back_ids)
-    slots = jnp.arange(total_tokens, dtype=jnp.int32)[None, :]
-    picked = nn((picks[:, None] == slots).astype(BF), table).astype(BF)
-    mine, other = picked[:n_atoms], lax.ppermute(picked[n_atoms:], "k", SWAP)
-    grad_atom = atom_cot.astype(F32) + jnp.where(core == 0, mine, other).astype(F32)
-    atom_out = (
-        atom_single.astype(F32) + jnp.where(core == 0, other, mine).astype(F32)
-    ).astype(BF)
-    grad_bias = jnp.transpose(weight[:heads] + weight[heads:])
+    grad_ids = ids // columns * at_back + ids % at_back
+    grad_ids = jnp.where(ids % columns // at_back == core, grad_ids, -1)
+    back_ids = rest // tile * at_back + of_row // 2 * tile + rest % tile
+    back_ids = jnp.where(of_row % 2 == core, back_ids, -1)
+    picked = jnp.concatenate(
+        [
+            nn((back_ids[:, None] == slots).astype(BF), back_table).astype(BF),
+            nn((grad_ids[:, None] == slots).astype(BF), grad_table).astype(BF),
+        ],
+        axis=1,
+    )
+    other = lax.ppermute(picked[n_atoms:], "k", SWAP)
+    picked = picked[:n_atoms].astype(F32) + other.astype(F32)
+    atom_out = (atom_single.astype(F32) + picked[:, :width]).astype(BF)
+    grad_atom = atom_cot.astype(F32) + picked[:, width:]
+    grad_bias = jnp.transpose(weight + lax.ppermute(weight, "k", SWAP))
     return (atom_out, grad_atom, grad_bias)
 
 

time: 155 us -> 147 us (0.948)
  waiting for transfers between devices: 44.6 us -> 38.4 us
  starting transfers between devices: 60.2 us -> 57.1 us
    all_to_all x7, waiting for transfers between devices: 36.5 us -> 25.1 us  [exchange(): return lax.all_to_all(blocks, axis, split_axis=0, concat_axis=0, tiled=True)]
    ppermute x4, starting transfers between devices: 6.96 us -> 3.35 us  [on_device(): conds += [piece, lax.ppermute(piece, 'k', SWAP)]]
    ppermute x3, waiting for transfers between devices: 6.64 us -> 9.62 us  [turn(): return lax.ppermute(value, axis, [(i, i ^ by) for i in range(size)])]
    unnamed x26 -> x31, local copies, waits for them, and re-layouts: 2.55 us -> 4.55 us
    ppermute x2 -> x5, waiting for transfers between devices: 0.24 us -> 2.09 us  [the longest x1 1.11 us: on_device(): block_counts = block_counts + lax.ppermute(block_counts, 'k', SWAP)]
    ppermute x2 -> x5, starting transfers between devices: 2.38 us -> 3.89 us  [the longest x1 3.19 us: on_device(): grad_bias = jnp.transpose(weight + lax.ppermute(weight, 'k', SWAP))]
  transfers between devices with their start and end apart: 19 -> 22, of which waited for: 11 -> 13; matrix products, arithmetic and copies ran while one was open for 14% -> 14% of each run, Pallas kernels for 11% -> 11%
where the time goes in v4:
time: 147 us; the launch traced here: 146 us
  starting transfers between devices  57.1 us (39%)
  waiting for transfers between devices  38.4 us (26%)
  Pallas kernels  21.4 us (15%)
  matrix products  13.1 us (9%)
  other arithmetic  7.86 us (5%)
  local copies, waits for them, and re-layouts  7.42 us (5%)
    all_to_all x7, starting transfers between devices, exchange(): return lax.all_to_all(blocks, axis, split_axis=0, concat_axis=0, tiled=True)  41.8 us
    all_to_all x7, waiting for transfers between devices, exchange(): return lax.all_to_all(blocks, axis, split_axis=0, concat_axis=0, tiled=True)  25.1 us
    pallas_call x3, Pallas kernels, call(): pl.pallas_call(kernel, in_specs=specs, out_specs=[anywhere] * n_out, out_...  21.4 us
    ppermute x3, waiting for transfers between devices, turn(): return lax.ppermute(value, axis, [(i, i ^ by) for i in range(size)])  9.62 us
    dot_general x1, matrix products, on_device(): jnp.einsum('ijc,ch->hij', pair, w_bias, preferred_element_type=F32)  5.66 us
    dot_general x1, matrix products, on_device(): jnp.einsum('ijc,hij->hc', pair, bias_back, preferred_element_type=F32)  5.12 us
    unnamed x31, local copies, waits for them, and re-layouts  4.55 us
    ppermute x3, starting transfers between devices, turn(): return lax.ppermute(value, axis, [(i, i ^ by) for i in range(size)])  3.86 us
  transfers between devices with their start and end apart: 22, of which 13 were waited for; matrix products, arithmetic and copies ran while one was open for 14% of the time, Pallas kernels for 11%

profile of v4, /device:TPU:1, one launch (start us, length us, event | category | flops | bytes accessed | tf_op | source)
XLA Modules:
  0.0 146.3 jit_solution(4097883554024161250)
XLA Ops:
  0.6 1.5 %collective-permute-start = (s32[128]{0:T(128)}, s32[128]{0:T(128)S(1)}, u32[]{:S(2)}, u32[]{:S(2)}) collective-permute-start(s32[128]{0:T(128)} %param.11), channel_id=1, source_target_pairs={{0,16},{16,0},{1,17},{17,1},{2,18},{18,2},{3,19},{19,3},{4,20},{20... | collective-permute-start | bytes 1544 | tf_op jit(solution)/shard_map/ppermute | solution.py:240
  6.1 11.2 %all-to-all-start = ((bf16[64,40,128]{2,1,0:T(8,128)(2,1)}), bf16[64,40,128]{2,1,0:T(8,128)(2,1)S(1)}, u32[]{:S(2)}, u32[]{:S(2)}) async-start(bf16[64,40,128]{2,1,0:T(8,128)(2,1)} %fusion.6), calls=%async_computation | async-start | bytes 1310720 | tf_op jit(solution)/shard_map/all_to_all | solution.py:32
  17.4 5.7 %fusion.42 = bf16[16,256,128]{2,0,1:T(8,128)(2,1)S(1)} fusion(bf16[256,128,128]{2,1,0:T(8,128)(2,1)} %param.14, bf16[128,16]{0,1:T(8,128)(2,1)S(1)} %copy-done), kind=kOutput, calls=%fused_computation.95 | convolution fusion | flops 134217728 | bytes 9441280 | tf_op jit(solution)/shard_map/ijc,ch->hij/dot_general | solution.py:259
  25.1 2.6 %collective-permute-start.4 = (bf16[256,768]{1,0:T(8,128)(2,1)S(1)}, bf16[256,768]{1,0:T(8,128)(2,1)S(1)}, u32[]{:S(2)}, u32[]{:S(2)}) collective-permute-start(bf16[256,768]{1,0:T(8,128)(2,1)S(1)} %copy-done.5), channel_id=1, source_target_pairs={{0,64},{32,96},{64,0},{96,32},{1,65},{33,97},{65,1},{97,33},{2,66}... | collective-permute-start | bytes 1179656 | tf_op jit(solution)/shard_map/ppermute | solution.py:218
  27.9 3.3 %all-to-all-done = bf16[64,40,128]{2,1,0:T(8,128)(2,1)S(1)} async-done(((bf16[64,40,128]{2,1,0:T(8,128)(2,1)}), bf16[64,40,128]{2,1,0:T(8,128)(2,1)S(1)}, u32[]{:S(2)}, u32[]{:S(2)}) %all-to-all-start) | async-done | bytes 655392 | tf_op jit(solution)/shard_map/all_to_all | solution.py:32
  32.3 6.3 %all-to-all-start.1 = ((bf16[64,16,128]{2,1,0:T(8,128)(2,1)}), bf16[64,16,128]{2,1,0:T(8,128)(2,1)S(1)}, u32[]{:S(2)}, u32[]{:S(2)}) async-start(bf16[64,16,128]{2,1,0:T(8,128)(2,1)} %broadcast_in_dim.96), calls=%async_computation.1 | async-start | bytes 524288 | tf_op jit(solution)/shard_map/all_to_all | solution.py:32
  39.8 9.6 %collective-permute-done.4.refs_5_ = bf16[256,768]{1,0:T(8,128)(2,1)S(1)} collective-permute-done((bf16[256,768]{1,0:T(8,128)(2,1)S(1)}, bf16[256,768]{1,0:T(8,128)(2,1)S(1)}, u32[]{:S(2)}, u32[]{:S(2)}) %collective-permute-start.4) | collective-permute-done | bytes 393248 | tf_op jit(solution)/shard_map/ppermute | solution.py:218
  50.6 5.2 %all-to-all-start.2 = ((bf16[16,288,128]{2,1,0:T(8,128)(2,1)}), bf16[16,288,128]{2,1,0:T(8,128)(2,1)S(1)}, u32[]{:S(2)}, u32[]{:S(2)}) async-start(bf16[16,288,128]{2,1,0:T(8,128)(2,1)} %pad_maximum_fusion), calls=%async_computation.2 | async-start | bytes 2359296 | tf_op jit(solution)/shard_map/all_to_all | solution.py:32
  55.8 2.8 %collective-permute-start.9 = (bf16[256,768]{1,0:T(8,128)(2,1)S(1)}, bf16[256,768]{1,0:T(8,128)(2,1)}, u32[]{:S(2)}, u32[]{:S(2)}) collective-permute-start(bf16[256,768]{1,0:T(8,128)(2,1)S(1)} %collective-permute-done.5.refs_7_), channel_id=1, source_target_pairs={{0,16},{16,0},{1,17},{17,1},{2,18},{18,2},{3,19},{19,3},{4,20},{20... | collective-permute-start | bytes 1179656 | tf_op jit(solution)/shard_map/ppermute | solution.py:281
  62.5 8.0 %shard_map.121 = (bf16[16,128,768]{2,1,0:T(8,128)(2,1)}, f32[16,128,1]{2,1,0:T(8,128)}, bf16[16,96,128]{2,1,0:T(8,128)(2,1)}, bf16[256,48]{1,0:T(8,128)(2,1)}, bf16[48,256]{1,0:T(8,128)(2,1)}) custom-call(s32[4]{0:T(128)} %pad_add_fusion.refs_0_, bf16[256,768]{1,0:T(8,128)(2,1)} %refs_1_, bf16[256,768]{1,0:T(8,128)(2,1)} %collective-permute-done.6.refs_2_, ...), custom_call_target="tpu_custom_call" | custom-call | flops 1000000000 | bytes 8388608 | tf_op jit(solution)/shard_map/pallas_call | solution.py:196
  70.5 1.6 %all-to-all-done.2.refs_3_ = bf16[16,288,128]{2,1,0:T(8,128)(2,1)S(1)} async-done(((bf16[16,288,128]{2,1,0:T(8,128)(2,1)}), bf16[16,288,128]{2,1,0:T(8,128)(2,1)S(1)}, u32[]{:S(2)}, u32[]{:S(2)}) %all-to-all-start.2) | async-done | bytes 1179680 | tf_op jit(solution)/shard_map/all_to_all | solution.py:32
  73.1 4.8 %shard_map.122 = (bf16[16,256,128]{2,1,0:T(8,128)(2,1)}, bf16[96,2048]{1,0:T(8,128)(2,1)}, bf16[256,48]{1,0:T(8,128)(2,1)}, bf16[256,48]{1,0:T(8,128)(2,1)}, f32[256,768]{1,0:T(8,128)}) custom-call(bf16[256,48]{1,0:T(8,128)(2,1)} %get-tuple-element.34.refs_0_, bf16[48,256]{1,0:T(8,128)(2,1)} %get-tuple-element.35.refs_1_, ...), custom_call_target="tpu_custom_call" | custom-call | flops 2000000000 | bytes 8388608 | tf_op jit(solution)/shard_map/pallas_call | solution.py:196
  77.8 5.3 %all-to-all-start.3 = ((bf16[16,256,128]{2,1,0:T(8,128)(2,1)}), bf16[16,256,128]{2,1,0:T(8,128)(2,1)S(1)}, u32[]{:S(2)}, u32[]{:S(2)}) async-start(bf16[16,256,128]{2,1,0:T(8,128)(2,1)} %get-tuple-element.47), calls=%async_computation.3 | async-start | bytes 2097152 | tf_op jit(solution)/shard_map/all_to_all | solution.py:32
  83.2 8.7 %shard_map.123 = (f32[16,64,128]{2,1,0:T(8,128)}, bf16[16,64,128]{2,1,0:T(8,128)(2,1)}, bf16[16,16,128]{2,1,0:T(8,128)(2,1)}) custom-call(s32[4]{0:T(128)} %pad_add_fusion.refs_0_, bf16[96,2048]{1,0:T(8,128)(2,1)} %get-tuple-element.38.refs_1_, bf16[256,48]{1,0:T(8,128)(2,1)} %get-tuple-element.39.refs_2_, bf16[256,48]{1,0:T(8,128)(2,1)} %get-tuple-element.40.refs_3_, ...), custom_call_target="tpu_custom_call" | custom-call | flops 1000000000 | bytes 8388608 | tf_op jit(solution)/shard_map/pallas_call | solution.py:196
  91.9 2.3 %collective-permute-start.11 = (bf16[16,64,128]{2,1,0:T(8,128)(2,1)}, bf16[16,64,128]{2,1,0:T(8,128)(2,1)S(1)}, u32[]{:S(2)}, u32[]{:S(2)}) collective-permute-start(bf16[16,64,128]{2,1,0:T(8,128)(2,1)} %get-tuple-element.45), channel_id=1, source_target_pairs={{0,16},{16,0},{1,17},{17,1},{2,18},{18,2},{3,19},{19,3},{4,20},{20... | collective-permute-start | bytes 786440 | tf_op jit(solution)/shard_map/ppermute | solution.py:327
  97.3 1.6 %pad_maximum_fusion.1 = bf16[16,80,128]{2,1,0:T(8,128)(2,1)} fusion(bf16[16,16,128]{2,1,0:T(8,128)(2,1)} %get-tuple-element.46, bf16[16,64,128]{2,1,0:T(8,128)(2,1)S(1)} %add_convert_fusion), kind=kLoop, calls=%fused_computation.25 | loop fusion | flops 655360 | bytes 655360 | tf_op jit(solution)/shard_map/concatenate | solution.py:328
  98.9 6.9 %all-to-all-start.4 = ((bf16[16,80,128]{2,1,0:T(8,128)(2,1)}), bf16[16,80,128]{2,1,0:T(8,128)(2,1)S(1)}, u32[]{:S(2)}, u32[]{:S(2)}) async-start(bf16[16,80,128]{2,1,0:T(8,128)(2,1)} %pad_maximum_fusion.1), calls=%async_computation.4 | async-start | bytes 655360 | tf_op jit(solution)/shard_map/all_to_all | solution.py:32
  105.8 5.1 %convolution_bitcast_fusion = f32[16,128]{1,0:T(8,128)S(1)} fusion(bf16[256,128,128]{2,1,0:T(8,128)(2,1)} %param.14, bf16[16,256,128]{2,1,0:T(8,128)(2,1)S(1)} %all-to-all-done.3), kind=kOutput, calls=%fused_computation.10 | convolution fusion | flops 134217728 | bytes 9445376 | tf_op jit(solution)/shard_map/ijc,hij->hc/dot_general | solution.py:331
  110.9 3.8 %all-to-all-done.4 = bf16[16,80,128]{2,1,0:T(8,128)(2,1)S(1)} async-done(((bf16[16,80,128]{2,1,0:T(8,128)(2,1)}), bf16[16,80,128]{2,1,0:T(8,128)(2,1)S(1)}, u32[]{:S(2)}, u32[]{:S(2)}) %all-to-all-start.4) | async-done | bytes 327712 | tf_op jit(solution)/shard_map/all_to_all | solution.py:32
  115.6 3.3 %all-to-all-start.5 = ((bf16[4,128,128]{2,1,0:T(8,128)(2,1)}), bf16[4,128,128]{2,1,0:T(8,128)(2,1)S(1)}, u32[]{:S(2)}, u32[]{:S(2)}) async-start(bf16[4,128,128]{2,1,0:T(8,128)(2,1)} %broadcast_in_dim.98), calls=%async_computation.5 | async-start | bytes 262144 | tf_op jit(solution)/shard_map/all_to_all | solution.py:32
  118.9 4.8 %all-to-all-done.5 = bf16[4,128,128]{2,1,0:T(8,128)(2,1)S(1)} async-done(((bf16[4,128,128]{2,1,0:T(8,128)(2,1)}), bf16[4,128,128]{2,1,0:T(8,128)(2,1)S(1)}, u32[]{:S(2)}, u32[]{:S(2)}) %all-to-all-start.5) | async-done | bytes 131104 | tf_op jit(solution)/shard_map/all_to_all | solution.py:32
  125.0 3.6 %all-to-all-start.6 = ((bf16[16,160,128]{2,1,0:T(8,128)(2,1)}), bf16[16,160,128]{2,1,0:T(8,128)(2,1)S(1)}, u32[]{:S(2)}, u32[]{:S(2)}) async-start(bf16[16,160,128]{2,1,0:T(8,128)(2,1)} %broadcast_in_dim.101), calls=%async_computation.6 | async-start | bytes 1310720 | tf_op jit(solution)/shard_map/all_to_all | solution.py:32
  128.9 10.5 %all-to-all-done.6 = bf16[16,160,128]{2,1,0:T(8,128)(2,1)S(1)} async-done(((bf16[16,160,128]{2,1,0:T(8,128)(2,1)}), bf16[16,160,128]{2,1,0:T(8,128)(2,1)S(1)}, u32[]{:S(2)}, u32[]{:S(2)}) %all-to-all-start.6) | async-done | bytes 655392 | tf_op jit(solution)/shard_map/all_to_all | solution.py:32
  139.4 3.2 %collective-permute-start.14 = (f32[16,128]{1,0:T(8,128)S(1)}, f32[16,128]{1,0:T(8,128)S(1)}, u32[]{:S(2)}, u32[]{:S(2)}) collective-permute-start(f32[16,128]{1,0:T(8,128)S(1)} %slice_add_fusion.2), channel_id=1, source_target_pairs={{0,16},{16,0},{1,17},{17,1},{2,18},{18,2},{3,19},{19,3},{4,20},{20... | collective-permute-start | bytes 24584 | tf_op jit(solution)/shard_map/ppermute | solution.py:381
  (114 shorter events, 23.8 us)
Async XLA Ops:
  0.6 2.7 %collective-permute-start = (s32[128]{0:T(128)}, s32[128]{0:T(128)S(1)}, u32[]{:S(2)}, u32[]{:S(2)}) collective-permute-start(s32[128]{0:T(128)} %param.11), channel_id=1, source_target_pairs={{0,16},{16,0},{1,17},{17,1},{2,18},{18,2},{3,19},{19,3},{4,20},{20... | collective-permute-start | bytes 1544 | tf_op jit(solution)/shard_map/ppermute | solution.py:240
  2.1 1.4 collective-permute-start.1
  2.2 1.5 %collective-permute-start.2 = (bf16[128,128]{1,0:T(8,128)(2,1)}, bf16[128,128]{1,0:T(8,128)(2,1)S(1)}, u32[]{:S(2)}, u32[]{:S(2)}) collective-permute-start(bf16[128,128]{1,0:T(8,128)(2,1)} %param.12), channel_id=1, source_target_pairs={{0,16},{16,0},{1,17},{17,1},{2,18},{18,2},{3,19},{19,3},{4,20},{20... | collective-permute-start | bytes 98312 | tf_op jit(solution)/shard_map/ppermute | solution.py:242
  6.1 25.1 %all-to-all-start = ((bf16[64,40,128]{2,1,0:T(8,128)(2,1)}), bf16[64,40,128]{2,1,0:T(8,128)(2,1)S(1)}, u32[]{:S(2)}, u32[]{:S(2)}) async-start(bf16[64,40,128]{2,1,0:T(8,128)(2,1)} %fusion.6), calls=%async_computation | async-start | bytes 1310720 | tf_op jit(solution)/shard_map/all_to_all | solution.py:32
  24.1 15.8 %collective-permute-start.3 = (bf16[256,768]{1,0:T(8,128)(2,1)S(1)}, bf16[256,768]{1,0:T(8,128)(2,1)S(1)}, u32[]{:S(2)}, u32[]{:S(2)}) collective-permute-start(bf16[256,768]{1,0:T(8,128)(2,1)S(1)} %copy-done.5), channel_id=1, source_target_pairs={{0,32},{32,0},{64,96},{96,64},{1,33},{33,1},{65,97},{97,65},{2,34}... | collective-permute-start | bytes 1179656 | tf_op jit(solution)/shard_map/ppermute | solution.py:218
  25.1 24.4 %collective-permute-start.4 = (bf16[256,768]{1,0:T(8,128)(2,1)S(1)}, bf16[256,768]{1,0:T(8,128)(2,1)S(1)}, u32[]{:S(2)}, u32[]{:S(2)}) collective-permute-start(bf16[256,768]{1,0:T(8,128)(2,1)S(1)} %copy-done.5), channel_id=1, source_target_pairs={{0,64},{32,96},{64,0},{96,32},{1,65},{33,97},{65,1},{97,33},{2,66}... | collective-permute-start | bytes 1179656 | tf_op jit(solution)/shard_map/ppermute | solution.py:218
  27.7 21.8 %collective-permute-start.5 = (bf16[256,768]{1,0:T(8,128)(2,1)S(1)}, bf16[256,768]{1,0:T(8,128)(2,1)S(1)}, u32[]{:S(2)}, u32[]{:S(2)}) collective-permute-start(bf16[256,768]{1,0:T(8,128)(2,1)S(1)} %copy-done.5), channel_id=1, source_target_pairs={{0,96},{32,64},{64,32},{96,0},{1,97},{33,65},{65,33},{97,1},{2,98}... | collective-permute-start | bytes 1179656 | tf_op jit(solution)/shard_map/ppermute | solution.py:218
  32.3 18.2 %all-to-all-start.1 = ((bf16[64,16,128]{2,1,0:T(8,128)(2,1)}), bf16[64,16,128]{2,1,0:T(8,128)(2,1)S(1)}, u32[]{:S(2)}, u32[]{:S(2)}) async-start(bf16[64,16,128]{2,1,0:T(8,128)(2,1)} %broadcast_in_dim.96), calls=%async_computation.1 | async-start | bytes 524288 | tf_op jit(solution)/shard_map/all_to_all | solution.py:32
  39.8 20.4 %copy-start.4 = (bf16[768,128]{1,0:T(8,128)(2,1)S(1)}, bf16[768,128]{1,0:T(8,128)(2,1)}, u32[]{:S(2)}) copy-start(bf16[768,128]{1,0:T(8,128)(2,1)} %refs_10_.1) | copy-start | bytes 589828
  39.8 22.3 %copy-start.6 = (bf16[256,768]{1,0:T(8,128)(2,1)}, bf16[256,768]{1,0:T(8,128)(2,1)S(1)}, u32[]{:S(2)}) copy-start(bf16[256,768]{1,0:T(8,128)(2,1)S(1)} %collective-permute-done.3.refs_3_) | copy-start | bytes 1179652
  50.6 21.5 %all-to-all-start.2 = ((bf16[16,288,128]{2,1,0:T(8,128)(2,1)}), bf16[16,288,128]{2,1,0:T(8,128)(2,1)S(1)}, u32[]{:S(2)}, u32[]{:S(2)}) async-start(bf16[16,288,128]{2,1,0:T(8,128)(2,1)} %pad_maximum_fusion), calls=%async_computation.2 | async-start | bytes 2359296 | tf_op jit(solution)/shard_map/all_to_all | solution.py:32
  55.8 6.0 %collective-permute-start.9 = (bf16[256,768]{1,0:T(8,128)(2,1)S(1)}, bf16[256,768]{1,0:T(8,128)(2,1)}, u32[]{:S(2)}, u32[]{:S(2)}) collective-permute-start(bf16[256,768]{1,0:T(8,128)(2,1)S(1)} %collective-permute-done.5.refs_7_), channel_id=1, source_target_pairs={{0,16},{16,0},{1,17},{17,1},{2,18},{18,2},{3,19},{19,3},{4,20},{20... | collective-permute-start | bytes 1179656 | tf_op jit(solution)/shard_map/ppermute | solution.py:281
  58.6 3.2 %collective-permute-start.8 = (bf16[256,768]{1,0:T(8,128)(2,1)}, bf16[256,768]{1,0:T(8,128)(2,1)}, u32[]{:S(2)}, u32[]{:S(2)}) collective-permute-start(bf16[256,768]{1,0:T(8,128)(2,1)} %copy-done.7), channel_id=1, source_target_pairs={{0,16},{16,0},{1,17},{17,1},{2,18},{18,2},{3,19},{19,3},{4,20},{20... | collective-permute-start | bytes 1179656 | tf_op jit(solution)/shard_map/ppermute | solution.py:281
  58.7 3.1 %collective-permute-start.7 = (bf16[256,768]{1,0:T(8,128)(2,1)S(1)}, bf16[256,768]{1,0:T(8,128)(2,1)}, u32[]{:S(2)}, u32[]{:S(2)}) collective-permute-start(bf16[256,768]{1,0:T(8,128)(2,1)S(1)} %collective-permute-done.3.refs_3_), channel_id=1, source_target_pairs={{0,16},{16,0},{1,17},{17,1},{2,18},{18,2},{3,19},{19,3},{4,20},{20... | collective-permute-start | bytes 1179656 | tf_op jit(solution)/shard_map/ppermute | solution.py:281
  59.1 3.0 %collective-permute-start.6 = (bf16[256,768]{1,0:T(8,128)(2,1)S(1)}, bf16[256,768]{1,0:T(8,128)(2,1)}, u32[]{:S(2)}, u32[]{:S(2)}) collective-permute-start(bf16[256,768]{1,0:T(8,128)(2,1)S(1)} %copy-done.5), channel_id=1, source_target_pairs={{0,16},{16,0},{1,17},{17,1},{2,18},{18,2},{3,19},{19,3},{4,20},{20... | collective-permute-start | bytes 1179656 | tf_op jit(solution)/shard_map/ppermute | solution.py:281
  59.2 2.6 %collective-permute-start.10 = (bf16[4,256,128]{2,1,0:T(8,128)(2,1)S(1)}, bf16[4,256,128]{2,1,0:T(8,128)(2,1)S(1)}, u32[]{:S(2)}, u32[]{:S(2)}) collective-permute-start(bf16[4,256,128]{2,1,0:T(8,128)(2,1)S(1)} %bitcast.33), channel_id=1, source_target_pairs={{0,16},{16,0},{1,17},{17,1},{2,18},{18,2},{3,19},{19,3},{4,20},{20... | collective-permute-start | bytes 786440 | tf_op jit(solution)/shard_map/ppermute | solution.py:282
  77.8 21.1 %all-to-all-start.3 = ((bf16[16,256,128]{2,1,0:T(8,128)(2,1)}), bf16[16,256,128]{2,1,0:T(8,128)(2,1)S(1)}, u32[]{:S(2)}, u32[]{:S(2)}) async-start(bf16[16,256,128]{2,1,0:T(8,128)(2,1)} %get-tuple-element.47), calls=%async_computation.3 | async-start | bytes 2097152 | tf_op jit(solution)/shard_map/all_to_all | solution.py:32
  91.9 4.3 %collective-permute-start.11 = (bf16[16,64,128]{2,1,0:T(8,128)(2,1)}, bf16[16,64,128]{2,1,0:T(8,128)(2,1)S(1)}, u32[]{:S(2)}, u32[]{:S(2)}) collective-permute-start(bf16[16,64,128]{2,1,0:T(8,128)(2,1)} %get-tuple-element.45), channel_id=1, source_target_pairs={{0,16},{16,0},{1,17},{17,1},{2,18},{18,2},{3,19},{19,3},{4,20},{20... | collective-permute-start | bytes 786440 | tf_op jit(solution)/shard_map/ppermute | solution.py:327
  95.0 1.2 collective-permute-start.12
  98.9 15.9 %all-to-all-start.4 = ((bf16[16,80,128]{2,1,0:T(8,128)(2,1)}), bf16[16,80,128]{2,1,0:T(8,128)(2,1)S(1)}, u32[]{:S(2)}, u32[]{:S(2)}) async-start(bf16[16,80,128]{2,1,0:T(8,128)(2,1)} %pad_maximum_fusion.1), calls=%async_computation.4 | async-start | bytes 655360 | tf_op jit(solution)/shard_map/all_to_all | solution.py:32
  115.6 8.1 %all-to-all-start.5 = ((bf16[4,128,128]{2,1,0:T(8,128)(2,1)}), bf16[4,128,128]{2,1,0:T(8,128)(2,1)S(1)}, u32[]{:S(2)}, u32[]{:S(2)}) async-start(bf16[4,128,128]{2,1,0:T(8,128)(2,1)} %broadcast_in_dim.98), calls=%async_computation.5 | async-start | bytes 262144 | tf_op jit(solution)/shard_map/all_to_all | solution.py:32
  125.0 14.4 %all-to-all-start.6 = ((bf16[16,160,128]{2,1,0:T(8,128)(2,1)}), bf16[16,160,128]{2,1,0:T(8,128)(2,1)S(1)}, u32[]{:S(2)}, u32[]{:S(2)}) async-start(bf16[16,160,128]{2,1,0:T(8,128)(2,1)} %broadcast_in_dim.101), calls=%async_computation.6 | async-start | bytes 1310720 | tf_op jit(solution)/shard_map/all_to_all | solution.py:32
  139.4 4.2 %collective-permute-start.14 = (f32[16,128]{1,0:T(8,128)S(1)}, f32[16,128]{1,0:T(8,128)S(1)}, u32[]{:S(2)}, u32[]{:S(2)}) collective-permute-start(f32[16,128]{1,0:T(8,128)S(1)} %slice_add_fusion.2), channel_id=1, source_target_pairs={{0,16},{16,0},{1,17},{17,1},{2,18},{18,2},{3,19},{19,3},{4,20},{20... | collective-permute-start | bytes 24584 | tf_op jit(solution)/shard_map/ppermute | solution.py:381
  143.5 1.3 collective-permute-start.13
  (10 other events, 100.7 us)

commit v5 on v4

--- a/solution.py
+++ b/solution.py
@@ -333,15 +333,13 @@
     block_counts = block_counts + lax.ppermute(block_counts, "k", SWAP)
     rest = jnp.sum(hop.astype(F32), axis=0)
     heads = weight_part.shape[0]
-    hop = spread(
-        jnp.concatenate(
-            [rest[: columns // 2].astype(BF), (tile_base + rest[columns // 2 :]).astype(BF)]
-            + high_low(weight_part)
-            + [jnp.pad(block_counts, ((0, 15), (0, 0)))],
-            axis=0,
-        ),
-        "z",
-    )
+    to_z = jnp.concatenate(
+        [rest[: columns // 2].astype(BF), (tile_base + rest[columns // 2 :]).astype(BF)]
+        + high_low(weight_part)
+        + [jnp.pad(block_counts, ((0, 15), (0, 0)))],
+        axis=0,
+    )
+    hop = jnp.stack([to_z] + [turn(to_z, "z", d) for d in (1, 2, 3)])
     at_back = columns // 2
     at_weight = at_back + tile
     at_counts = at_weight + 2 * heads
@@ -365,19 +363,16 @@
     of_row, rest = ids // tok_rows, ids % tok_rows
     grad_ids = ids // columns * at_back + ids % at_back
     grad_ids = jnp.where(ids % columns // at_back == core, grad_ids, -1)
-    back_ids = rest // tile * at_back + of_row // 2 * tile + rest % tile
+    back_ids = rest // tile * at_back + jnp.bitwise_xor(of_row // 2, z) * tile + rest % tile
     back_ids = jnp.where(of_row % 2 == core, back_ids, -1)
-    picked = jnp.concatenate(
-        [
-            nn((back_ids[:, None] == slots).astype(BF), back_table).astype(BF),
-            nn((grad_ids[:, None] == slots).astype(BF), grad_table).astype(BF),
-        ],
-        axis=1,
-    )
-    other = lax.ppermute(picked[n_atoms:], "k", SWAP)
-    picked = picked[:n_atoms].astype(F32) + other.astype(F32)
-    atom_out = (atom_single.astype(F32) + picked[:, :width]).astype(BF)
-    grad_atom = atom_cot.astype(F32) + picked[:, width:]
+    backs = nn((back_ids[:, None] == slots).astype(BF), back_table).astype(BF)
+    grads = nn((grad_ids[:, None] == slots).astype(BF), grad_table).astype(BF)
+    other_backs = lax.ppermute(backs[n_atoms:], "k", SWAP)
+    other_grads = lax.ppermute(grads[n_atoms:], "k", SWAP)
+    backs = backs[:n_atoms].astype(F32) + other_backs.astype(F32)
+    grads = grads[:n_atoms].astype(F32) + other_grads.astype(F32)
+    atom_out = (atom_single.astype(F32) + backs).astype(BF)
+    grad_atom = atom_cot.astype(F32) + grads
     grad_bias = jnp.transpose(weight + lax.ppermute(weight, "k", SWAP))
     return (atom_out, grad_atom, grad_bias)
 

time: 147 us -> 144 us (0.980)
  waiting for transfers between devices: 38.4 us -> 33.7 us
  local copies, waits for them, and re-layouts: 7.42 us -> 5.06 us
  starting transfers between devices: 57.1 us -> 59.4 us
    all_to_all x7 -> x6, waiting for transfers between devices: 25.1 us -> 19.7 us  [exchange(): return lax.all_to_all(blocks, axis, split_axis=0, concat_axis=0, tiled=True)]
    ppermute x3 -> x6, starting transfers between devices: 3.86 us -> 8.01 us  [turn(): return lax.ppermute(value, axis, [(i, i ^ by) for i in range(size)])]
    all_to_all x7 -> x6, starting transfers between devices: 41.8 us -> 38.5 us  [exchange(): return lax.all_to_all(blocks, axis, split_axis=0, concat_axis=0, tiled=True)]
    unnamed x31 -> x27, local copies, waits for them, and re-layouts: 4.55 us -> 2.87 us
    ppermute x3 -> x6, waiting for transfers between devices: 9.62 us -> 10.9 us  [turn(): return lax.ppermute(value, axis, [(i, i ^ by) for i in range(size)])]
  transfers between devices with their start and end apart: 22 -> 25, of which waited for: 13 -> 13; matrix products, arithmetic and copies ran while one was open for 14% -> 14% of each run, Pallas kernels for 11% -> 12%
where the time goes in v5:
time: 144 us; the launch traced here: 143 us
  starting transfers between devices  59.4 us (41%)
  waiting for transfers between devices  33.7 us (23%)
  Pallas kernels  21.4 us (15%)
  matrix products  13 us (9%)
  other arithmetic  9.08 us (6%)
  local copies, waits for them, and re-layouts  5.06 us (4%)
    all_to_all x6, starting transfers between devices, exchange(): return lax.all_to_all(blocks, axis, split_axis=0, concat_axis=0, tiled=True)  38.5 us
    pallas_call x3, Pallas kernels, call(): pl.pallas_call(kernel, in_specs=specs, out_specs=[anywhere] * n_out, out_...  21.4 us
    all_to_all x6, waiting for transfers between devices, exchange(): return lax.all_to_all(blocks, axis, split_axis=0, concat_axis=0, tiled=True)  19.7 us
    ppermute x6, waiting for transfers between devices, turn(): return lax.ppermute(value, axis, [(i, i ^ by) for i in range(size)])  10.9 us
    ppermute x6, starting transfers between devices, turn(): return lax.ppermute(value, axis, [(i, i ^ by) for i in range(size)])  8.01 us
    dot_general x1, matrix products, on_device(): jnp.einsum('ijc,ch->hij', pair, w_bias, preferred_element_type=F32)  5.66 us
    dot_general x1, matrix products, on_device(): jnp.einsum('ijc,hij->hc', pair, bias_back, preferred_element_type=F32)  5.12 us
    ppermute x1, starting transfers between devices, on_device(): grad_bias = jnp.transpose(weight + lax.ppermute(weight, 'k', SWAP))  4.1 us
  transfers between devices with their start and end apart: 25, of which 13 were waited for; matrix products, arithmetic and copies ran while one was open for 14% of the time, Pallas kernels for 12%

profile of v5, /device:TPU:1, one launch (start us, length us, event | category | flops | bytes accessed | tf_op | source)
XLA Modules:
  0.0 142.6 jit_solution(17275830682659787042)
XLA Ops:
  0.6 1.5 %collective-permute-start = (s32[128]{0:T(128)}, s32[128]{0:T(128)S(1)}, u32[]{:S(2)}, u32[]{:S(2)}) collective-permute-start(s32[128]{0:T(128)} %param.11), channel_id=1, source_target_pairs={{0,16},{16,0},{1,17},{17,1},{2,18},{18,2},{3,19},{19,3},{4,20},{20... | collective-permute-start | bytes 1544 | tf_op jit(solution)/shard_map/ppermute | solution.py:240
  6.2 11.2 %all-to-all-start = ((bf16[64,40,128]{2,1,0:T(8,128)(2,1)}), bf16[64,40,128]{2,1,0:T(8,128)(2,1)S(1)}, u32[]{:S(2)}, u32[]{:S(2)}) async-start(bf16[64,40,128]{2,1,0:T(8,128)(2,1)} %fusion.6), calls=%async_computation | async-start | bytes 1310720 | tf_op jit(solution)/shard_map/all_to_all | solution.py:32
  17.4 5.7 %fusion.40 = bf16[16,256,128]{2,0,1:T(8,128)(2,1)S(1)} fusion(bf16[256,128,128]{2,1,0:T(8,128)(2,1)} %param.14, bf16[128,16]{0,1:T(8,128)(2,1)S(1)} %copy-done), kind=kOutput, calls=%fused_computation.91 | convolution fusion | flops 134217728 | bytes 9441280 | tf_op jit(solution)/shard_map/ijc,ch->hij/dot_general | solution.py:259
  25.1 2.6 %collective-permute-start.4 = (bf16[256,768]{1,0:T(8,128)(2,1)S(1)}, bf16[256,768]{1,0:T(8,128)(2,1)S(1)}, u32[]{:S(2)}, u32[]{:S(2)}) collective-permute-start(bf16[256,768]{1,0:T(8,128)(2,1)S(1)} %copy-done.5), channel_id=1, source_target_pairs={{0,64},{32,96},{64,0},{96,32},{1,65},{33,97},{65,1},{97,33},{2,66}... | collective-permute-start | bytes 1179656 | tf_op jit(solution)/shard_map/ppermute | solution.py:218
  27.9 3.3 %all-to-all-done = bf16[64,40,128]{2,1,0:T(8,128)(2,1)S(1)} async-done(((bf16[64,40,128]{2,1,0:T(8,128)(2,1)}), bf16[64,40,128]{2,1,0:T(8,128)(2,1)S(1)}, u32[]{:S(2)}, u32[]{:S(2)}) %all-to-all-start) | async-done | bytes 655392 | tf_op jit(solution)/shard_map/all_to_all | solution.py:32
  32.4 6.3 %all-to-all-start.1 = ((bf16[64,16,128]{2,1,0:T(8,128)(2,1)}), bf16[64,16,128]{2,1,0:T(8,128)(2,1)S(1)}, u32[]{:S(2)}, u32[]{:S(2)}) async-start(bf16[64,16,128]{2,1,0:T(8,128)(2,1)} %broadcast_in_dim.90), calls=%async_computation.1 | async-start | bytes 524288 | tf_op jit(solution)/shard_map/all_to_all | solution.py:32
  39.9 9.6 %collective-permute-done.4.refs_5_ = bf16[256,768]{1,0:T(8,128)(2,1)S(1)} collective-permute-done((bf16[256,768]{1,0:T(8,128)(2,1)S(1)}, bf16[256,768]{1,0:T(8,128)(2,1)S(1)}, u32[]{:S(2)}, u32[]{:S(2)}) %collective-permute-start.4) | collective-permute-done | bytes 393248 | tf_op jit(solution)/shard_map/ppermute | solution.py:218
  50.6 5.2 %all-to-all-start.2 = ((bf16[16,288,128]{2,1,0:T(8,128)(2,1)}), bf16[16,288,128]{2,1,0:T(8,128)(2,1)S(1)}, u32[]{:S(2)}, u32[]{:S(2)}) async-start(bf16[16,288,128]{2,1,0:T(8,128)(2,1)} %pad_maximum_fusion), calls=%async_computation.2 | async-start | bytes 2359296 | tf_op jit(solution)/shard_map/all_to_all | solution.py:32
  55.8 2.8 %collective-permute-start.9 = (bf16[256,768]{1,0:T(8,128)(2,1)S(1)}, bf16[256,768]{1,0:T(8,128)(2,1)}, u32[]{:S(2)}, u32[]{:S(2)}) collective-permute-start(bf16[256,768]{1,0:T(8,128)(2,1)S(1)} %collective-permute-done.5.refs_7_), channel_id=1, source_target_pairs={{0,16},{16,0},{1,17},{17,1},{2,18},{18,2},{3,19},{19,3},{4,20},{20... | collective-permute-start | bytes 1179656 | tf_op jit(solution)/shard_map/ppermute | solution.py:281
  60.5 1.3 collective-permute-done.10.refs_10_
  62.5 8.0 %shard_map.121 = (bf16[16,128,768]{2,1,0:T(8,128)(2,1)}, f32[16,128,1]{2,1,0:T(8,128)}, bf16[16,96,128]{2,1,0:T(8,128)(2,1)}, bf16[256,48]{1,0:T(8,128)(2,1)}, bf16[48,256]{1,0:T(8,128)(2,1)}) custom-call(s32[4]{0:T(128)} %pad_add_fusion.refs_0_, bf16[256,768]{1,0:T(8,128)(2,1)} %refs_1_, bf16[256,768]{1,0:T(8,128)(2,1)} %collective-permute-done.6.refs_2_, ...), custom_call_target="tpu_custom_call" | custom-call | flops 1000000000 | bytes 8388608 | tf_op jit(solution)/shard_map/pallas_call | solution.py:196
  70.5 1.6 %all-to-all-done.2.refs_3_ = bf16[16,288,128]{2,1,0:T(8,128)(2,1)S(1)} async-done(((bf16[16,288,128]{2,1,0:T(8,128)(2,1)}), bf16[16,288,128]{2,1,0:T(8,128)(2,1)S(1)}, u32[]{:S(2)}, u32[]{:S(2)}) %all-to-all-start.2) | async-done | bytes 1179680 | tf_op jit(solution)/shard_map/all_to_all | solution.py:32
  73.1 4.7 %shard_map.122 = (bf16[16,256,128]{2,1,0:T(8,128)(2,1)}, bf16[96,2048]{1,0:T(8,128)(2,1)}, bf16[256,48]{1,0:T(8,128)(2,1)}, bf16[256,48]{1,0:T(8,128)(2,1)}, f32[256,768]{1,0:T(8,128)}) custom-call(bf16[256,48]{1,0:T(8,128)(2,1)} %get-tuple-element.34.refs_0_, bf16[48,256]{1,0:T(8,128)(2,1)} %get-tuple-element.35.refs_1_, ...), custom_call_target="tpu_custom_call" | custom-call | flops 2000000000 | bytes 8388608 | tf_op jit(solution)/shard_map/pallas_call | solution.py:196
  77.8 5.3 %all-to-all-start.3 = ((bf16[16,256,128]{2,1,0:T(8,128)(2,1)}), bf16[16,256,128]{2,1,0:T(8,128)(2,1)S(1)}, u32[]{:S(2)}, u32[]{:S(2)}) async-start(bf16[16,256,128]{2,1,0:T(8,128)(2,1)} %get-tuple-element.47), calls=%async_computation.3 | async-start | bytes 2097152 | tf_op jit(solution)/shard_map/all_to_all | solution.py:32
  83.2 8.7 %shard_map.123 = (f32[16,64,128]{2,1,0:T(8,128)}, bf16[16,64,128]{2,1,0:T(8,128)(2,1)}, bf16[16,16,128]{2,1,0:T(8,128)(2,1)}) custom-call(s32[4]{0:T(128)} %pad_add_fusion.refs_0_, bf16[96,2048]{1,0:T(8,128)(2,1)} %get-tuple-element.38.refs_1_, bf16[256,48]{1,0:T(8,128)(2,1)} %get-tuple-element.39.refs_2_, bf16[256,48]{1,0:T(8,128)(2,1)} %get-tuple-element.40.refs_3_, ...), custom_call_target="tpu_custom_call" | custom-call | flops 1000000000 | bytes 8388608 | tf_op jit(solution)/shard_map/pallas_call | solution.py:196
  91.9 2.2 %collective-permute-start.11 = (bf16[16,64,128]{2,1,0:T(8,128)(2,1)}, bf16[16,64,128]{2,1,0:T(8,128)(2,1)S(1)}, u32[]{:S(2)}, u32[]{:S(2)}) collective-permute-start(bf16[16,64,128]{2,1,0:T(8,128)(2,1)} %get-tuple-element.45), channel_id=1, source_target_pairs={{0,16},{16,0},{1,17},{17,1},{2,18},{18,2},{3,19},{19,3},{4,20},{20... | collective-permute-start | bytes 786440 | tf_op jit(solution)/shard_map/ppermute | solution.py:327
  97.2 1.6 %pad_maximum_fusion.1 = bf16[16,80,128]{2,1,0:T(8,128)(2,1)} fusion(bf16[16,16,128]{2,1,0:T(8,128)(2,1)} %get-tuple-element.46, bf16[16,64,128]{2,1,0:T(8,128)(2,1)S(1)} %add_convert_fusion), kind=kLoop, calls=%fused_computation.25 | loop fusion | flops 655360 | bytes 655360 | tf_op jit(solution)/shard_map/concatenate | solution.py:328
  98.8 6.9 %all-to-all-start.4 = ((bf16[16,80,128]{2,1,0:T(8,128)(2,1)}), bf16[16,80,128]{2,1,0:T(8,128)(2,1)S(1)}, u32[]{:S(2)}, u32[]{:S(2)}) async-start(bf16[16,80,128]{2,1,0:T(8,128)(2,1)} %pad_maximum_fusion.1), calls=%async_computation.4 | async-start | bytes 655360 | tf_op jit(solution)/shard_map/all_to_all | solution.py:32
  105.7 5.1 %convolution_bitcast_fusion = f32[16,128]{1,0:T(8,128)S(1)} fusion(bf16[256,128,128]{2,1,0:T(8,128)(2,1)} %param.14, bf16[16,256,128]{2,1,0:T(8,128)(2,1)S(1)} %all-to-all-done.3), kind=kOutput, calls=%fused_computation.10 | convolution fusion | flops 134217728 | bytes 9445376 | tf_op jit(solution)/shard_map/ijc,hij->hc/dot_general | solution.py:331
  110.8 3.9 %all-to-all-done.4 = bf16[16,80,128]{2,1,0:T(8,128)(2,1)S(1)} async-done(((bf16[16,80,128]{2,1,0:T(8,128)(2,1)}), bf16[16,80,128]{2,1,0:T(8,128)(2,1)S(1)}, u32[]{:S(2)}, u32[]{:S(2)}) %all-to-all-start.4) | async-done | bytes 327712 | tf_op jit(solution)/shard_map/all_to_all | solution.py:32
  116.3 2.7 %collective-permute-start.15 = (bf16[128,128]{1,0:T(8,128)(2,1)S(1)}, bf16[128,128]{1,0:T(8,128)(2,1)S(1)}, u32[]{:S(2)}, u32[]{:S(2)}) collective-permute-start(bf16[128,128]{1,0:T(8,128)(2,1)S(1)} %constant_dynamic-update-slice_fusion.1), channel_id=1, source_target_pairs={{0,96},{32,64},{64,32},{96,0},{1,97},{33,65},{65,33},{97,1},{2,98}... | collective-permute-start | bytes 98312 | tf_op jit(solution)/shard_map/ppermute | solution.py:218
  121.7 3.6 %all-to-all-start.5 = ((bf16[16,160,128]{2,1,0:T(8,128)(2,1)}), bf16[16,160,128]{2,1,0:T(8,128)(2,1)S(1)}, u32[]{:S(2)}, u32[]{:S(2)}) async-start(bf16[16,160,128]{2,1,0:T(8,128)(2,1)} %broadcast_in_dim.94), calls=%async_computation.5 | async-start | bytes 1310720 | tf_op jit(solution)/shard_map/all_to_all | solution.py:32
  125.3 9.8 %all-to-all-done.5 = bf16[16,160,128]{2,1,0:T(8,128)(2,1)S(1)} async-done(((bf16[16,160,128]{2,1,0:T(8,128)(2,1)}), bf16[16,160,128]{2,1,0:T(8,128)(2,1)S(1)}, u32[]{:S(2)}, u32[]{:S(2)}) %all-to-all-start.5) | async-done | bytes 655392 | tf_op jit(solution)/shard_map/all_to_all | solution.py:32
  135.1 4.1 %collective-permute-start.18 = (f32[16,128]{1,0:T(8,128)S(1)}, f32[16,128]{1,0:T(8,128)S(1)}, u32[]{:S(2)}, u32[]{:S(2)}) collective-permute-start(f32[16,128]{1,0:T(8,128)S(1)} %slice_add_fusion), channel_id=1, source_target_pairs={{0,16},{16,0},{1,17},{17,1},{2,18},{18,2},{3,19},{19,3},{4,20},{20... | collective-permute-start | bytes 24584 | tf_op jit(solution)/shard_map/ppermute | solution.py:376
  (116 shorter events, 24.0 us)
Async XLA Ops:
  0.6 2.7 %collective-permute-start = (s32[128]{0:T(128)}, s32[128]{0:T(128)S(1)}, u32[]{:S(2)}, u32[]{:S(2)}) collective-permute-start(s32[128]{0:T(128)} %param.11), channel_id=1, source_target_pairs={{0,16},{16,0},{1,17},{17,1},{2,18},{18,2},{3,19},{19,3},{4,20},{20... | collective-permute-start | bytes 1544 | tf_op jit(solution)/shard_map/ppermute | solution.py:240
  2.1 1.4 collective-permute-start.1
  2.2 1.5 %collective-permute-start.2 = (bf16[128,128]{1,0:T(8,128)(2,1)}, bf16[128,128]{1,0:T(8,128)(2,1)S(1)}, u32[]{:S(2)}, u32[]{:S(2)}) collective-permute-start(bf16[128,128]{1,0:T(8,128)(2,1)} %param.12), channel_id=1, source_target_pairs={{0,16},{16,0},{1,17},{17,1},{2,18},{18,2},{3,19},{19,3},{4,20},{20... | collective-permute-start | bytes 98312 | tf_op jit(solution)/shard_map/ppermute | solution.py:242
  6.2 25.1 %all-to-all-start = ((bf16[64,40,128]{2,1,0:T(8,128)(2,1)}), bf16[64,40,128]{2,1,0:T(8,128)(2,1)S(1)}, u32[]{:S(2)}, u32[]{:S(2)}) async-start(bf16[64,40,128]{2,1,0:T(8,128)(2,1)} %fusion.6), calls=%async_computation | async-start | bytes 1310720 | tf_op jit(solution)/shard_map/all_to_all | solution.py:32
  24.1 15.8 %collective-permute-start.3 = (bf16[256,768]{1,0:T(8,128)(2,1)S(1)}, bf16[256,768]{1,0:T(8,128)(2,1)S(1)}, u32[]{:S(2)}, u32[]{:S(2)}) collective-permute-start(bf16[256,768]{1,0:T(8,128)(2,1)S(1)} %copy-done.5), channel_id=1, source_target_pairs={{0,32},{32,0},{64,96},{96,64},{1,33},{33,1},{65,97},{97,65},{2,34}... | collective-permute-start | bytes 1179656 | tf_op jit(solution)/shard_map/ppermute | solution.py:218
  25.1 24.4 %collective-permute-start.4 = (bf16[256,768]{1,0:T(8,128)(2,1)S(1)}, bf16[256,768]{1,0:T(8,128)(2,1)S(1)}, u32[]{:S(2)}, u32[]{:S(2)}) collective-permute-start(bf16[256,768]{1,0:T(8,128)(2,1)S(1)} %copy-done.5), channel_id=1, source_target_pairs={{0,64},{32,96},{64,0},{96,32},{1,65},{33,97},{65,1},{97,33},{2,66}... | collective-permute-start | bytes 1179656 | tf_op jit(solution)/shard_map/ppermute | solution.py:218
  27.7 21.8 %collective-permute-start.5 = (bf16[256,768]{1,0:T(8,128)(2,1)S(1)}, bf16[256,768]{1,0:T(8,128)(2,1)S(1)}, u32[]{:S(2)}, u32[]{:S(2)}) collective-permute-start(bf16[256,768]{1,0:T(8,128)(2,1)S(1)} %copy-done.5), channel_id=1, source_target_pairs={{0,96},{32,64},{64,32},{96,0},{1,97},{33,65},{65,33},{97,1},{2,98}... | collective-permute-start | bytes 1179656 | tf_op jit(solution)/shard_map/ppermute | solution.py:218
  32.4 18.2 %all-to-all-start.1 = ((bf16[64,16,128]{2,1,0:T(8,128)(2,1)}), bf16[64,16,128]{2,1,0:T(8,128)(2,1)S(1)}, u32[]{:S(2)}, u32[]{:S(2)}) async-start(bf16[64,16,128]{2,1,0:T(8,128)(2,1)} %broadcast_in_dim.90), calls=%async_computation.1 | async-start | bytes 524288 | tf_op jit(solution)/shard_map/all_to_all | solution.py:32
  50.6 21.5 %all-to-all-start.2 = ((bf16[16,288,128]{2,1,0:T(8,128)(2,1)}), bf16[16,288,128]{2,1,0:T(8,128)(2,1)S(1)}, u32[]{:S(2)}, u32[]{:S(2)}) async-start(bf16[16,288,128]{2,1,0:T(8,128)(2,1)} %pad_maximum_fusion), calls=%async_computation.2 | async-start | bytes 2359296 | tf_op jit(solution)/shard_map/all_to_all | solution.py:32
  55.8 6.0 %collective-permute-start.9 = (bf16[256,768]{1,0:T(8,128)(2,1)S(1)}, bf16[256,768]{1,0:T(8,128)(2,1)}, u32[]{:S(2)}, u32[]{:S(2)}) collective-permute-start(bf16[256,768]{1,0:T(8,128)(2,1)S(1)} %collective-permute-done.5.refs_7_), channel_id=1, source_target_pairs={{0,16},{16,0},{1,17},{17,1},{2,18},{18,2},{3,19},{19,3},{4,20},{20... | collective-permute-start | bytes 1179656 | tf_op jit(solution)/shard_map/ppermute | solution.py:281
  58.6 3.2 %collective-permute-start.8 = (bf16[256,768]{1,0:T(8,128)(2,1)}, bf16[256,768]{1,0:T(8,128)(2,1)}, u32[]{:S(2)}, u32[]{:S(2)}) collective-permute-start(bf16[256,768]{1,0:T(8,128)(2,1)} %copy-done.7), channel_id=1, source_target_pairs={{0,16},{16,0},{1,17},{17,1},{2,18},{18,2},{3,19},{19,3},{4,20},{20... | collective-permute-start | bytes 1179656 | tf_op jit(solution)/shard_map/ppermute | solution.py:281
  58.7 3.1 %collective-permute-start.7 = (bf16[256,768]{1,0:T(8,128)(2,1)S(1)}, bf16[256,768]{1,0:T(8,128)(2,1)}, u32[]{:S(2)}, u32[]{:S(2)}) collective-permute-start(bf16[256,768]{1,0:T(8,128)(2,1)S(1)} %collective-permute-done.3.refs_3_), channel_id=1, source_target_pairs={{0,16},{16,0},{1,17},{17,1},{2,18},{18,2},{3,19},{19,3},{4,20},{20... | collective-permute-start | bytes 1179656 | tf_op jit(solution)/shard_map/ppermute | solution.py:281
  59.1 3.0 %collective-permute-start.6 = (bf16[256,768]{1,0:T(8,128)(2,1)S(1)}, bf16[256,768]{1,0:T(8,128)(2,1)}, u32[]{:S(2)}, u32[]{:S(2)}) collective-permute-start(bf16[256,768]{1,0:T(8,128)(2,1)S(1)} %copy-done.5), channel_id=1, source_target_pairs={{0,16},{16,0},{1,17},{17,1},{2,18},{18,2},{3,19},{19,3},{4,20},{20... | collective-permute-start | bytes 1179656 | tf_op jit(solution)/shard_map/ppermute | solution.py:281
  59.2 2.6 %collective-permute-start.10 = (bf16[4,256,128]{2,1,0:T(8,128)(2,1)S(1)}, bf16[4,256,128]{2,1,0:T(8,128)(2,1)S(1)}, u32[]{:S(2)}, u32[]{:S(2)}) collective-permute-start(bf16[4,256,128]{2,1,0:T(8,128)(2,1)S(1)} %bitcast.37), channel_id=1, source_target_pairs={{0,16},{16,0},{1,17},{17,1},{2,18},{18,2},{3,19},{19,3},{4,20},{20... | collective-permute-start | bytes 786440 | tf_op jit(solution)/shard_map/ppermute | solution.py:282
  77.8 21.0 %all-to-all-start.3 = ((bf16[16,256,128]{2,1,0:T(8,128)(2,1)}), bf16[16,256,128]{2,1,0:T(8,128)(2,1)S(1)}, u32[]{:S(2)}, u32[]{:S(2)}) async-start(bf16[16,256,128]{2,1,0:T(8,128)(2,1)} %get-tuple-element.47), calls=%async_computation.3 | async-start | bytes 2097152 | tf_op jit(solution)/shard_map/all_to_all | solution.py:32
  91.9 4.3 %collective-permute-start.11 = (bf16[16,64,128]{2,1,0:T(8,128)(2,1)}, bf16[16,64,128]{2,1,0:T(8,128)(2,1)S(1)}, u32[]{:S(2)}, u32[]{:S(2)}) collective-permute-start(bf16[16,64,128]{2,1,0:T(8,128)(2,1)} %get-tuple-element.45), channel_id=1, source_target_pairs={{0,16},{16,0},{1,17},{17,1},{2,18},{18,2},{3,19},{19,3},{4,20},{20... | collective-permute-start | bytes 786440 | tf_op jit(solution)/shard_map/ppermute | solution.py:327
  98.8 15.9 %all-to-all-start.4 = ((bf16[16,80,128]{2,1,0:T(8,128)(2,1)}), bf16[16,80,128]{2,1,0:T(8,128)(2,1)S(1)}, u32[]{:S(2)}, u32[]{:S(2)}) async-start(bf16[16,80,128]{2,1,0:T(8,128)(2,1)} %pad_maximum_fusion.1), calls=%async_computation.4 | async-start | bytes 655360 | tf_op jit(solution)/shard_map/all_to_all | solution.py:32
  114.8 4.2 %collective-permute-start.13 = (bf16[128,128]{1,0:T(8,128)(2,1)S(1)}, bf16[128,128]{1,0:T(8,128)(2,1)S(1)}, u32[]{:S(2)}, u32[]{:S(2)}) collective-permute-start(bf16[128,128]{1,0:T(8,128)(2,1)S(1)} %constant_dynamic-update-slice_fusion.1), channel_id=1, source_target_pairs={{0,32},{32,0},{64,96},{96,64},{1,33},{33,1},{65,97},{97,65},{2,34}... | collective-permute-start | bytes 98312 | tf_op jit(solution)/shard_map/ppermute | solution.py:218
  115.2 4.6 %collective-permute-start.14 = (bf16[128,128]{1,0:T(8,128)(2,1)S(1)}, bf16[128,128]{1,0:T(8,128)(2,1)S(1)}, u32[]{:S(2)}, u32[]{:S(2)}) collective-permute-start(bf16[128,128]{1,0:T(8,128)(2,1)S(1)} %constant_dynamic-update-slice_fusion.1), channel_id=1, source_target_pairs={{0,64},{32,96},{64,0},{96,32},{1,65},{33,97},{65,1},{97,33},{2,66}... | collective-permute-start | bytes 98312 | tf_op jit(solution)/shard_map/ppermute | solution.py:218
  116.3 4.0 %collective-permute-start.15 = (bf16[128,128]{1,0:T(8,128)(2,1)S(1)}, bf16[128,128]{1,0:T(8,128)(2,1)S(1)}, u32[]{:S(2)}, u32[]{:S(2)}) collective-permute-start(bf16[128,128]{1,0:T(8,128)(2,1)S(1)} %constant_dynamic-update-slice_fusion.1), channel_id=1, source_target_pairs={{0,96},{32,64},{64,32},{96,0},{1,97},{33,65},{65,33},{97,1},{2,98}... | collective-permute-start | bytes 98312 | tf_op jit(solution)/shard_map/ppermute | solution.py:218
  121.7 13.4 %all-to-all-start.5 = ((bf16[16,160,128]{2,1,0:T(8,128)(2,1)}), bf16[16,160,128]{2,1,0:T(8,128)(2,1)S(1)}, u32[]{:S(2)}, u32[]{:S(2)}) async-start(bf16[16,160,128]{2,1,0:T(8,128)(2,1)} %broadcast_in_dim.94), calls=%async_computation.5 | async-start | bytes 1310720 | tf_op jit(solution)/shard_map/all_to_all | solution.py:32
  135.1 5.6 %collective-permute-start.18 = (f32[16,128]{1,0:T(8,128)S(1)}, f32[16,128]{1,0:T(8,128)S(1)}, u32[]{:S(2)}, u32[]{:S(2)}) collective-permute-start(f32[16,128]{1,0:T(8,128)S(1)} %slice_add_fusion), channel_id=1, source_target_pairs={{0,16},{16,0},{1,17},{17,1},{2,18},{18,2},{3,19},{19,3},{4,20},{20... | collective-permute-start | bytes 24584 | tf_op jit(solution)/shard_map/ppermute | solution.py:376
  139.7 1.6 %collective-permute-start.17 = (bf16[128,128]{1,0:T(8,128)(2,1)S(1)}, bf16[128,128]{1,0:T(8,128)(2,1)S(1)}, u32[]{:S(2)}, u32[]{:S(2)}) collective-permute-start(bf16[128,128]{1,0:T(8,128)(2,1)S(1)} %slice.121), channel_id=1, source_target_pairs={{0,16},{16,0},{1,17},{17,1},{2,18},{18,2},{3,19},{19,3},{4,20},{20... | collective-permute-start | bytes 98312 | tf_op jit(solution)/shard_map/ppermute | solution.py:371
  140.1 1.8 %collective-permute-start.16 = (bf16[128,128]{1,0:T(8,128)(2,1)S(1)}, bf16[128,128]{1,0:T(8,128)(2,1)S(1)}, u32[]{:S(2)}, u32[]{:S(2)}) collective-permute-start(bf16[128,128]{1,0:T(8,128)(2,1)S(1)} %slice.118), channel_id=1, source_target_pairs={{0,16},{16,0},{1,17},{17,1},{2,18},{18,2},{3,19},{19,3},{4,20},{20... | collective-permute-start | bytes 98312 | tf_op jit(solution)/shard_map/ppermute | solution.py:370
  (13 other events, 141.9 us)

commit v6 on v5

--- a/solution.py
+++ b/solution.py
@@ -238,13 +238,19 @@
     w_t = jnp.transpose(w_qkv, (0, 2, 1)).reshape(3 * HD, -1)
 
     ids = jnp.concatenate([atom_token, lax.ppermute(atom_token, "k", SWAP)])
-    singles = jnp.concatenate([atom_single, lax.ppermute(atom_single, "k", SWAP)], axis=0)
-    cots = jnp.concatenate([atom_cot, lax.ppermute(atom_cot, "k", SWAP)], axis=0)
+    other_single = lax.ppermute(atom_single, "k", SWAP)
+    other_cot = lax.ppermute(atom_cot, "k", SWAP)
     slots = jnp.arange(total_tokens // 2, dtype=jnp.int32)
     slots = (slots // tok_rows * 2 + core) * tok_rows + slots % tok_rows
-    onehot = (slots[:, None] == ids[None, :]).astype(BF)
-    with_ones = jnp.concatenate([singles, cots, jnp.ones_like(singles)], axis=1)
-    partial = nn(onehot, with_ones).reshape(peers, tile, 3 * width)
+    partial = 0.0
+    for held, single, cot in (
+        (ids[:n_atoms], atom_single, atom_cot),
+        (ids[n_atoms:], other_single, other_cot),
+    ):
+        onehot = (slots[:, None] == held[None, :]).astype(BF)
+        with_ones = jnp.concatenate([single, cot, jnp.ones_like(single)], axis=1)
+        partial = partial + nn(onehot, with_ones)
+    partial = partial.reshape(peers, tile, 3 * width)
     place = jnp.eye(tile, width, dtype=F32)
     partial_counts = jnp.sum(partial[:, :, 2 * width :] * place, axis=1, keepdims=True)
     to_tiles = jnp.concatenate(
@@ -256,9 +262,13 @@
         axis=1,
     )
 
-    bias = jnp.einsum("ijc,ch->hij", pair, w_bias, preferred_element_type=F32).astype(BF)
+    first, late_w = tok_rows // 4, after(w_bias, to_tiles)
+    biases = [
+        jnp.einsum("ijc,ch->hij", part, late_w, preferred_element_type=F32).astype(BF)
+        for part in (pair[:first], pair[first:])
+    ]
     from_all = exchange(to_tiles, SAME_CORE)
-    from_all = after(from_all, bias)
+    from_all = after(from_all, *biases)
     sums = jnp.sum(from_all.astype(F32), axis=0)
     tile_counts = jnp.sum(sums[2 * tile : 2 * tile + 1] * place, axis=1, keepdims=True)
     pooled_tile = (sums[:tile] / tile_counts).astype(BF)
@@ -270,10 +280,10 @@
     shared = jnp.concatenate([sums[tile : 2 * tile], count_row], axis=0).astype(BF)
     shared = jnp.broadcast_to(shared[None], (cols, 2 * tile, width))
     pooled = spread(pooled_tile, SAME_CORE)
-    late_cond = after(token_cond, bias)
+    late_cond = after(token_cond, biases[0])
     pieces = [turn(late_cond, "z", d) for d in (1, 2, 3)]
     pooled = pooled.reshape(rows // 2, tok_rows, width)
-    to_col = after(jnp.concatenate([bias, shared], axis=1), pooled, *pieces)
+    to_col = after(jnp.concatenate(biases + [shared], axis=1), pooled, *pieces)
     bias_cot = exchange(to_col, COL)
     conds = []
     for piece in [token_cond] + pieces:

time: 144 us -> 142 us (0.986)
  starting transfers between devices: 59.4 us -> 55.3 us
  waiting for transfers between devices: 33.7 us -> 35.9 us
  matrix products: 13 us -> 14.5 us
    all_to_all x6, waiting for transfers between devices: 19.7 us -> 22.7 us  [exchange(): return lax.all_to_all(blocks, axis, split_axis=0, concat_axis=0, tiled=True)]
    ppermute x4, starting transfers between devices: 3.35 us -> 1.5 us  [on_device(): conds += [piece, lax.ppermute(piece, 'k', SWAP)]]
    unnamed x27 -> x29, local copies, waits for them, and re-layouts: 2.87 us -> 1.14 us
    all_to_all x6, starting transfers between devices: 38.5 us -> 37 us  [exchange(): return lax.all_to_all(blocks, axis, split_axis=0, concat_axis=0, tiled=True)]
    dot_general x1 -> x2, matrix products: 5.66 us -> 6.81 us  [on_device(): jnp.einsum('ijc,ch->hij', part, late_w, preferred_element_type=F32)]
  transfers between devices with their start and end apart: 25 -> 25, of which waited for: 13 -> 12; matrix products, arithmetic and copies ran while one was open for 14% -> 16% of each run, Pallas kernels for 12% -> 12%
where the time goes in v6:
time: 142 us; the launch traced here: 141 us
  starting transfers between devices  55.3 us (39%)
  waiting for transfers between devices  35.9 us (25%)
  Pallas kernels  21.4 us (15%)
  matrix products  14.5 us (10%)
  other arithmetic  9.11 us (6%)
  local copies, waits for them, and re-layouts  4.03 us (3%)
    all_to_all x6, starting transfers between devices, exchange(): return lax.all_to_all(blocks, axis, split_axis=0, concat_axis=0, tiled=True)  37 us
    all_to_all x6, waiting for transfers between devices, exchange(): return lax.all_to_all(blocks, axis, split_axis=0, concat_axis=0, tiled=True)  22.7 us
    pallas_call x3, Pallas kernels, call(): pl.pallas_call(kernel, in_specs=specs, out_specs=[anywhere] * n_out, out_...  21.4 us
    ppermute x6, waiting for transfers between devices, turn(): return lax.ppermute(value, axis, [(i, i ^ by) for i in range(size)])  10.5 us
    ppermute x6, starting transfers between devices, turn(): return lax.ppermute(value, axis, [(i, i ^ by) for i in range(size)])  8.1 us
    dot_general x2, matrix products, on_device(): jnp.einsum('ijc,ch->hij', part, late_w, preferred_element_type=F32)  6.81 us
    dot_general x1, matrix products, on_device(): jnp.einsum('ijc,hij->hc', pair, bias_back, preferred_element_type=F32)  5.12 us
    ppermute x1, starting transfers between devices, on_device(): grad_bias = jnp.transpose(weight + lax.ppermute(weight, 'k', SWAP))  4.1 us
  transfers between devices with their start and end apart: 25, of which 12 were waited for; matrix products, arithmetic and copies ran while one was open for 16% of the time, Pallas kernels for 12%

profile of v6, /device:TPU:1, one launch (start us, length us, event | category | flops | bytes accessed | tf_op | source)
XLA Modules:
  0.0 141.4 jit_solution(5730665471616580082)
XLA Ops:
  0.6 1.5 %collective-permute-start = (s32[128]{0:T(128)}, s32[128]{0:T(128)S(1)}, u32[]{:S(2)}, u32[]{:S(2)}) collective-permute-start(s32[128]{0:T(128)} %param.11), channel_id=1, source_target_pairs={{0,16},{16,0},{1,17},{17,1},{2,18},{18,2},{3,19},{19,3},{4,20},{20... | collective-permute-start | bytes 1544 | tf_op jit(solution)/shard_map/ppermute | solution.py:240
  5.6 11.2 %all-to-all-start = ((bf16[64,40,128]{2,1,0:T(8,128)(2,1)}), bf16[64,40,128]{2,1,0:T(8,128)(2,1)S(1)}, u32[]{:S(2)}, u32[]{:S(2)}) async-start(bf16[64,40,128]{2,1,0:T(8,128)(2,1)} %fusion.8), calls=%async_computation | async-start | bytes 1310720 | tf_op jit(solution)/shard_map/all_to_all | solution.py:32
  16.8 2.3 %fusion.2 = bf16[16,64,128]{2,0,1:T(8,128)(2,1)S(1)} fusion(bf16[256,128,128]{2,1,0:T(8,128)(2,1)} %param.14, bf16[128,16]{0,1:T(8,128)(2,1)S(1)} %copy-done), kind=kOutput, calls=%fused_computation.2 | convolution fusion | flops 33554432 | bytes 2363392 | tf_op jit(solution)/shard_map/ijc,ch->hij/dot_general | solution.py:267
  20.3 2.6 %collective-permute-start.4 = (bf16[256,768]{1,0:T(8,128)(2,1)S(1)}, bf16[256,768]{1,0:T(8,128)(2,1)S(1)}, u32[]{:S(2)}, u32[]{:S(2)}) collective-permute-start(bf16[256,768]{1,0:T(8,128)(2,1)S(1)} %copy-done.5), channel_id=1, source_target_pairs={{0,64},{32,96},{64,0},{96,32},{1,65},{33,97},{65,1},{97,33},{2,66}... | collective-permute-start | bytes 1179656 | tf_op jit(solution)/shard_map/ppermute | solution.py:218
  23.2 4.5 %fusion = bf16[16,192,128]{2,0,1:T(8,128)(2,1)S(1)} fusion(bf16[256,128,128]{2,1,0:T(8,128)(2,1)} %param.14, bf16[128,16]{0,1:T(8,128)(2,1)S(1)} %copy-done), kind=kOutput, calls=%fused_computation | convolution fusion | flops 100663296 | bytes 7081984 | tf_op jit(solution)/shard_map/ijc,ch->hij/dot_general | solution.py:267
  27.9 3.0 %all-to-all-done = bf16[64,40,128]{2,1,0:T(8,128)(2,1)S(1)} async-done(((bf16[64,40,128]{2,1,0:T(8,128)(2,1)}), bf16[64,40,128]{2,1,0:T(8,128)(2,1)S(1)}, u32[]{:S(2)}, u32[]{:S(2)}) %all-to-all-start) | async-done | bytes 655392 | tf_op jit(solution)/shard_map/all_to_all | solution.py:32
  32.0 6.6 %all-to-all-start.1 = ((bf16[64,16,128]{2,1,0:T(8,128)(2,1)}), bf16[64,16,128]{2,1,0:T(8,128)(2,1)S(1)}, u32[]{:S(2)}, u32[]{:S(2)}) async-start(bf16[64,16,128]{2,1,0:T(8,128)(2,1)} %broadcast_in_dim.60), calls=%async_computation.1 | async-start | bytes 524288 | tf_op jit(solution)/shard_map/all_to_all | solution.py:32
  40.5 7.5 %collective-permute-done.4.refs_5_ = bf16[256,768]{1,0:T(8,128)(2,1)S(1)} collective-permute-done((bf16[256,768]{1,0:T(8,128)(2,1)S(1)}, bf16[256,768]{1,0:T(8,128)(2,1)S(1)}, u32[]{:S(2)}, u32[]{:S(2)}) %collective-permute-start.4) | collective-permute-done | bytes 393248 | tf_op jit(solution)/shard_map/ppermute | solution.py:218
  49.4 4.6 %all-to-all-start.2 = ((bf16[16,288,128]{2,1,0:T(8,128)(2,1)}), bf16[16,288,128]{2,1,0:T(8,128)(2,1)S(1)}, u32[]{:S(2)}, u32[]{:S(2)}) async-start(bf16[16,288,128]{2,1,0:T(8,128)(2,1)} %pad_maximum_fusion), calls=%async_computation.2 | async-start | bytes 2359296 | tf_op jit(solution)/shard_map/all_to_all | solution.py:32
  56.8 1.6 %collective-permute-done.10.refs_10_ = bf16[4,256,128]{2,1,0:T(8,128)(2,1)} collective-permute-done((bf16[4,256,128]{2,1,0:T(8,128)(2,1)S(1)}, bf16[4,256,128]{2,1,0:T(8,128)(2,1)}, u32[]{:S(2)}, u32[]{:S(2)}) %collective-permute-start.10) | collective-permute-done | bytes 262176 | tf_op jit(solution)/shard_map/ppermute | solution.py:292
  58.5 8.0 %shard_map.121 = (bf16[16,128,768]{2,1,0:T(8,128)(2,1)}, f32[16,128,1]{2,1,0:T(8,128)}, bf16[16,96,128]{2,1,0:T(8,128)(2,1)}, bf16[256,48]{1,0:T(8,128)(2,1)}, bf16[48,256]{1,0:T(8,128)(2,1)}) custom-call(s32[4]{0:T(128)} %pad_add_fusion.refs_0_, bf16[256,768]{1,0:T(8,128)(2,1)} %refs_1_, bf16[256,768]{1,0:T(8,128)(2,1)} %collective-permute-done.6.refs_2_, ...), custom_call_target="tpu_custom_call" | custom-call | flops 1000000000 | bytes 8388608 | tf_op jit(solution)/shard_map/pallas_call | solution.py:196
  66.5 5.0 %all-to-all-done.2.refs_3_ = bf16[16,288,128]{2,1,0:T(8,128)(2,1)S(1)} async-done(((bf16[16,288,128]{2,1,0:T(8,128)(2,1)}), bf16[16,288,128]{2,1,0:T(8,128)(2,1)S(1)}, u32[]{:S(2)}, u32[]{:S(2)}) %all-to-all-start.2) | async-done | bytes 1179680 | tf_op jit(solution)/shard_map/all_to_all | solution.py:32
  72.5 4.7 %shard_map.122 = (bf16[16,256,128]{2,1,0:T(8,128)(2,1)}, bf16[96,2048]{1,0:T(8,128)(2,1)}, bf16[256,48]{1,0:T(8,128)(2,1)}, bf16[256,48]{1,0:T(8,128)(2,1)}, f32[256,768]{1,0:T(8,128)}) custom-call(bf16[256,48]{1,0:T(8,128)(2,1)} %get-tuple-element.36.refs_0_, bf16[48,256]{1,0:T(8,128)(2,1)} %get-tuple-element.37.refs_1_, ...), custom_call_target="tpu_custom_call" | custom-call | flops 2000000000 | bytes 8388608 | tf_op jit(solution)/shard_map/pallas_call | solution.py:196
  77.3 5.0 %all-to-all-start.3 = ((bf16[16,256,128]{2,1,0:T(8,128)(2,1)}), bf16[16,256,128]{2,1,0:T(8,128)(2,1)S(1)}, u32[]{:S(2)}, u32[]{:S(2)}) async-start(bf16[16,256,128]{2,1,0:T(8,128)(2,1)} %get-tuple-element.49), calls=%async_computation.3 | async-start | bytes 2097152 | tf_op jit(solution)/shard_map/all_to_all | solution.py:32
  82.3 8.7 %shard_map.123 = (f32[16,64,128]{2,1,0:T(8,128)}, bf16[16,64,128]{2,1,0:T(8,128)(2,1)}, bf16[16,16,128]{2,1,0:T(8,128)(2,1)}) custom-call(s32[4]{0:T(128)} %pad_add_fusion.refs_0_, bf16[96,2048]{1,0:T(8,128)(2,1)} %get-tuple-element.40.refs_1_, bf16[256,48]{1,0:T(8,128)(2,1)} %get-tuple-element.41.refs_2_, bf16[256,48]{1,0:T(8,128)(2,1)} %get-tuple-element.42.refs_3_, ...), custom_call_target="tpu_custom_call" | custom-call | flops 1000000000 | bytes 8388608 | tf_op jit(solution)/shard_map/pallas_call | solution.py:196
  91.0 1.4 collective-permute-start.11
  95.5 1.6 %pad_maximum_fusion.1 = bf16[16,80,128]{2,1,0:T(8,128)(2,1)} fusion(bf16[16,16,128]{2,1,0:T(8,128)(2,1)} %get-tuple-element.48, bf16[16,64,128]{2,1,0:T(8,128)(2,1)S(1)} %add_convert_fusion), kind=kLoop, calls=%fused_computation.30 | loop fusion | flops 655360 | bytes 655360 | tf_op jit(solution)/shard_map/concatenate | solution.py:338
  98.0 6.0 %all-to-all-start.4 = ((bf16[16,80,128]{2,1,0:T(8,128)(2,1)}), bf16[16,80,128]{2,1,0:T(8,128)(2,1)S(1)}, u32[]{:S(2)}, u32[]{:S(2)}) async-start(bf16[16,80,128]{2,1,0:T(8,128)(2,1)} %pad_maximum_fusion.1), calls=%async_computation.4 | async-start | bytes 655360 | tf_op jit(solution)/shard_map/all_to_all | solution.py:32
  104.0 5.1 %convolution_bitcast_fusion = f32[16,128]{1,0:T(8,128)S(1)} fusion(bf16[256,128,128]{2,1,0:T(8,128)(2,1)} %param.14, bf16[16,256,128]{2,1,0:T(8,128)(2,1)S(1)} %all-to-all-done.3), kind=kOutput, calls=%fused_computation.15 | convolution fusion | flops 134217728 | bytes 9445376 | tf_op jit(solution)/shard_map/ijc,hij->hc/dot_general | solution.py:341
  109.1 3.9 %all-to-all-done.4 = bf16[16,80,128]{2,1,0:T(8,128)(2,1)S(1)} async-done(((bf16[16,80,128]{2,1,0:T(8,128)(2,1)}), bf16[16,80,128]{2,1,0:T(8,128)(2,1)S(1)}, u32[]{:S(2)}, u32[]{:S(2)}) %all-to-all-start.4) | async-done | bytes 327712 | tf_op jit(solution)/shard_map/all_to_all | solution.py:32
  115.2 2.1 %collective-permute-start.15 = (bf16[128,128]{1,0:T(8,128)(2,1)S(1)}, bf16[128,128]{1,0:T(8,128)(2,1)S(1)}, u32[]{:S(2)}, u32[]{:S(2)}) collective-permute-start(bf16[128,128]{1,0:T(8,128)(2,1)S(1)} %constant_dynamic-update-slice_fusion.1), channel_id=1, source_target_pairs={{0,96},{32,64},{64,32},{96,0},{1,97},{33,65},{65,33},{97,1},{2,98}... | collective-permute-start | bytes 98312 | tf_op jit(solution)/shard_map/ppermute | solution.py:218
  120.5 3.6 %all-to-all-start.5 = ((bf16[16,160,128]{2,1,0:T(8,128)(2,1)}), bf16[16,160,128]{2,1,0:T(8,128)(2,1)S(1)}, u32[]{:S(2)}, u32[]{:S(2)}) async-start(bf16[16,160,128]{2,1,0:T(8,128)(2,1)} %broadcast_in_dim.92), calls=%async_computation.5 | async-start | bytes 1310720 | tf_op jit(solution)/shard_map/all_to_all | solution.py:32
  124.2 9.7 %all-to-all-done.5 = bf16[16,160,128]{2,1,0:T(8,128)(2,1)S(1)} async-done(((bf16[16,160,128]{2,1,0:T(8,128)(2,1)}), bf16[16,160,128]{2,1,0:T(8,128)(2,1)S(1)}, u32[]{:S(2)}, u32[]{:S(2)}) %all-to-all-start.5) | async-done | bytes 655392 | tf_op jit(solution)/shard_map/all_to_all | solution.py:32
  133.9 4.1 %collective-permute-start.18 = (f32[16,128]{1,0:T(8,128)S(1)}, f32[16,128]{1,0:T(8,128)S(1)}, u32[]{:S(2)}, u32[]{:S(2)}) collective-permute-start(f32[16,128]{1,0:T(8,128)S(1)} %slice_add_fusion), channel_id=1, source_target_pairs={{0,16},{16,0},{1,17},{17,1},{2,18},{18,2},{3,19},{19,3},{4,20},{20... | collective-permute-start | bytes 24584 | tf_op jit(solution)/shard_map/ppermute | solution.py:386
  (121 shorter events, 25.8 us)
Async XLA Ops:
  0.6 3.3 %collective-permute-start = (s32[128]{0:T(128)}, s32[128]{0:T(128)S(1)}, u32[]{:S(2)}, u32[]{:S(2)}) collective-permute-start(s32[128]{0:T(128)} %param.11), channel_id=1, source_target_pairs={{0,16},{16,0},{1,17},{17,1},{2,18},{18,2},{3,19},{19,3},{4,20},{20... | collective-permute-start | bytes 1544 | tf_op jit(solution)/shard_map/ppermute | solution.py:240
  2.1 1.8 %collective-permute-start.1 = (bf16[128,128]{1,0:T(8,128)(2,1)}, bf16[128,128]{1,0:T(8,128)(2,1)S(1)}, u32[]{:S(2)}, u32[]{:S(2)}) collective-permute-start(bf16[128,128]{1,0:T(8,128)(2,1)} %param.10), channel_id=1, source_target_pairs={{0,16},{16,0},{1,17},{17,1},{2,18},{18,2},{3,19},{19,3},{4,20},{20... | collective-permute-start | bytes 98312 | tf_op jit(solution)/shard_map/ppermute | solution.py:241
  2.2 1.7 %collective-permute-start.2 = (bf16[128,128]{1,0:T(8,128)(2,1)}, bf16[128,128]{1,0:T(8,128)(2,1)S(1)}, u32[]{:S(2)}, u32[]{:S(2)}) collective-permute-start(bf16[128,128]{1,0:T(8,128)(2,1)} %param.12), channel_id=1, source_target_pairs={{0,16},{16,0},{1,17},{17,1},{2,18},{18,2},{3,19},{19,3},{4,20},{20... | collective-permute-start | bytes 98312 | tf_op jit(solution)/shard_map/ppermute | solution.py:242
  5.6 25.4 %all-to-all-start = ((bf16[64,40,128]{2,1,0:T(8,128)(2,1)}), bf16[64,40,128]{2,1,0:T(8,128)(2,1)S(1)}, u32[]{:S(2)}, u32[]{:S(2)}) async-start(bf16[64,40,128]{2,1,0:T(8,128)(2,1)} %fusion.8), calls=%async_computation | async-start | bytes 1310720 | tf_op jit(solution)/shard_map/all_to_all | solution.py:32
  19.2 21.3 %collective-permute-start.3 = (bf16[256,768]{1,0:T(8,128)(2,1)S(1)}, bf16[256,768]{1,0:T(8,128)(2,1)S(1)}, u32[]{:S(2)}, u32[]{:S(2)}) collective-permute-start(bf16[256,768]{1,0:T(8,128)(2,1)S(1)} %copy-done.5), channel_id=1, source_target_pairs={{0,32},{32,0},{64,96},{96,64},{1,33},{33,1},{65,97},{97,65},{2,34}... | collective-permute-start | bytes 1179656 | tf_op jit(solution)/shard_map/ppermute | solution.py:218
  20.3 27.7 %collective-permute-start.4 = (bf16[256,768]{1,0:T(8,128)(2,1)S(1)}, bf16[256,768]{1,0:T(8,128)(2,1)S(1)}, u32[]{:S(2)}, u32[]{:S(2)}) collective-permute-start(bf16[256,768]{1,0:T(8,128)(2,1)S(1)} %copy-done.5), channel_id=1, source_target_pairs={{0,64},{32,96},{64,0},{96,32},{1,65},{33,97},{65,1},{97,33},{2,66}... | collective-permute-start | bytes 1179656 | tf_op jit(solution)/shard_map/ppermute | solution.py:218
  22.9 26.3 %collective-permute-start.5 = (bf16[256,768]{1,0:T(8,128)(2,1)S(1)}, bf16[256,768]{1,0:T(8,128)(2,1)S(1)}, u32[]{:S(2)}, u32[]{:S(2)}) collective-permute-start(bf16[256,768]{1,0:T(8,128)(2,1)S(1)} %copy-done.5), channel_id=1, source_target_pairs={{0,96},{32,64},{64,32},{96,0},{1,97},{33,65},{65,33},{97,1},{2,98}... | collective-permute-start | bytes 1179656 | tf_op jit(solution)/shard_map/ppermute | solution.py:218
  32.0 17.3 %all-to-all-start.1 = ((bf16[64,16,128]{2,1,0:T(8,128)(2,1)}), bf16[64,16,128]{2,1,0:T(8,128)(2,1)S(1)}, u32[]{:S(2)}, u32[]{:S(2)}) async-start(bf16[64,16,128]{2,1,0:T(8,128)(2,1)} %broadcast_in_dim.60), calls=%async_computation.1 | async-start | bytes 524288 | tf_op jit(solution)/shard_map/all_to_all | solution.py:32
  49.4 22.2 %all-to-all-start.2 = ((bf16[16,288,128]{2,1,0:T(8,128)(2,1)}), bf16[16,288,128]{2,1,0:T(8,128)(2,1)S(1)}, u32[]{:S(2)}, u32[]{:S(2)}) async-start(bf16[16,288,128]{2,1,0:T(8,128)(2,1)} %pad_maximum_fusion), calls=%async_computation.2 | async-start | bytes 2359296 | tf_op jit(solution)/shard_map/all_to_all | solution.py:32
  54.0 4.4 %collective-permute-start.9 = (bf16[256,768]{1,0:T(8,128)(2,1)S(1)}, bf16[256,768]{1,0:T(8,128)(2,1)}, u32[]{:S(2)}, u32[]{:S(2)}) collective-permute-start(bf16[256,768]{1,0:T(8,128)(2,1)S(1)} %collective-permute-done.5.refs_7_), channel_id=1, source_target_pairs={{0,16},{16,0},{1,17},{17,1},{2,18},{18,2},{3,19},{19,3},{4,20},{20... | collective-permute-start | bytes 1179656 | tf_op jit(solution)/shard_map/ppermute | solution.py:291
  54.9 3.5 %collective-permute-start.8 = (bf16[256,768]{1,0:T(8,128)(2,1)S(1)}, bf16[256,768]{1,0:T(8,128)(2,1)}, u32[]{:S(2)}, u32[]{:S(2)}) collective-permute-start(bf16[256,768]{1,0:T(8,128)(2,1)S(1)} %collective-permute-done.4.refs_5_), channel_id=1, source_target_pairs={{0,16},{16,0},{1,17},{17,1},{2,18},{18,2},{3,19},{19,3},{4,20},{20... | collective-permute-start | bytes 1179656 | tf_op jit(solution)/shard_map/ppermute | solution.py:291
  55.0 3.5 %collective-permute-start.7 = (bf16[256,768]{1,0:T(8,128)(2,1)S(1)}, bf16[256,768]{1,0:T(8,128)(2,1)}, u32[]{:S(2)}, u32[]{:S(2)}) collective-permute-start(bf16[256,768]{1,0:T(8,128)(2,1)S(1)} %collective-permute-done.3.refs_3_), channel_id=1, source_target_pairs={{0,16},{16,0},{1,17},{17,1},{2,18},{18,2},{3,19},{19,3},{4,20},{20... | collective-permute-start | bytes 1179656 | tf_op jit(solution)/shard_map/ppermute | solution.py:291
  55.4 3.0 %collective-permute-start.6 = (bf16[256,768]{1,0:T(8,128)(2,1)S(1)}, bf16[256,768]{1,0:T(8,128)(2,1)}, u32[]{:S(2)}, u32[]{:S(2)}) collective-permute-start(bf16[256,768]{1,0:T(8,128)(2,1)S(1)} %copy-done.5), channel_id=1, source_target_pairs={{0,16},{16,0},{1,17},{17,1},{2,18},{18,2},{3,19},{19,3},{4,20},{20... | collective-permute-start | bytes 1179656 | tf_op jit(solution)/shard_map/ppermute | solution.py:291
  55.5 2.9 %collective-permute-start.10 = (bf16[4,256,128]{2,1,0:T(8,128)(2,1)S(1)}, bf16[4,256,128]{2,1,0:T(8,128)(2,1)}, u32[]{:S(2)}, u32[]{:S(2)}) collective-permute-start(bf16[4,256,128]{2,1,0:T(8,128)(2,1)S(1)} %bitcast.38), channel_id=1, source_target_pairs={{0,16},{16,0},{1,17},{17,1},{2,18},{18,2},{3,19},{19,3},{4,20},{20... | collective-permute-start | bytes 786440 | tf_op jit(solution)/shard_map/ppermute | solution.py:292
  77.3 20.7 %all-to-all-start.3 = ((bf16[16,256,128]{2,1,0:T(8,128)(2,1)}), bf16[16,256,128]{2,1,0:T(8,128)(2,1)S(1)}, u32[]{:S(2)}, u32[]{:S(2)}) async-start(bf16[16,256,128]{2,1,0:T(8,128)(2,1)} %get-tuple-element.49), calls=%async_computation.3 | async-start | bytes 2097152 | tf_op jit(solution)/shard_map/all_to_all | solution.py:32
  91.0 3.4 %collective-permute-start.11 = (bf16[16,64,128]{2,1,0:T(8,128)(2,1)}, bf16[16,64,128]{2,1,0:T(8,128)(2,1)S(1)}, u32[]{:S(2)}, u32[]{:S(2)}) collective-permute-start(bf16[16,64,128]{2,1,0:T(8,128)(2,1)} %get-tuple-element.47), channel_id=1, source_target_pairs={{0,16},{16,0},{1,17},{17,1},{2,18},{18,2},{3,19},{19,3},{4,20},{20... | collective-permute-start | bytes 786440 | tf_op jit(solution)/shard_map/ppermute | solution.py:337
  98.0 15.0 %all-to-all-start.4 = ((bf16[16,80,128]{2,1,0:T(8,128)(2,1)}), bf16[16,80,128]{2,1,0:T(8,128)(2,1)S(1)}, u32[]{:S(2)}, u32[]{:S(2)}) async-start(bf16[16,80,128]{2,1,0:T(8,128)(2,1)} %pad_maximum_fusion.1), calls=%async_computation.4 | async-start | bytes 655360 | tf_op jit(solution)/shard_map/all_to_all | solution.py:32
  113.1 4.2 %collective-permute-start.13 = (bf16[128,128]{1,0:T(8,128)(2,1)S(1)}, bf16[128,128]{1,0:T(8,128)(2,1)S(1)}, u32[]{:S(2)}, u32[]{:S(2)}) collective-permute-start(bf16[128,128]{1,0:T(8,128)(2,1)S(1)} %constant_dynamic-update-slice_fusion.1), channel_id=1, source_target_pairs={{0,32},{32,0},{64,96},{96,64},{1,33},{33,1},{65,97},{97,65},{2,34}... | collective-permute-start | bytes 98312 | tf_op jit(solution)/shard_map/ppermute | solution.py:218
  113.7 4.4 %collective-permute-start.14 = (bf16[128,128]{1,0:T(8,128)(2,1)S(1)}, bf16[128,128]{1,0:T(8,128)(2,1)S(1)}, u32[]{:S(2)}, u32[]{:S(2)}) collective-permute-start(bf16[128,128]{1,0:T(8,128)(2,1)S(1)} %constant_dynamic-update-slice_fusion.1), channel_id=1, source_target_pairs={{0,64},{32,96},{64,0},{96,32},{1,65},{33,97},{65,1},{97,33},{2,66}... | collective-permute-start | bytes 98312 | tf_op jit(solution)/shard_map/ppermute | solution.py:218
  115.2 4.0 %collective-permute-start.15 = (bf16[128,128]{1,0:T(8,128)(2,1)S(1)}, bf16[128,128]{1,0:T(8,128)(2,1)S(1)}, u32[]{:S(2)}, u32[]{:S(2)}) collective-permute-start(bf16[128,128]{1,0:T(8,128)(2,1)S(1)} %constant_dynamic-update-slice_fusion.1), channel_id=1, source_target_pairs={{0,96},{32,64},{64,32},{96,0},{1,97},{33,65},{65,33},{97,1},{2,98}... | collective-permute-start | bytes 98312 | tf_op jit(solution)/shard_map/ppermute | solution.py:218
  120.5 13.4 %all-to-all-start.5 = ((bf16[16,160,128]{2,1,0:T(8,128)(2,1)}), bf16[16,160,128]{2,1,0:T(8,128)(2,1)S(1)}, u32[]{:S(2)}, u32[]{:S(2)}) async-start(bf16[16,160,128]{2,1,0:T(8,128)(2,1)} %broadcast_in_dim.92), calls=%async_computation.5 | async-start | bytes 1310720 | tf_op jit(solution)/shard_map/all_to_all | solution.py:32
  133.9 5.6 %collective-permute-start.18 = (f32[16,128]{1,0:T(8,128)S(1)}, f32[16,128]{1,0:T(8,128)S(1)}, u32[]{:S(2)}, u32[]{:S(2)}) collective-permute-start(f32[16,128]{1,0:T(8,128)S(1)} %slice_add_fusion), channel_id=1, source_target_pairs={{0,16},{16,0},{1,17},{17,1},{2,18},{18,2},{3,19},{19,3},{4,20},{20... | collective-permute-start | bytes 24584 | tf_op jit(solution)/shard_map/ppermute | solution.py:386
  138.5 1.6 %collective-permute-start.17 = (bf16[128,128]{1,0:T(8,128)(2,1)S(1)}, bf16[128,128]{1,0:T(8,128)(2,1)S(1)}, u32[]{:S(2)}, u32[]{:S(2)}) collective-permute-start(bf16[128,128]{1,0:T(8,128)(2,1)S(1)} %slice.129), channel_id=1, source_target_pairs={{0,16},{16,0},{1,17},{17,1},{2,18},{18,2},{3,19},{19,3},{4,20},{20... | collective-permute-start | bytes 98312 | tf_op jit(solution)/shard_map/ppermute | solution.py:381
  138.9 1.8 %collective-permute-start.16 = (bf16[128,128]{1,0:T(8,128)(2,1)S(1)}, bf16[128,128]{1,0:T(8,128)(2,1)S(1)}, u32[]{:S(2)}, u32[]{:S(2)}) collective-permute-start(bf16[128,128]{1,0:T(8,128)(2,1)S(1)} %slice.126), channel_id=1, source_target_pairs={{0,16},{16,0},{1,17},{17,1},{2,18},{18,2},{3,19},{19,3},{4,20},{20... | collective-permute-start | bytes 98312 | tf_op jit(solution)/shard_map/ppermute | solution.py:380
  (14 other events, 144.3 us)

commit v7 on v6

--- a/solution.py
+++ b/solution.py
@@ -346,7 +346,7 @@
     to_z = jnp.concatenate(
         [rest[: columns // 2].astype(BF), (tile_base + rest[columns // 2 :]).astype(BF)]
         + high_low(weight_part)
-        + [jnp.pad(block_counts, ((0, 15), (0, 0)))],
+        + [jnp.pad(block_counts, ((0, 7), (0, 0)))],
         axis=0,
     )
     hop = jnp.stack([to_z] + [turn(to_z, "z", d) for d in (1, 2, 3)])

time: 142 us -> 142 us (level)
  no operation moved by 1% of the time
where the time goes in v7:
time: 142 us; the launch traced here: 141 us
  starting transfers between devices  55.3 us (39%)
  waiting for transfers between devices  35.9 us (25%)
  Pallas kernels  21.4 us (15%)
  matrix products  14.5 us (10%)
  other arithmetic  9.11 us (6%)
  local copies, waits for them, and re-layouts  4.03 us (3%)
    all_to_all x6, starting transfers between devices, exchange(): return lax.all_to_all(blocks, axis, split_axis=0, concat_axis=0, tiled=True)  37 us
    all_to_all x6, waiting for transfers between devices, exchange(): return lax.all_to_all(blocks, axis, split_axis=0, concat_axis=0, tiled=True)  22.7 us
    pallas_call x3, Pallas kernels, call(): pl.pallas_call(kernel, in_specs=specs, out_specs=[anywhere] * n_out, out_...  21.4 us
    ppermute x6, waiting for transfers between devices, turn(): return lax.ppermute(value, axis, [(i, i ^ by) for i in range(size)])  10.5 us
    ppermute x6, starting transfers between devices, turn(): return lax.ppermute(value, axis, [(i, i ^ by) for i in range(size)])  8.1 us
    dot_general x2, matrix products, on_device(): jnp.einsum('ijc,ch->hij', part, late_w, preferred_element_type=F32)  6.81 us
    dot_general x1, matrix products, on_device(): jnp.einsum('ijc,hij->hc', pair, bias_back, preferred_element_type=F32)  5.12 us
    ppermute x1, starting transfers between devices, on_device(): grad_bias = jnp.transpose(weight + lax.ppermute(weight, 'k', SWAP))  4.1 us
  transfers between devices with their start and end apart: 25, of which 12 were waited for; matrix products, arithmetic and copies ran while one was open for 16% of the time, Pallas kernels for 12%

profile of v7, /device:TPU:1, one launch (start us, length us, event | category | flops | bytes accessed | tf_op | source)
XLA Modules:
  0.0 141.4 jit_solution(16122985868195978222)
XLA Ops:
  0.6 1.5 %collective-permute-start = (s32[128]{0:T(128)}, s32[128]{0:T(128)S(1)}, u32[]{:S(2)}, u32[]{:S(2)}) collective-permute-start(s32[128]{0:T(128)} %param.11), channel_id=1, source_target_pairs={{0,16},{16,0},{1,17},{17,1},{2,18},{18,2},{3,19},{19,3},{4,20},{20... | collective-permute-start | bytes 1544 | tf_op jit(solution)/shard_map/ppermute | solution.py:240
  5.6 11.2 %all-to-all-start = ((bf16[64,40,128]{2,1,0:T(8,128)(2,1)}), bf16[64,40,128]{2,1,0:T(8,128)(2,1)S(1)}, u32[]{:S(2)}, u32[]{:S(2)}) async-start(bf16[64,40,128]{2,1,0:T(8,128)(2,1)} %fusion.8), calls=%async_computation | async-start | bytes 1310720 | tf_op jit(solution)/shard_map/all_to_all | solution.py:32
  16.8 2.3 %fusion.2 = bf16[16,64,128]{2,0,1:T(8,128)(2,1)S(1)} fusion(bf16[256,128,128]{2,1,0:T(8,128)(2,1)} %param.14, bf16[128,16]{0,1:T(8,128)(2,1)S(1)} %copy-done), kind=kOutput, calls=%fused_computation.2 | convolution fusion | flops 33554432 | bytes 2363392 | tf_op jit(solution)/shard_map/ijc,ch->hij/dot_general | solution.py:267
  20.3 2.6 %collective-permute-start.4 = (bf16[256,768]{1,0:T(8,128)(2,1)S(1)}, bf16[256,768]{1,0:T(8,128)(2,1)S(1)}, u32[]{:S(2)}, u32[]{:S(2)}) collective-permute-start(bf16[256,768]{1,0:T(8,128)(2,1)S(1)} %copy-done.5), channel_id=1, source_target_pairs={{0,64},{32,96},{64,0},{96,32},{1,65},{33,97},{65,1},{97,33},{2,66}... | collective-permute-start | bytes 1179656 | tf_op jit(solution)/shard_map/ppermute | solution.py:218
  23.2 4.5 %fusion = bf16[16,192,128]{2,0,1:T(8,128)(2,1)S(1)} fusion(bf16[256,128,128]{2,1,0:T(8,128)(2,1)} %param.14, bf16[128,16]{0,1:T(8,128)(2,1)S(1)} %copy-done), kind=kOutput, calls=%fused_computation | convolution fusion | flops 100663296 | bytes 7081984 | tf_op jit(solution)/shard_map/ijc,ch->hij/dot_general | solution.py:267
  27.9 3.0 %all-to-all-done = bf16[64,40,128]{2,1,0:T(8,128)(2,1)S(1)} async-done(((bf16[64,40,128]{2,1,0:T(8,128)(2,1)}), bf16[64,40,128]{2,1,0:T(8,128)(2,1)S(1)}, u32[]{:S(2)}, u32[]{:S(2)}) %all-to-all-start) | async-done | bytes 655392 | tf_op jit(solution)/shard_map/all_to_all | solution.py:32
  32.0 6.6 %all-to-all-start.1 = ((bf16[64,16,128]{2,1,0:T(8,128)(2,1)}), bf16[64,16,128]{2,1,0:T(8,128)(2,1)S(1)}, u32[]{:S(2)}, u32[]{:S(2)}) async-start(bf16[64,16,128]{2,1,0:T(8,128)(2,1)} %broadcast_in_dim.60), calls=%async_computation.1 | async-start | bytes 524288 | tf_op jit(solution)/shard_map/all_to_all | solution.py:32
  40.5 7.5 %collective-permute-done.4.refs_5_ = bf16[256,768]{1,0:T(8,128)(2,1)S(1)} collective-permute-done((bf16[256,768]{1,0:T(8,128)(2,1)S(1)}, bf16[256,768]{1,0:T(8,128)(2,1)S(1)}, u32[]{:S(2)}, u32[]{:S(2)}) %collective-permute-start.4) | collective-permute-done | bytes 393248 | tf_op jit(solution)/shard_map/ppermute | solution.py:218
  49.4 4.6 %all-to-all-start.2 = ((bf16[16,288,128]{2,1,0:T(8,128)(2,1)}), bf16[16,288,128]{2,1,0:T(8,128)(2,1)S(1)}, u32[]{:S(2)}, u32[]{:S(2)}) async-start(bf16[16,288,128]{2,1,0:T(8,128)(2,1)} %pad_maximum_fusion), calls=%async_computation.2 | async-start | bytes 2359296 | tf_op jit(solution)/shard_map/all_to_all | solution.py:32
  56.8 1.6 %collective-permute-done.10.refs_10_ = bf16[4,256,128]{2,1,0:T(8,128)(2,1)} collective-permute-done((bf16[4,256,128]{2,1,0:T(8,128)(2,1)S(1)}, bf16[4,256,128]{2,1,0:T(8,128)(2,1)}, u32[]{:S(2)}, u32[]{:S(2)}) %collective-permute-start.10) | collective-permute-done | bytes 262176 | tf_op jit(solution)/shard_map/ppermute | solution.py:292
  58.5 8.0 %shard_map.121 = (bf16[16,128,768]{2,1,0:T(8,128)(2,1)}, f32[16,128,1]{2,1,0:T(8,128)}, bf16[16,96,128]{2,1,0:T(8,128)(2,1)}, bf16[256,48]{1,0:T(8,128)(2,1)}, bf16[48,256]{1,0:T(8,128)(2,1)}) custom-call(s32[4]{0:T(128)} %pad_add_fusion.refs_0_, bf16[256,768]{1,0:T(8,128)(2,1)} %refs_1_, bf16[256,768]{1,0:T(8,128)(2,1)} %collective-permute-done.6.refs_2_, ...), custom_call_target="tpu_custom_call" | custom-call | flops 1000000000 | bytes 8388608 | tf_op jit(solution)/shard_map/pallas_call | solution.py:196
  66.5 5.0 %all-to-all-done.2.refs_3_ = bf16[16,288,128]{2,1,0:T(8,128)(2,1)S(1)} async-done(((bf16[16,288,128]{2,1,0:T(8,128)(2,1)}), bf16[16,288,128]{2,1,0:T(8,128)(2,1)S(1)}, u32[]{:S(2)}, u32[]{:S(2)}) %all-to-all-start.2) | async-done | bytes 1179680 | tf_op jit(solution)/shard_map/all_to_all | solution.py:32
  72.5 4.7 %shard_map.122 = (bf16[16,256,128]{2,1,0:T(8,128)(2,1)}, bf16[96,2048]{1,0:T(8,128)(2,1)}, bf16[256,48]{1,0:T(8,128)(2,1)}, bf16[256,48]{1,0:T(8,128)(2,1)}, f32[256,768]{1,0:T(8,128)}) custom-call(bf16[256,48]{1,0:T(8,128)(2,1)} %get-tuple-element.36.refs_0_, bf16[48,256]{1,0:T(8,128)(2,1)} %get-tuple-element.37.refs_1_, ...), custom_call_target="tpu_custom_call" | custom-call | flops 2000000000 | bytes 8388608 | tf_op jit(solution)/shard_map/pallas_call | solution.py:196
  77.3 5.0 %all-to-all-start.3 = ((bf16[16,256,128]{2,1,0:T(8,128)(2,1)}), bf16[16,256,128]{2,1,0:T(8,128)(2,1)S(1)}, u32[]{:S(2)}, u32[]{:S(2)}) async-start(bf16[16,256,128]{2,1,0:T(8,128)(2,1)} %get-tuple-element.49), calls=%async_computation.3 | async-start | bytes 2097152 | tf_op jit(solution)/shard_map/all_to_all | solution.py:32
  82.3 8.7 %shard_map.123 = (f32[16,64,128]{2,1,0:T(8,128)}, bf16[16,64,128]{2,1,0:T(8,128)(2,1)}, bf16[16,16,128]{2,1,0:T(8,128)(2,1)}) custom-call(s32[4]{0:T(128)} %pad_add_fusion.refs_0_, bf16[96,2048]{1,0:T(8,128)(2,1)} %get-tuple-element.40.refs_1_, bf16[256,48]{1,0:T(8,128)(2,1)} %get-tuple-element.41.refs_2_, bf16[256,48]{1,0:T(8,128)(2,1)} %get-tuple-element.42.refs_3_, ...), custom_call_target="tpu_custom_call" | custom-call | flops 1000000000 | bytes 8388608 | tf_op jit(solution)/shard_map/pallas_call | solution.py:196
  91.0 1.4 collective-permute-start.11
  95.5 1.6 %pad_maximum_fusion.1 = bf16[16,80,128]{2,1,0:T(8,128)(2,1)} fusion(bf16[16,16,128]{2,1,0:T(8,128)(2,1)} %get-tuple-element.48, bf16[16,64,128]{2,1,0:T(8,128)(2,1)S(1)} %add_convert_fusion), kind=kLoop, calls=%fused_computation.30 | loop fusion | flops 655360 | bytes 655360 | tf_op jit(solution)/shard_map/concatenate | solution.py:338
  98.0 6.0 %all-to-all-start.4 = ((bf16[16,80,128]{2,1,0:T(8,128)(2,1)}), bf16[16,80,128]{2,1,0:T(8,128)(2,1)S(1)}, u32[]{:S(2)}, u32[]{:S(2)}) async-start(bf16[16,80,128]{2,1,0:T(8,128)(2,1)} %pad_maximum_fusion.1), calls=%async_computation.4 | async-start | bytes 655360 | tf_op jit(solution)/shard_map/all_to_all | solution.py:32
  104.0 5.1 %convolution_bitcast_fusion = f32[16,128]{1,0:T(8,128)S(1)} fusion(bf16[256,128,128]{2,1,0:T(8,128)(2,1)} %param.14, bf16[16,256,128]{2,1,0:T(8,128)(2,1)S(1)} %all-to-all-done.3), kind=kOutput, calls=%fused_computation.15 | convolution fusion | flops 134217728 | bytes 9445376 | tf_op jit(solution)/shard_map/ijc,hij->hc/dot_general | solution.py:341
  109.1 3.9 %all-to-all-done.4 = bf16[16,80,128]{2,1,0:T(8,128)(2,1)S(1)} async-done(((bf16[16,80,128]{2,1,0:T(8,128)(2,1)}), bf16[16,80,128]{2,1,0:T(8,128)(2,1)S(1)}, u32[]{:S(2)}, u32[]{:S(2)}) %all-to-all-start.4) | async-done | bytes 327712 | tf_op jit(solution)/shard_map/all_to_all | solution.py:32
  115.2 2.1 %collective-permute-start.15 = (bf16[120,128]{1,0:T(8,128)(2,1)S(1)}, bf16[120,128]{1,0:T(8,128)(2,1)S(1)}, u32[]{:S(2)}, u32[]{:S(2)}) collective-permute-start(bf16[120,128]{1,0:T(8,128)(2,1)S(1)} %constant_dynamic-update-slice_fusion.1), channel_id=1, source_target_pairs={{0,96},{32,64},{64,32},{96,0},{1,97},{33,65},{65,33},{97,1},{2,98}... | collective-permute-start | bytes 92168 | tf_op jit(solution)/shard_map/ppermute | solution.py:218
  120.4 3.6 %all-to-all-start.5 = ((bf16[16,160,128]{2,1,0:T(8,128)(2,1)}), bf16[16,160,128]{2,1,0:T(8,128)(2,1)S(1)}, u32[]{:S(2)}, u32[]{:S(2)}) async-start(bf16[16,160,128]{2,1,0:T(8,128)(2,1)} %broadcast_in_dim.92), calls=%async_computation.5 | async-start | bytes 1310720 | tf_op jit(solution)/shard_map/all_to_all | solution.py:32
  124.1 9.7 %all-to-all-done.5 = bf16[16,160,128]{2,1,0:T(8,128)(2,1)S(1)} async-done(((bf16[16,160,128]{2,1,0:T(8,128)(2,1)}), bf16[16,160,128]{2,1,0:T(8,128)(2,1)S(1)}, u32[]{:S(2)}, u32[]{:S(2)}) %all-to-all-start.5) | async-done | bytes 655392 | tf_op jit(solution)/shard_map/all_to_all | solution.py:32
  133.9 4.1 %collective-permute-start.18 = (f32[16,128]{1,0:T(8,128)S(1)}, f32[16,128]{1,0:T(8,128)S(1)}, u32[]{:S(2)}, u32[]{:S(2)}) collective-permute-start(f32[16,128]{1,0:T(8,128)S(1)} %slice_add_fusion), channel_id=1, source_target_pairs={{0,16},{16,0},{1,17},{17,1},{2,18},{18,2},{3,19},{19,3},{4,20},{20... | collective-permute-start | bytes 24584 | tf_op jit(solution)/shard_map/ppermute | solution.py:386
  (121 shorter events, 25.8 us)
Async XLA Ops:
  0.6 3.3 %collective-permute-start = (s32[128]{0:T(128)}, s32[128]{0:T(128)S(1)}, u32[]{:S(2)}, u32[]{:S(2)}) collective-permute-start(s32[128]{0:T(128)} %param.11), channel_id=1, source_target_pairs={{0,16},{16,0},{1,17},{17,1},{2,18},{18,2},{3,19},{19,3},{4,20},{20... | collective-permute-start | bytes 1544 | tf_op jit(solution)/shard_map/ppermute | solution.py:240
  2.1 1.8 %collective-permute-start.1 = (bf16[128,128]{1,0:T(8,128)(2,1)}, bf16[128,128]{1,0:T(8,128)(2,1)S(1)}, u32[]{:S(2)}, u32[]{:S(2)}) collective-permute-start(bf16[128,128]{1,0:T(8,128)(2,1)} %param.10), channel_id=1, source_target_pairs={{0,16},{16,0},{1,17},{17,1},{2,18},{18,2},{3,19},{19,3},{4,20},{20... | collective-permute-start | bytes 98312 | tf_op jit(solution)/shard_map/ppermute | solution.py:241
  2.2 1.7 %collective-permute-start.2 = (bf16[128,128]{1,0:T(8,128)(2,1)}, bf16[128,128]{1,0:T(8,128)(2,1)S(1)}, u32[]{:S(2)}, u32[]{:S(2)}) collective-permute-start(bf16[128,128]{1,0:T(8,128)(2,1)} %param.12), channel_id=1, source_target_pairs={{0,16},{16,0},{1,17},{17,1},{2,18},{18,2},{3,19},{19,3},{4,20},{20... | collective-permute-start | bytes 98312 | tf_op jit(solution)/shard_map/ppermute | solution.py:242
  5.6 25.4 %all-to-all-start = ((bf16[64,40,128]{2,1,0:T(8,128)(2,1)}), bf16[64,40,128]{2,1,0:T(8,128)(2,1)S(1)}, u32[]{:S(2)}, u32[]{:S(2)}) async-start(bf16[64,40,128]{2,1,0:T(8,128)(2,1)} %fusion.8), calls=%async_computation | async-start | bytes 1310720 | tf_op jit(solution)/shard_map/all_to_all | solution.py:32
  19.2 21.3 %collective-permute-start.3 = (bf16[256,768]{1,0:T(8,128)(2,1)S(1)}, bf16[256,768]{1,0:T(8,128)(2,1)S(1)}, u32[]{:S(2)}, u32[]{:S(2)}) collective-permute-start(bf16[256,768]{1,0:T(8,128)(2,1)S(1)} %copy-done.5), channel_id=1, source_target_pairs={{0,32},{32,0},{64,96},{96,64},{1,33},{33,1},{65,97},{97,65},{2,34}... | collective-permute-start | bytes 1179656 | tf_op jit(solution)/shard_map/ppermute | solution.py:218
  20.3 27.7 %collective-permute-start.4 = (bf16[256,768]{1,0:T(8,128)(2,1)S(1)}, bf16[256,768]{1,0:T(8,128)(2,1)S(1)}, u32[]{:S(2)}, u32[]{:S(2)}) collective-permute-start(bf16[256,768]{1,0:T(8,128)(2,1)S(1)} %copy-done.5), channel_id=1, source_target_pairs={{0,64},{32,96},{64,0},{96,32},{1,65},{33,97},{65,1},{97,33},{2,66}... | collective-permute-start | bytes 1179656 | tf_op jit(solution)/shard_map/ppermute | solution.py:218
  22.9 26.3 %collective-permute-start.5 = (bf16[256,768]{1,0:T(8,128)(2,1)S(1)}, bf16[256,768]{1,0:T(8,128)(2,1)S(1)}, u32[]{:S(2)}, u32[]{:S(2)}) collective-permute-start(bf16[256,768]{1,0:T(8,128)(2,1)S(1)} %copy-done.5), channel_id=1, source_target_pairs={{0,96},{32,64},{64,32},{96,0},{1,97},{33,65},{65,33},{97,1},{2,98}... | collective-permute-start | bytes 1179656 | tf_op jit(solution)/shard_map/ppermute | solution.py:218
  32.0 17.3 %all-to-all-start.1 = ((bf16[64,16,128]{2,1,0:T(8,128)(2,1)}), bf16[64,16,128]{2,1,0:T(8,128)(2,1)S(1)}, u32[]{:S(2)}, u32[]{:S(2)}) async-start(bf16[64,16,128]{2,1,0:T(8,128)(2,1)} %broadcast_in_dim.60), calls=%async_computation.1 | async-start | bytes 524288 | tf_op jit(solution)/shard_map/all_to_all | solution.py:32
  49.4 22.2 %all-to-all-start.2 = ((bf16[16,288,128]{2,1,0:T(8,128)(2,1)}), bf16[16,288,128]{2,1,0:T(8,128)(2,1)S(1)}, u32[]{:S(2)}, u32[]{:S(2)}) async-start(bf16[16,288,128]{2,1,0:T(8,128)(2,1)} %pad_maximum_fusion), calls=%async_computation.2 | async-start | bytes 2359296 | tf_op jit(solution)/shard_map/all_to_all | solution.py:32
  54.0 4.4 %collective-permute-start.9 = (bf16[256,768]{1,0:T(8,128)(2,1)S(1)}, bf16[256,768]{1,0:T(8,128)(2,1)}, u32[]{:S(2)}, u32[]{:S(2)}) collective-permute-start(bf16[256,768]{1,0:T(8,128)(2,1)S(1)} %collective-permute-done.5.refs_7_), channel_id=1, source_target_pairs={{0,16},{16,0},{1,17},{17,1},{2,18},{18,2},{3,19},{19,3},{4,20},{20... | collective-permute-start | bytes 1179656 | tf_op jit(solution)/shard_map/ppermute | solution.py:291
  54.9 3.5 %collective-permute-start.8 = (bf16[256,768]{1,0:T(8,128)(2,1)S(1)}, bf16[256,768]{1,0:T(8,128)(2,1)}, u32[]{:S(2)}, u32[]{:S(2)}) collective-permute-start(bf16[256,768]{1,0:T(8,128)(2,1)S(1)} %collective-permute-done.4.refs_5_), channel_id=1, source_target_pairs={{0,16},{16,0},{1,17},{17,1},{2,18},{18,2},{3,19},{19,3},{4,20},{20... | collective-permute-start | bytes 1179656 | tf_op jit(solution)/shard_map/ppermute | solution.py:291
  55.0 3.5 %collective-permute-start.7 = (bf16[256,768]{1,0:T(8,128)(2,1)S(1)}, bf16[256,768]{1,0:T(8,128)(2,1)}, u32[]{:S(2)}, u32[]{:S(2)}) collective-permute-start(bf16[256,768]{1,0:T(8,128)(2,1)S(1)} %collective-permute-done.3.refs_3_), channel_id=1, source_target_pairs={{0,16},{16,0},{1,17},{17,1},{2,18},{18,2},{3,19},{19,3},{4,20},{20... | collective-permute-start | bytes 1179656 | tf_op jit(solution)/shard_map/ppermute | solution.py:291
  55.4 3.0 %collective-permute-start.6 = (bf16[256,768]{1,0:T(8,128)(2,1)S(1)}, bf16[256,768]{1,0:T(8,128)(2,1)}, u32[]{:S(2)}, u32[]{:S(2)}) collective-permute-start(bf16[256,768]{1,0:T(8,128)(2,1)S(1)} %copy-done.5), channel_id=1, source_target_pairs={{0,16},{16,0},{1,17},{17,1},{2,18},{18,2},{3,19},{19,3},{4,20},{20... | collective-permute-start | bytes 1179656 | tf_op jit(solution)/shard_map/ppermute | solution.py:291
  55.5 2.9 %collective-permute-start.10 = (bf16[4,256,128]{2,1,0:T(8,128)(2,1)S(1)}, bf16[4,256,128]{2,1,0:T(8,128)(2,1)}, u32[]{:S(2)}, u32[]{:S(2)}) collective-permute-start(bf16[4,256,128]{2,1,0:T(8,128)(2,1)S(1)} %bitcast.38), channel_id=1, source_target_pairs={{0,16},{16,0},{1,17},{17,1},{2,18},{18,2},{3,19},{19,3},{4,20},{20... | collective-permute-start | bytes 786440 | tf_op jit(solution)/shard_map/ppermute | solution.py:292
  77.3 20.7 %all-to-all-start.3 = ((bf16[16,256,128]{2,1,0:T(8,128)(2,1)}), bf16[16,256,128]{2,1,0:T(8,128)(2,1)S(1)}, u32[]{:S(2)}, u32[]{:S(2)}) async-start(bf16[16,256,128]{2,1,0:T(8,128)(2,1)} %get-tuple-element.49), calls=%async_computation.3 | async-start | bytes 2097152 | tf_op jit(solution)/shard_map/all_to_all | solution.py:32
  91.0 3.4 %collective-permute-start.11 = (bf16[16,64,128]{2,1,0:T(8,128)(2,1)}, bf16[16,64,128]{2,1,0:T(8,128)(2,1)S(1)}, u32[]{:S(2)}, u32[]{:S(2)}) collective-permute-start(bf16[16,64,128]{2,1,0:T(8,128)(2,1)} %get-tuple-element.47), channel_id=1, source_target_pairs={{0,16},{16,0},{1,17},{17,1},{2,18},{18,2},{3,19},{19,3},{4,20},{20... | collective-permute-start | bytes 786440 | tf_op jit(solution)/shard_map/ppermute | solution.py:337
  98.0 15.0 %all-to-all-start.4 = ((bf16[16,80,128]{2,1,0:T(8,128)(2,1)}), bf16[16,80,128]{2,1,0:T(8,128)(2,1)S(1)}, u32[]{:S(2)}, u32[]{:S(2)}) async-start(bf16[16,80,128]{2,1,0:T(8,128)(2,1)} %pad_maximum_fusion.1), calls=%async_computation.4 | async-start | bytes 655360 | tf_op jit(solution)/shard_map/all_to_all | solution.py:32
  113.1 4.2 %collective-permute-start.13 = (bf16[120,128]{1,0:T(8,128)(2,1)S(1)}, bf16[120,128]{1,0:T(8,128)(2,1)S(1)}, u32[]{:S(2)}, u32[]{:S(2)}) collective-permute-start(bf16[120,128]{1,0:T(8,128)(2,1)S(1)} %constant_dynamic-update-slice_fusion.1), channel_id=1, source_target_pairs={{0,32},{32,0},{64,96},{96,64},{1,33},{33,1},{65,97},{97,65},{2,34}... | collective-permute-start | bytes 92168 | tf_op jit(solution)/shard_map/ppermute | solution.py:218
  113.7 4.3 %collective-permute-start.14 = (bf16[120,128]{1,0:T(8,128)(2,1)S(1)}, bf16[120,128]{1,0:T(8,128)(2,1)S(1)}, u32[]{:S(2)}, u32[]{:S(2)}) collective-permute-start(bf16[120,128]{1,0:T(8,128)(2,1)S(1)} %constant_dynamic-update-slice_fusion.1), channel_id=1, source_target_pairs={{0,64},{32,96},{64,0},{96,32},{1,65},{33,97},{65,1},{97,33},{2,66}... | collective-permute-start | bytes 92168 | tf_op jit(solution)/shard_map/ppermute | solution.py:218
  115.2 4.0 %collective-permute-start.15 = (bf16[120,128]{1,0:T(8,128)(2,1)S(1)}, bf16[120,128]{1,0:T(8,128)(2,1)S(1)}, u32[]{:S(2)}, u32[]{:S(2)}) collective-permute-start(bf16[120,128]{1,0:T(8,128)(2,1)S(1)} %constant_dynamic-update-slice_fusion.1), channel_id=1, source_target_pairs={{0,96},{32,64},{64,32},{96,0},{1,97},{33,65},{65,33},{97,1},{2,98}... | collective-permute-start | bytes 92168 | tf_op jit(solution)/shard_map/ppermute | solution.py:218
  120.4 13.4 %all-to-all-start.5 = ((bf16[16,160,128]{2,1,0:T(8,128)(2,1)}), bf16[16,160,128]{2,1,0:T(8,128)(2,1)S(1)}, u32[]{:S(2)}, u32[]{:S(2)}) async-start(bf16[16,160,128]{2,1,0:T(8,128)(2,1)} %broadcast_in_dim.92), calls=%async_computation.5 | async-start | bytes 1310720 | tf_op jit(solution)/shard_map/all_to_all | solution.py:32
  133.9 5.6 %collective-permute-start.18 = (f32[16,128]{1,0:T(8,128)S(1)}, f32[16,128]{1,0:T(8,128)S(1)}, u32[]{:S(2)}, u32[]{:S(2)}) collective-permute-start(f32[16,128]{1,0:T(8,128)S(1)} %slice_add_fusion), channel_id=1, source_target_pairs={{0,16},{16,0},{1,17},{17,1},{2,18},{18,2},{3,19},{19,3},{4,20},{20... | collective-permute-start | bytes 24584 | tf_op jit(solution)/shard_map/ppermute | solution.py:386
  138.5 1.6 %collective-permute-start.17 = (bf16[128,128]{1,0:T(8,128)(2,1)S(1)}, bf16[128,128]{1,0:T(8,128)(2,1)S(1)}, u32[]{:S(2)}, u32[]{:S(2)}) collective-permute-start(bf16[128,128]{1,0:T(8,128)(2,1)S(1)} %slice.129), channel_id=1, source_target_pairs={{0,16},{16,0},{1,17},{17,1},{2,18},{18,2},{3,19},{19,3},{4,20},{20... | collective-permute-start | bytes 98312 | tf_op jit(solution)/shard_map/ppermute | solution.py:381
  138.9 1.8 %collective-permute-start.16 = (bf16[128,128]{1,0:T(8,128)(2,1)S(1)}, bf16[128,128]{1,0:T(8,128)(2,1)S(1)}, u32[]{:S(2)}, u32[]{:S(2)}) collective-permute-start(bf16[128,128]{1,0:T(8,128)(2,1)S(1)} %slice.126), channel_id=1, source_target_pairs={{0,16},{16,0},{1,17},{17,1},{2,18},{18,2},{3,19},{19,3},{4,20},{20... | collective-permute-start | bytes 98312 | tf_op jit(solution)/shard_map/ppermute | solution.py:380
  (14 other events, 144.3 us)
